TPU v7x, 32 devices: a whole 2x2x4 slice. The times are simulated.
32 devices in a mesh: dp: 8 (over z, x), ns: 4 (over y, core).
Axes of the slice: x: 2, y: 2, z: 4, core: 2. Of those that a mesh axis runs over, the one named last changes fastest.
Arguments:
- patches: bfloat16 [32768, 768], P(('dp', 'ns')), may hold values from -6 to 6
- counts: int32 [32, 16], P(('dp', 'ns')), may hold values from 0 to 576, as said below
- owners: int32 [32, 16], P(('dp', 'ns')), may hold values from 0 to 7, as said below
- pooled_cot: bfloat16 [512, 768], P(('dp', 'ns')), may hold values from -96 to 96
- patch_cot: bfloat16 [32768, 768], P(('dp', 'ns')), may hold values from -6 to 6
- master_qkv: float32 [2304, 768], P('ns'), may hold values from -0.21875 to 0.21875
- master_out: float32 [768, 768], P('ns'), may hold values from -0.4375 to 0.4375
- master_up: float32 [3072, 768], P('ns'), may hold values from -0.21875 to 0.21875
- master_down: float32 [3072, 768], P('ns'), may hold values from -0.109375 to 0.109375
- mom_qkv: float32 [2304, 768], P('ns')
- mom_out: float32 [768, 768], P('ns')
- mom_up: float32 [3072, 768], P('ns')
- mom_down: float32 [3072, 768], P('ns')
- vectors: float32 [10176], replicated
- vec_first: float32 [10176], replicated
- vec_second: float32 [10176], replicated, may hold values from 6553 to 27852
Outputs:
- out_patches: bfloat16 [32768, 768], P(('dp', 'ns'))
- pooled_rows: bfloat16 [512, 768], P(('dp', 'ns'))
- patch_grad: float32 [32768, 768], P(('dp', 'ns'))
- grad_qkv: float32 [2304, 768], P('ns')
- grad_out: float32 [768, 768], P('ns')
- grad_up: float32 [3072, 768], P('ns')
- grad_down: float32 [3072, 768], P('ns')
- moment_qkv: float32 [2304, 768], P('ns')
- moment_out: float32 [768, 768], P('ns')
- moment_up: float32 [3072, 768], P('ns')
- moment_down: float32 [3072, 768], P('ns')
- new_qkv: float32 [2304, 768], P('ns')
- new_out: float32 [768, 768], P('ns')
- new_up: float32 [3072, 768], P('ns')
- new_down: float32 [3072, 768], P('ns')
- copy_qkv: bfloat16 [2304, 768], P('ns')
- copy_out: bfloat16 [768, 768], P('ns')
- copy_up: bfloat16 [3072, 768], P('ns')
- copy_down: bfloat16 [3072, 768], P('ns')
- vector_grad: float32 [10176], replicated
- vector_first: float32 [10176], replicated
- vector_second: float32 [10176], replicated
- vector_new: float32 [10176], replicated
Inputs may be any that keep to these rules, and one draw needn't show every extreme that they name: `counts`: row 4 * i + j lists the images of the device at index i along dp and j along ns in the order of its slots: at most one of 576 patches, and only first in its row, the others of 64, then zeros. The first 2 entries of every row are nonzero, a row sums to at most 1024, and some row sums to exactly 1024. `owners`: in a row no value stands more than 2 times. The first 2 entries of a row are equal, and this value is the same in all rows of one index along ns.
All inputs are finite; a program needn't handle non-finite values.
Results may differ from a plain program's by a relative error of at most 0.04.
Values may be sent and summed in bfloat16 or wider, within the bound.
No kernel may reach another device: no remote copies, remote signals or barrier semaphores. Data moves between devices by JAX's collectives and lax.ppermute only.
A program may use at most 320 MiB of HBM per device.

v0:
```python
import math

import jax
import jax.numpy as jnp
from jax import lax
from jax.sharding import PartitionSpec as P

D = 768
HD = 64
FF = 3072
ITERS = 4
STEP = 10


HIGHEST = lax.Precision.HIGHEST
NS_A = 3.4445
NS_B = -4.775
NS_C = 2.0315
MUON_RATE = 0.8
MUON_DECAY = 0.5
MUON_SHRINK = 0.01
ADAM_RATE = 0.5
BETA_ONE = 0.9
BETA_TWO = 0.95
MASKED = -1e30


def layer_norm(values, gain_vec, bias_vec):
    row_mean = jnp.mean(values, axis=-1, keepdims=True)
    centred = values - row_mean
    variance = jnp.mean(centred * centred, axis=-1, keepdims=True)
    return centred * lax.rsqrt(variance + 1e-06) * gain_vec + bias_vec


def gelu_exact(values):
    return jax.nn.gelu(values, approximate=False)


def head_norms(queries, key_rows, gain_query, bias_query, gain_key):
    return (layer_norm(queries, gain_query, bias_query), layer_norm(key_rows, gain_key, 0.0))


def split_vectors(vectors):
    widths = [D, D, 3 * D, HD, HD, HD, D, D, D, FF, D]
    pieces = []
    start = 0
    for width in widths:
        pieces.append(vectors[start : start + width])
        start = start + width
    return pieces


def split_rows(block_value, lengths):
    pieces = []
    start = 0
    for length in lengths:
        pieces.append(block_value[start : start + length])
        start = start + length
    return pieces


def segment_of(counts_row, slot_count):
    image_ends = jnp.cumsum(counts_row)
    position = jnp.arange(slot_count, dtype=jnp.int32)
    return jnp.sum((image_ends[None, :] <= position[:, None]).astype(jnp.int32), axis=1)


def owner_slots(owners_row, capacity):
    image_total = owners_row.shape[0]
    ordering = jnp.arange(image_total, dtype=jnp.int32)
    earlier = (owners_row[None, :] == owners_row[:, None]) & (ordering[None, :] < ordering[:, None])
    same_before = jnp.sum(earlier.astype(jnp.int32), axis=1)
    return owners_row * capacity + same_before


def masked_scores(query_block, key_low, segment_block, segment):
    scores = (
        jnp.einsum("qhe,khe->hqk", query_block, key_low, preferred_element_type=jnp.float32) * 0.125
    )
    allowed = segment_block[:, None] == segment[None, :]
    return jnp.where(allowed[None], scores, MASKED)


def gram_of(orthogonal):
    return jnp.einsum(
        "rd,re->de", orthogonal, orthogonal, preferred_element_type=jnp.float32
    ).astype(jnp.bfloat16)


def per_device(
    patches,
    counts,
    owners,
    pooled_cot,
    patch_cot,
    master_qkv,
    master_out,
    master_up,
    master_down,
    mom_qkv,
    mom_out,
    mom_up,
    mom_down,
    vectors,
    vec_first,
    vec_second,
):
    dp_count = lax.axis_size("dp")
    ns_count = lax.axis_size("ns")
    slot_count = patches.shape[0]
    image_total = counts.shape[1]
    capacity = pooled_cot.shape[0] // dp_count
    head_count = D // HD
    w_qkv, w_out, w_up, w_down = (
        lax.all_gather(master_qkv.astype(jnp.bfloat16), "ns", axis=0, tiled=True),
        lax.all_gather(master_out.astype(jnp.bfloat16), "ns", axis=0, tiled=True),
        lax.all_gather(master_up.astype(jnp.bfloat16), "ns", axis=0, tiled=True),
        lax.all_gather(master_down.astype(jnp.bfloat16), "ns", axis=0, tiled=True),
    )
    (
        gain_one,
        bias_one,
        bias_qkv,
        gain_query,
        bias_query,
        gain_key,
        bias_out,
        gain_two,
        bias_two,
        bias_up,
        bias_down,
    ) = split_vectors(vectors)
    segment = segment_of(counts[0], slot_count)
    live_mask = (segment < image_total).astype(jnp.float32)
    inputs = patches.astype(jnp.float32)
    normed_one, back_one = jax.vjp(layer_norm, inputs, gain_one, bias_one)
    first_low = normed_one.astype(jnp.bfloat16)
    qkv = jnp.einsum("sd,rd->sr", first_low, w_qkv, preferred_element_type=jnp.float32) + bias_qkv
    queries = qkv[:, :D].reshape(slot_count, head_count, HD)
    key_rows = qkv[:, D : 2 * D].reshape(slot_count, head_count, HD)
    value_rows = qkv[:, 2 * D :].reshape(slot_count, head_count, HD)
    (query_norm, key_norm), back_heads = jax.vjp(
        head_norms, queries, key_rows, gain_query, bias_query, gain_key
    )
    query_low = query_norm.astype(jnp.bfloat16)
    key_low = key_norm.astype(jnp.bfloat16)
    value_low = value_rows.astype(jnp.bfloat16)
    block_rows = min(512, slot_count)
    block_count = slot_count // block_rows
    query_blocks = query_low.reshape(block_count, block_rows, head_count, HD)
    segment_blocks = segment.reshape(block_count, block_rows)

    def attend(operands):
        query_block, segment_block = operands
        scores = masked_scores(query_block, key_low, segment_block, segment)
        row_peak = jnp.max(scores, axis=-1, keepdims=True)
        exponent = jnp.exp(scores - row_peak)
        row_total = jnp.sum(exponent, axis=-1, keepdims=True)
        attn_prob = (exponent / row_total).astype(jnp.bfloat16)
        result = jnp.einsum(
            "hqk,khe->qhe", attn_prob, value_low, preferred_element_type=jnp.float32
        )
        return (result, row_peak + jnp.log(row_total))

    attended, log_totals = lax.map(attend, (query_blocks, segment_blocks))
    attn_low = attended.reshape(slot_count, D).astype(jnp.bfloat16)
    branch = jnp.einsum("sd,ed->se", attn_low, w_out, preferred_element_type=jnp.float32) + bias_out
    middle = inputs + branch
    normed_two, back_two = jax.vjp(layer_norm, middle, gain_two, bias_two)
    second_low = normed_two.astype(jnp.bfloat16)
    pre_act = (
        jnp.einsum("sd,fd->sf", second_low, w_up, preferred_element_type=jnp.float32) + bias_up
    )
    activated, back_gelu = jax.vjp(gelu_exact, pre_act)
    hidden_low = activated.astype(jnp.bfloat16)
    mixed_rows = jnp.dot(hidden_low, w_down, preferred_element_type=jnp.float32) + bias_down
    result_rows = middle + mixed_rows
    out_patches = result_rows.astype(jnp.bfloat16)
    image_ids = jnp.arange(image_total, dtype=jnp.int32)
    picker = (segment[None, :] == image_ids[:, None]).astype(jnp.float32)
    image_sizes = jnp.maximum(counts[0], 1).astype(jnp.float32)[:, None]
    pooled = (jnp.dot(picker, result_rows, precision=HIGHEST) / image_sizes).astype(jnp.bfloat16)
    targets = owner_slots(owners[0], capacity)
    routing = (
        jnp.arange(dp_count * capacity, dtype=jnp.int32)[:, None] == targets[None, :]
    ).astype(jnp.float32)
    outgoing = (
        jnp.dot(routing, pooled.astype(jnp.float32), precision=HIGHEST)
        .astype(jnp.bfloat16)
        .reshape(dp_count, capacity, D)
    )
    arrived = lax.all_to_all(outgoing, "dp", split_axis=0, concat_axis=0, tiled=True)
    pooled_rows = arrived.reshape(dp_count * capacity, D)
    returned = lax.all_to_all(
        pooled_cot.reshape(dp_count, capacity, D), "dp", split_axis=0, concat_axis=0, tiled=True
    )
    image_grad = (
        jnp.dot(
            routing.T,
            returned.reshape(dp_count * capacity, D).astype(jnp.float32),
            precision=HIGHEST,
        )
        / image_sizes
    )
    row_grad = live_mask[:, None] * patch_cot.astype(jnp.float32) + jnp.dot(
        picker.T, image_grad, precision=HIGHEST
    )
    mixed_low = row_grad.astype(jnp.bfloat16)
    grad_down = jnp.einsum("sf,sd->fd", hidden_low, mixed_low, preferred_element_type=jnp.float32)
    down_bias_grad = jnp.sum(mixed_low, axis=0, dtype=jnp.float32)
    hidden_grad = jnp.einsum("sd,fd->sf", mixed_low, w_down, preferred_element_type=jnp.float32)
    (pre_grad,) = back_gelu(hidden_grad)
    pre_low = pre_grad.astype(jnp.bfloat16)
    grad_up = jnp.einsum("sf,sd->fd", pre_low, second_low, preferred_element_type=jnp.float32)
    up_bias_grad = jnp.sum(pre_low, axis=0, dtype=jnp.float32)
    second_grad = jnp.dot(pre_low, w_up, preferred_element_type=jnp.float32)
    middle_part, gain_two_grad, bias_two_grad = back_two(second_grad)
    middle_grad = row_grad + middle_part
    branch_low = middle_grad.astype(jnp.bfloat16)
    grad_out = jnp.einsum("se,sd->ed", branch_low, attn_low, preferred_element_type=jnp.float32)
    out_bias_grad = jnp.sum(branch_low, axis=0, dtype=jnp.float32)
    attn_grad = jnp.dot(branch_low, w_out, preferred_element_type=jnp.float32).astype(jnp.bfloat16)
    grad_blocks_in = attn_grad.reshape(block_count, block_rows, head_count, HD)

    def attend_back(carried, operands):
        key_acc, value_acc = carried
        query_block, segment_block, grad_block, log_total = operands
        scores = masked_scores(query_block, key_low, segment_block, segment)
        attn_prob = jnp.exp(scores - log_total)
        prob_grad = jnp.einsum(
            "qhe,khe->hqk", grad_block, value_low, preferred_element_type=jnp.float32
        )
        row_inner = jnp.sum(attn_prob * prob_grad, axis=-1, keepdims=True)
        score_low = (attn_prob * (prob_grad - row_inner)).astype(jnp.bfloat16)
        query_part = (
            jnp.einsum("hqk,khe->qhe", score_low, key_low, preferred_element_type=jnp.float32)
            * 0.125
        )
        key_acc = (
            key_acc
            + jnp.einsum("hqk,qhe->khe", score_low, query_block, preferred_element_type=jnp.float32)
            * 0.125
        )
        value_acc = value_acc + jnp.einsum(
            "hqk,qhe->khe",
            attn_prob.astype(jnp.bfloat16),
            grad_block,
            preferred_element_type=jnp.float32,
        )
        return ((key_acc, value_acc), query_part)

    zero_grad = jnp.zeros((slot_count, head_count, HD), jnp.float32)
    (key_grad, value_grad), query_parts = lax.scan(
        attend_back,
        (zero_grad, zero_grad),
        (query_blocks, segment_blocks, grad_blocks_in, log_totals),
    )
    query_grad = query_parts.reshape(slot_count, head_count, HD)
    query_raw, key_raw, gain_query_grad, bias_query_grad, gain_key_grad = back_heads(
        (query_grad, key_grad)
    )
    qkv_low = jnp.concatenate(
        [
            query_raw.reshape(slot_count, D),
            key_raw.reshape(slot_count, D),
            value_grad.reshape(slot_count, D),
        ],
        axis=1,
    ).astype(jnp.bfloat16)
    grad_qkv = jnp.einsum("sr,sd->rd", qkv_low, first_low, preferred_element_type=jnp.float32)
    qkv_bias_grad = jnp.sum(qkv_low, axis=0, dtype=jnp.float32)
    first_grad = jnp.dot(qkv_low, w_qkv, preferred_element_type=jnp.float32)
    input_part, gain_one_grad, bias_one_grad = back_one(first_grad)
    patch_grad = middle_grad + input_part
    vector_local = jnp.concatenate(
        [
            gain_one_grad,
            bias_one_grad,
            qkv_bias_grad,
            gain_query_grad,
            bias_query_grad,
            gain_key_grad,
            out_bias_grad,
            gain_two_grad,
            bias_two_grad,
            up_bias_grad,
            down_bias_grad,
        ]
    )
    gradients = (grad_qkv, grad_out, grad_up, grad_down)
    lengths = [gradient.shape[0] // ns_count for gradient in gradients]
    stacked = jnp.concatenate(
        [gradient.reshape(ns_count, length, D) for gradient, length in zip(gradients, lengths)],
        axis=1,
    )
    block_height = stacked.shape[1]
    piece_count = block_height // dp_count
    spread = (
        stacked.reshape(ns_count, dp_count, piece_count, D)
        .transpose(1, 0, 2, 3)
        .reshape(dp_count * ns_count * piece_count, D)
    )
    own_piece = lax.psum_scatter(spread, ("dp", "ns"), scatter_dimension=0, tiled=True)
    old_block = jnp.concatenate([mom_qkv, mom_out, mom_up, mom_down], axis=0)
    vector_grad = lax.psum(vector_local, ("dp", "ns"))
    full_grad = lax.all_gather(own_piece.astype(jnp.bfloat16), "dp", axis=0, tiled=True).astype(
        own_piece.dtype
    )
    full_moment = MUON_DECAY * old_block + full_grad
    moment_list = split_rows(full_moment, lengths)
    norm_squares = lax.psum(jnp.stack([jnp.sum(moment * moment) for moment in moment_list]), "ns")
    grad_parts = split_rows(full_grad, lengths)
    moment_parts = split_rows(full_moment, lengths)
    ortho_list = [
        (moment_parts[kind_index] / (jnp.sqrt(norm_squares[kind_index]) + 1e-07)).astype(
            jnp.bfloat16
        )
        for kind_index in range(4)
    ]
    for iteration in range(ITERS):
        gram_parts = (
            lax.psum_scatter(gram_of(ortho_list[0]), "ns", scatter_dimension=0, tiled=True).astype(
                jnp.float32
            ),
            lax.psum_scatter(gram_of(ortho_list[1]), "ns", scatter_dimension=0, tiled=True).astype(
                jnp.float32
            ),
            lax.psum_scatter(gram_of(ortho_list[2]), "ns", scatter_dimension=0, tiled=True).astype(
                jnp.float32
            ),
            lax.psum_scatter(gram_of(ortho_list[3]), "ns", scatter_dimension=0, tiled=True).astype(
                jnp.float32
            ),
        )
        gram_sums = (
            lax.all_gather(gram_parts[0].astype(jnp.bfloat16), "ns", axis=0, tiled=True).astype(
                jnp.float32
            ),
            lax.all_gather(gram_parts[1].astype(jnp.bfloat16), "ns", axis=0, tiled=True).astype(
                jnp.float32
            ),
            lax.all_gather(gram_parts[2].astype(jnp.bfloat16), "ns", axis=0, tiled=True).astype(
                jnp.float32
            ),
            lax.all_gather(gram_parts[3].astype(jnp.bfloat16), "ns", axis=0, tiled=True).astype(
                jnp.float32
            ),
        )
        renewed = []
        for orthogonal, gram_sum in zip(ortho_list, gram_sums):
            gram_low = gram_sum.astype(jnp.bfloat16)
            squared = jnp.dot(gram_low, gram_low, preferred_element_type=jnp.float32)
            mixer_low = (NS_B * gram_sum + NS_C * squared).astype(jnp.bfloat16)
            renewed.append(
                (
                    NS_A * orthogonal.astype(jnp.float32)
                    + jnp.dot(orthogonal, mixer_low, preferred_element_type=jnp.float32)
                ).astype(jnp.bfloat16)
            )
        ortho_list = renewed
    masters = (master_qkv, master_out, master_up, master_down)
    new_masters = []
    for kind_index in range(4):
        full_rows = lengths[kind_index] * ns_count
        step_scale = MUON_RATE * math.sqrt(max(1.0, full_rows / D))
        new_masters.append(
            masters[kind_index] * (1.0 - MUON_RATE * MUON_SHRINK)
            - step_scale * ortho_list[kind_index].astype(jnp.float32)
        )
    vector_first = BETA_ONE * vec_first + (1.0 - BETA_ONE) * vector_grad
    vector_second = BETA_TWO * vec_second + (1.0 - BETA_TWO) * vector_grad * vector_grad
    first_hat = vector_first / (1.0 - BETA_ONE**STEP)
    second_hat = vector_second / (1.0 - BETA_TWO**STEP)
    vector_new = vectors - ADAM_RATE * first_hat / (jnp.sqrt(second_hat) + 1e-08)
    return (
        out_patches,
        pooled_rows,
        patch_grad,
        grad_parts[0],
        grad_parts[1],
        grad_parts[2],
        grad_parts[3],
        moment_parts[0],
        moment_parts[1],
        moment_parts[2],
        moment_parts[3],
        new_masters[0],
        new_masters[1],
        new_masters[2],
        new_masters[3],
        new_masters[0].astype(jnp.bfloat16),
        new_masters[1].astype(jnp.bfloat16),
        new_masters[2].astype(jnp.bfloat16),
        new_masters[3].astype(jnp.bfloat16),
        vector_grad,
        vector_first,
        vector_second,
        vector_new,
    )


def solution(mesh):
    placed = (
        P(("dp", "ns"), None),
        P(("dp", "ns"), None),
        P(("dp", "ns"), None),
        P(("dp", "ns"), None),
        P(("dp", "ns"), None),
        P("ns", None),
        P("ns", None),
        P("ns", None),
        P("ns", None),
        P("ns", None),
        P("ns", None),
        P("ns", None),
        P("ns", None),
        P(),
        P(),
        P(),
    )
    return jax.shard_map(
        per_device,
        mesh=mesh,
        in_specs=placed,
        out_specs=(
            P(("dp", "ns"), None),
            P(("dp", "ns"), None),
            P(("dp", "ns"), None),
            P("ns", None),
            P("ns", None),
            P("ns", None),
            P("ns", None),
            P("ns", None),
            P("ns", None),
            P("ns", None),
            P("ns", None),
            P("ns", None),
            P("ns", None),
            P("ns", None),
            P("ns", None),
            P("ns", None),
            P("ns", None),
            P("ns", None),
            P("ns", None),
            P(),
            P(),
            P(),
            P(),
        ),
        check_vma=False,
    )
```

profile of v0, /device:TPU:0, one launch (start us, length us, event | category | flops | bytes accessed | tf_op | source)
XLA Modules:
  0.0 1678.0 jit_solution(7972354581490045434)
XLA Ops:
  79.6 75.1 %while.29 = (s32[]{:T(128)}, bf16[2,512,12,64]{1,3,2,0:T(8,128)(2,1)}, f32[2,12,512,1]{2,1,3,0:T(8,128)S(1)}, s32[2,512]{1,0:T(2,128)S(1)}, s32[1024]{0:T(1024)S...) while((s32[]{:T(128)}, ...), condition=%wide.region_11.12_spmd.clone, body=%wide.region_8.11_spmd.sunk.clone | while | flops 1686628352 | bytes 196593840 | solution.py:165
  169.5 38.2 %multiply_convert_fusion.1 = (bf16[1024,3072]{1,0:T(8,128)(2,1)}, f32[1024,3072]{1,0:T(8,128)}, f32[1024,3072]{1,0:T(8,128)}) fusion(f32[3072]{0:T(1024)S(1)} %copy-done.108, bf16[3072,768]{1,0:T(8,128)(2,1)} %all-gather.26.cloned.1.call-done, f32[1024,768]{0,1:T(8,128)} %copy-done.25, f32[768]{0:T(1024)S(1)} %copy-done.115, f32[768]{0:T(1024)S(1)} %copy-done.97, ...), kind=kOutput, calls=%fused_computation.49 | convolution fusion | flops 5043388416 | bytes 39348224 | tf_op jit(solution)/shard_map/sd,fd->sf/dot_general | solution.py:172
  207.7 19.4 %convert_reduce_fusion = (f32[3072]{0:T(1024)}, bf16[1024,3072]{1,0:T(8,128)(2,1)}) fusion(f32[1024,3072]{1,0:T(8,128)} %get-tuple-element.357, bf16[1024,768]{0,1:T(8,128)(2,1)} %get-tuple-element.343, bf16[3072,768]{1,0:T(8,128)(2,1)} %all-gather.28.cloned.1.call-done, f32[1024,3072]{1,0:T(8,128)} %get-tuple-element.386, f32[3072]{0:T(1024)S(1)} %copy-done.108), kind=kOutput, calls=%fused_computation.47 | convolution fusion | flops 4885312512 | bytes 37773312 | tf_op jit(solution)/shard_map/sd,fd->sf/dot_general | solution.py:211
  255.0 168.5 %while.30 = (s32[]{:T(128)}, f32[1024,12,64]{0,2,1:T(8,128)}, f32[1024,12,64]{0,2,1:T(8,128)}, f32[2,512,12,64]{1,3,2,0:T(8,128)}, bf16[2,512,12,64]{1,3,2,0:T(8...) while((s32[]{:T(128)}, f32[1024,12,64]{0,2,1:T(8,128)}, ...), condition=%wide.region_19.20_spmd.clone.clone, body=%wide.region_17.19_spmd.clone.sunk.clone | while | flops 4125747200 | bytes 257091888 | solution.py:253
  267.8 18.1 %multiply_reduce_fusion.16 = (f32[12,512]{1,0:T(8,128)S(1)}, f32[12,512,1024]{2,1,0:T(8,128)}) fusion(f32[12,512,1024]{2,1,0:T(8,128)} %fusion.271, f32[12,512]{1,0:T(8,128)S(1)} %dynamic-slice_bitcast_fusion.3, pred[512,1024]{1,0:T(8,128)(4,1)S(1)} %broadcast_compare_fusion.7, bf16[1024,12,64]{0,2,1:T(8,128)(2,1)} %copy-done.6, ...), kind=kOutput, calls=%fused_computation.17.clone.1.clone | convolution fusion | flops 836757504 | bytes 53264388 | tf_op jit(solution)/shard_map/while/body/eval_jaxpr/qhe,khe->hqk/dot_general | solution.py:230
  285.9 21.2 %multiply_convert_fusion.5 = bf16[12,512,1024]{2,1,0:T(8,128)(2,1)} fusion(f32[12,512,1024]{2,1,0:T(8,128)} %get-tuple-element.560, f32[12,512,1024]{2,1,0:T(8,128)} %fusion.271, f32[12,512]{1,0:T(8,128)S(1)} %get-tuple-element.561, f32[12,512]{1,0:T(8,128)S(1)} %dynamic-slice_bitcast_fusion.3, pred[512,1024]{1,0:T(8,128)(4,1)S(1)} %broadcast_compare_fusion.7), kind=kLoop, calls=%fused_computation.16.clone.1.clone | loop fusion | flops 37748736 | bytes 63488000 | tf_op jit(solution)/shard_map/while/body/eval_jaxpr/convert_element_type | solution.py:234
  351.3 18.1 %multiply_reduce_fusion.16 = (f32[12,512]{1,0:T(8,128)S(1)}, f32[12,512,1024]{2,1,0:T(8,128)}) fusion(f32[12,512,1024]{2,1,0:T(8,128)} %fusion.271, f32[12,512]{1,0:T(8,128)S(1)} %dynamic-slice_bitcast_fusion.3, pred[512,1024]{1,0:T(8,128)(4,1)S(1)} %broadcast_compare_fusion.7, bf16[1024,12,64]{0,2,1:T(8,128)(2,1)} %copy-done.6, ...), kind=kOutput, calls=%fused_computation.17.clone.1.clone | convolution fusion | flops 836757504 | bytes 53264388 | tf_op jit(solution)/shard_map/while/body/eval_jaxpr/qhe,khe->hqk/dot_general | solution.py:230
  369.4 21.2 %multiply_convert_fusion.5 = bf16[12,512,1024]{2,1,0:T(8,128)(2,1)} fusion(f32[12,512,1024]{2,1,0:T(8,128)} %get-tuple-element.560, f32[12,512,1024]{2,1,0:T(8,128)} %fusion.271, f32[12,512]{1,0:T(8,128)S(1)} %get-tuple-element.561, f32[12,512]{1,0:T(8,128)S(1)} %dynamic-slice_bitcast_fusion.3, pred[512,1024]{1,0:T(8,128)(4,1)S(1)} %broadcast_compare_fusion.7), kind=kLoop, calls=%fused_computation.16.clone.1.clone | loop fusion | flops 37748736 | bytes 63488000 | tf_op jit(solution)/shard_map/while/body/eval_jaxpr/convert_element_type | solution.py:234
  457.0 13.0 multiply_reduce_fusion.3
  514.6 17.7 %pad_maximum_fusion = f32[4,2304,768]{2,1,0:T(8,128)} fusion(f32[4,768,768]{2,1,0:T(8,128)} %bitcast.280, f32[4,768,768]{2,1,0:T(8,128)} %bitcast.279, f32[4,192,768]{2,1,0:T(8,128)} %fusion.53, f32[4,576,768]{2,1,0:T(8,128)S(1)} %bitcast.281), kind=kLoop, calls=%fused_computation.44 | loop fusion | flops 21233664 | bytes 56623104 | tf_op jit(solution)/shard_map/concatenate | solution.py:292
  532.3 20.2 %copy.114 = f32[4,8,288,768]{3,2,0,1:T(8,128)} copy(f32[4,8,288,768]{3,2,1,0:T(8,128)} %bitcast.266) | data formatting | bytes 56623104 | tf_op jit(solution)/shard_map/reshape | solution.py:299
  552.6 263.7 %reduce-scatter.18.cloned.1.call-done = f32[288,768]{1,0:T(8,128)} async-done(((f32[9216,768]{1,0:T(8,128)}), f32[288,768]{1,0:T(8,128)}) %reduce-scatter.18.cloned.1.call-update) | async-done | bytes 884752 | tf_op jit(solution)/shard_map/reduce_scatter | solution.py:303
  818.3 65.4 %all-gather.30.cloned.1.call-done = bf16[2304,768]{1,0:T(8,128)(2,1)} async-done(((bf16[288,768]{1,0:T(8,128)(2,1)}), bf16[2304,768]{1,0:T(8,128)(2,1)}) %all-gather.30.cloned.1.call-update) | async-done | bytes 3538960 | tf_op jit(solution)/shard_map/all_gather | solution.py:306
  928.9 29.0 %reduce-scatter.20.cloned.1.call-done = bf16[192,768]{1,0:T(8,128)(2,1)} async-done(((bf16[768,768]{1,0:T(8,128)(2,1)}), bf16[192,768]{1,0:T(8,128)(2,1)}) %reduce-scatter.20.cloned.1.call-update) | async-done | bytes 294928 | tf_op jit(solution)/shard_map/reduce_scatter | solution.py:322
  957.9 28.8 %reduce-scatter.36.cloned.1.call-done = bf16[192,768]{1,0:T(8,128)(2,1)} async-done(((bf16[768,768]{1,0:T(8,128)(2,1)}), bf16[192,768]{1,0:T(8,128)(2,1)}) %reduce-scatter.36.cloned.1.call-update) | async-done | bytes 294928 | tf_op jit(solution)/shard_map/reduce_scatter | solution.py:328
  986.8 28.8 %reduce-scatter.44.cloned.1.call-done = bf16[192,768]{1,0:T(8,128)(2,1)} async-done(((bf16[768,768]{1,0:T(8,128)(2,1)}), bf16[192,768]{1,0:T(8,128)(2,1)}) %reduce-scatter.44.cloned.1.call-update) | async-done | bytes 294928 | tf_op jit(solution)/shard_map/reduce_scatter | solution.py:331
  1015.7 19.0 %all-gather.40.cloned.1.call-done = bf16[768,768]{1,0:T(8,128)(2,1)} async-done(((bf16[192,768]{1,0:T(8,128)(2,1)}), bf16[768,768]{1,0:T(8,128)(2,1)}) %all-gather.40.cloned.1.call-update) | async-done | bytes 1179664 | tf_op jit(solution)/shard_map/all_gather | solution.py:339
  1040.0 13.6 all-gather.32.cloned.1.call-done
  1101.0 19.3 %reduce-scatter.30.cloned.1.call-done = bf16[192,768]{1,0:T(8,128)(2,1)} async-done(((bf16[768,768]{1,0:T(8,128)(2,1)}), bf16[192,768]{1,0:T(8,128)(2,1)}) %reduce-scatter.30.cloned.1.call-update) | async-done | bytes 294928 | tf_op jit(solution)/shard_map/reduce_scatter | solution.py:325
  1120.4 28.8 %reduce-scatter.22.cloned.1.call-done = bf16[192,768]{1,0:T(8,128)(2,1)} async-done(((bf16[768,768]{1,0:T(8,128)(2,1)}), bf16[192,768]{1,0:T(8,128)(2,1)}) %reduce-scatter.22.cloned.1.call-update) | async-done | bytes 294928 | tf_op jit(solution)/shard_map/reduce_scatter | solution.py:322
  1149.3 28.7 %reduce-scatter.38.cloned.1.call-done = bf16[192,768]{1,0:T(8,128)(2,1)} async-done(((bf16[768,768]{1,0:T(8,128)(2,1)}), bf16[192,768]{1,0:T(8,128)(2,1)}) %reduce-scatter.38.cloned.1.call-update) | async-done | bytes 294928 | tf_op jit(solution)/shard_map/reduce_scatter | solution.py:328
  1178.0 28.3 %reduce-scatter.46.cloned.1.call-done = bf16[192,768]{1,0:T(8,128)(2,1)} async-done(((bf16[768,768]{1,0:T(8,128)(2,1)}), bf16[192,768]{1,0:T(8,128)(2,1)}) %reduce-scatter.46.cloned.1.call-update) | async-done | bytes 294928 | tf_op jit(solution)/shard_map/reduce_scatter | solution.py:331
  1206.4 19.0 %all-gather.42.cloned.1.call-done = bf16[768,768]{1,0:T(8,128)(2,1)} async-done(((bf16[192,768]{1,0:T(8,128)(2,1)}), bf16[768,768]{1,0:T(8,128)(2,1)}) %all-gather.42.cloned.1.call-update) | async-done | bytes 1179664 | tf_op jit(solution)/shard_map/all_gather | solution.py:339
  1230.6 13.6 all-gather.34.cloned.1.call-done
  1291.7 19.5 %reduce-scatter.32.cloned.1.call-done = bf16[192,768]{1,0:T(8,128)(2,1)} async-done(((bf16[768,768]{1,0:T(8,128)(2,1)}), bf16[192,768]{1,0:T(8,128)(2,1)}) %reduce-scatter.32.cloned.1.call-update) | async-done | bytes 294928 | tf_op jit(solution)/shard_map/reduce_scatter | solution.py:325
  1311.3 28.8 %reduce-scatter.24.cloned.1.call-done = bf16[192,768]{1,0:T(8,128)(2,1)} async-done(((bf16[768,768]{1,0:T(8,128)(2,1)}), bf16[192,768]{1,0:T(8,128)(2,1)}) %reduce-scatter.24.cloned.1.call-update) | async-done | bytes 294928 | tf_op jit(solution)/shard_map/reduce_scatter | solution.py:322
  1340.2 28.8 %reduce-scatter.40.cloned.1.call-done = bf16[192,768]{1,0:T(8,128)(2,1)} async-done(((bf16[768,768]{1,0:T(8,128)(2,1)}), bf16[192,768]{1,0:T(8,128)(2,1)}) %reduce-scatter.40.cloned.1.call-update) | async-done | bytes 294928 | tf_op jit(solution)/shard_map/reduce_scatter | solution.py:328
  1369.1 28.3 %reduce-scatter.48.cloned.1.call-done = bf16[192,768]{1,0:T(8,128)(2,1)} async-done(((bf16[768,768]{1,0:T(8,128)(2,1)}), bf16[192,768]{1,0:T(8,128)(2,1)}) %reduce-scatter.48.cloned.1.call-update) | async-done | bytes 294928 | tf_op jit(solution)/shard_map/reduce_scatter | solution.py:331
  1397.5 18.8 %all-gather.44.cloned.1.call-done = bf16[768,768]{1,0:T(8,128)(2,1)} async-done(((bf16[192,768]{1,0:T(8,128)(2,1)}), bf16[768,768]{1,0:T(8,128)(2,1)}) %all-gather.44.cloned.1.call-update) | async-done | bytes 1179664 | tf_op jit(solution)/shard_map/all_gather | solution.py:339
  1421.7 13.6 all-gather.36.cloned.1.call-done
  1482.9 19.3 %reduce-scatter.34.cloned.1.call-done = bf16[192,768]{1,0:T(8,128)(2,1)} async-done(((bf16[768,768]{1,0:T(8,128)(2,1)}), bf16[192,768]{1,0:T(8,128)(2,1)}) %reduce-scatter.34.cloned.1.call-update) | async-done | bytes 294928 | tf_op jit(solution)/shard_map/reduce_scatter | solution.py:325
  1562.7 39.9 %psum.15 = f32[10176]{0:T(1024)S(1)} all-reduce(f32[10176]{0:T(1024)S(1)} %concatenate.16), channel_id=1, replica_groups=mesh['dp'=8,'ns'=4] {'dp','ns'}, use_global_device_ids=true, to_apply=%region_59.60 | all-reduce | flops 10176 | bytes 81408 | tf_op jit(solution)/shard_map/psum | solution.py:305
  (569 shorter events, 687.9 us)
Async XLA Ops:
  9.9 149.4 %all-gather.24.cloned.1.call-start = ((), (), s32[]{:S(2)}) async-start(), calls=%async_computation.20 | async-start | bytes 1474560 | tf_op jit(solution)/shard_map/all_gather | solution.py:116
  10.8 158.8 %all-gather.26.cloned.1.call-start = ((), (), s32[]{:S(2)}) async-start(), calls=%async_computation.21 | async-start | bytes 5898240 | tf_op jit(solution)/shard_map/all_gather | solution.py:117
  19.9 187.8 %all-gather.28.cloned.1.call-start = ((), (), s32[]{:S(2)}) async-start(), calls=%async_computation.22 | async-start | bytes 5898240 | tf_op jit(solution)/shard_map/all_gather | solution.py:118
  23.1 793.2 %reduce-scatter.18.cloned.1.call-start = ((), (), s32[]{:S(2)}) async-start(), calls=%async_computation.23 | async-start | bytes 29196288 | tf_op jit(solution)/shard_map/reduce_scatter | solution.py:303
  552.5 331.2 %all-gather.30.cloned.1.call-start = ((), (), s32[]{:S(2)}) async-start(), calls=%async_computation.24 | async-start | bytes 3981312 | tf_op jit(solution)/shard_map/all_gather | solution.py:306
  818.3 110.5 %reduce-scatter.28.cloned.1.call-start = ((), (), s32[]{:S(2)}) async-start(), calls=%async_computation.33 | async-start | bytes 1474560 | tf_op jit(solution)/shard_map/reduce_scatter | solution.py:325
  917.5 117.2 %all-gather.40.cloned.1.call-start = ((), (), s32[]{:S(2)}) async-start(), calls=%async_computation.34 | async-start | bytes 1474560 | tf_op jit(solution)/shard_map/all_gather | solution.py:339
  928.8 124.8 %all-gather.32.cloned.1.call-start = ((), (), s32[]{:S(2)}) async-start(), calls=%async_computation.26 | async-start | bytes 1474560 | tf_op jit(solution)/shard_map/all_gather | solution.py:336
  957.9 114.8 %all-gather.48.cloned.1.call-start = ((), (), s32[]{:S(2)}) async-start(), calls=%async_computation.42 | async-start | bytes 1474560 | tf_op jit(solution)/shard_map/all_gather | solution.py:342
  986.7 104.8 %all-gather.56.cloned.1.call-start = ((), (), s32[]{:S(2)}) async-start(), calls=%async_computation.50 | async-start | bytes 1474560 | tf_op jit(solution)/shard_map/all_gather | solution.py:345
  1015.6 104.7 %reduce-scatter.30.cloned.1.call-start = ((), (), s32[]{:S(2)}) async-start(), calls=%async_computation.35 | async-start | bytes 1474560 | tf_op jit(solution)/shard_map/reduce_scatter | solution.py:325
  1039.9 109.3 %reduce-scatter.22.cloned.1.call-start = ((), (), s32[]{:S(2)}) async-start(), calls=%async_computation.27 | async-start | bytes 1474560 | tf_op jit(solution)/shard_map/reduce_scatter | solution.py:322
  1060.7 117.3 %reduce-scatter.38.cloned.1.call-start = ((), (), s32[]{:S(2)}) async-start(), calls=%async_computation.43 | async-start | bytes 1474560 | tf_op jit(solution)/shard_map/reduce_scatter | solution.py:328
  1083.2 123.1 %reduce-scatter.46.cloned.1.call-start = ((), (), s32[]{:S(2)}) async-start(), calls=%async_computation.51 | async-start | bytes 1474560 | tf_op jit(solution)/shard_map/reduce_scatter | solution.py:331
  1100.9 124.4 %all-gather.42.cloned.1.call-start = ((), (), s32[]{:S(2)}) async-start(), calls=%async_computation.36 | async-start | bytes 1474560 | tf_op jit(solution)/shard_map/all_gather | solution.py:339
  1120.3 123.9 %all-gather.34.cloned.1.call-start = ((), (), s32[]{:S(2)}) async-start(), calls=%async_computation.28 | async-start | bytes 1474560 | tf_op jit(solution)/shard_map/all_gather | solution.py:336
  1149.2 114.1 %all-gather.50.cloned.1.call-start = ((), (), s32[]{:S(2)}) async-start(), calls=%async_computation.44 | async-start | bytes 1474560 | tf_op jit(solution)/shard_map/all_gather | solution.py:342
  1206.3 104.9 %reduce-scatter.32.cloned.1.call-start = ((), (), s32[]{:S(2)}) async-start(), calls=%async_computation.37 | async-start | bytes 1474560 | tf_op jit(solution)/shard_map/reduce_scatter | solution.py:325
  1230.6 109.6 %reduce-scatter.24.cloned.1.call-start = ((), (), s32[]{:S(2)}) async-start(), calls=%async_computation.29 | async-start | bytes 1474560 | tf_op jit(solution)/shard_map/reduce_scatter | solution.py:322
  1250.5 118.6 %reduce-scatter.40.cloned.1.call-start = ((), (), s32[]{:S(2)}) async-start(), calls=%async_computation.45 | async-start | bytes 1474560 | tf_op jit(solution)/shard_map/reduce_scatter | solution.py:328
  1272.5 124.9 %reduce-scatter.48.cloned.1.call-start = ((), (), s32[]{:S(2)}) async-start(), calls=%async_computation.53 | async-start | bytes 1474560 | tf_op jit(solution)/shard_map/reduce_scatter | solution.py:331
  1291.7 124.6 %all-gather.44.cloned.1.call-start = ((), (), s32[]{:S(2)}) async-start(), calls=%async_computation.38 | async-start | bytes 1474560 | tf_op jit(solution)/shard_map/all_gather | solution.py:339
  1311.3 124.1 %all-gather.36.cloned.1.call-start = ((), (), s32[]{:S(2)}) async-start(), calls=%async_computation.30 | async-start | bytes 1474560 | tf_op jit(solution)/shard_map/all_gather | solution.py:336
  1340.2 114.2 %all-gather.52.cloned.1.call-start = ((), (), s32[]{:S(2)}) async-start(), calls=%async_computation.46 | async-start | bytes 1474560 | tf_op jit(solution)/shard_map/all_gather | solution.py:342
  1397.4 104.8 %reduce-scatter.34.cloned.1.call-start = ((), (), s32[]{:S(2)}) async-start(), calls=%async_computation.39 | async-start | bytes 1474560 | tf_op jit(solution)/shard_map/reduce_scatter | solution.py:325
  1421.7 109.7 %reduce-scatter.26.cloned.1.call-start = ((), (), s32[]{:S(2)}) async-start(), calls=%async_computation.31 | async-start | bytes 1474560 | tf_op jit(solution)/shard_map/reduce_scatter | solution.py:322
  1441.8 117.7 %reduce-scatter.42.cloned.1.call-start = ((), (), s32[]{:S(2)}) async-start(), calls=%async_computation.47 | async-start | bytes 1474560 | tf_op jit(solution)/shard_map/reduce_scatter | solution.py:328
  1460.9 157.4 %reduce-scatter.50.cloned.1.call-start = ((), (), s32[]{:S(2)}) async-start(), calls=%async_computation.55 | async-start | bytes 1474560 | tf_op jit(solution)/shard_map/reduce_scatter | solution.py:331
  1482.5 140.6 %all-gather.46.cloned.1.call-start = ((), (), s32[]{:S(2)}) async-start(), calls=%async_computation.40 | async-start | bytes 1474560 | tf_op jit(solution)/shard_map/all_gather | solution.py:339
  1520.1 107.9 %all-gather.38.cloned.1.call-start = ((), (), s32[]{:S(2)}) async-start(), calls=%async_computation.32 | async-start | bytes 1474560 | tf_op jit(solution)/shard_map/all_gather | solution.py:336
  1531.4 113.9 %all-gather.54.cloned.1.call-start = ((), (), s32[]{:S(2)}) async-start(), calls=%async_computation.48 | async-start | bytes 1474560 | tf_op jit(solution)/shard_map/all_gather | solution.py:342
  1559.6 104.6 %all-gather.62.cloned.1.call-start = ((), (), s32[]{:S(2)}) async-start(), calls=%async_computation.56 | async-start | bytes 1474560 | tf_op jit(solution)/shard_map/all_gather | solution.py:345
  (150 other events, 3178.2 us)
Sparse Core Ops, SparseCore 0:
  10.2 33.4 all-gather.21
  45.8 17.4 all-gather.23
  65.5 37.4 all-gather.25
  104.9 37.4 all-gather.27
  552.7 263.5 reduce-scatter.17
  818.9 64.7 all-gather.29
  904.3 24.4 reduce-scatter.27
  932.1 25.6 reduce-scatter.19
  961.0 25.6 reduce-scatter.35
  989.9 25.6 reduce-scatter.43
  1017.2 17.4 all-gather.39
  1036.1 17.4 all-gather.31
  1055.1 17.4 all-gather.47
  1094.5 25.7 reduce-scatter.29
  1123.5 25.7 reduce-scatter.21
  1152.2 25.7 reduce-scatter.37
  1180.5 25.6 reduce-scatter.45
  1226.7 17.4 all-gather.33
  1245.8 17.4 all-gather.49
  1264.9 17.4 all-gather.57
  1285.5 25.7 reduce-scatter.31
  1314.4 25.7 reduce-scatter.23
  1343.3 25.7 reduce-scatter.39
  1371.7 25.6 reduce-scatter.47
  1398.8 17.4 all-gather.43
  1455.8 17.4 all-gather.59
  1476.5 25.7 reduce-scatter.33
  1505.5 25.7 reduce-scatter.25
  1533.8 25.7 reduce-scatter.41
  1562.2 25.7 reduce-scatter.49
  1589.6 17.9 all-gather.45
  1627.7 17.4 all-gather.53
  (6 shorter events, 104.2 us)
where the time goes:
time: 1690 us; the launch traced here: 1680 us
  waiting for transfers between devices  877 us (52%)
  matrix products  424 us (25%)
  other arithmetic  167 us (10%)
  local copies, waits for them, and re-layouts  130 us (8%)
  blocking collectives  45.5 us (3%)
  between operations  18.8 us (1%)
    reduce_scatter x1, waiting for transfers between devices, per_device(): lax.psum_scatter(spread, ('dp', 'ns'), scatter_dimension=0, tiled=True)  264 us
    reduce_scatter x4, waiting for transfers between devices, per_device(): lax.psum_scatter(gram_of(ortho_list[2]), 'ns', scatter_dimension=0, tiled...  98.4 us
    reduce_scatter x4, waiting for transfers between devices, per_device(): lax.psum_scatter(gram_of(ortho_list[0]), 'ns', scatter_dimension=0, tiled...  97.8 us
    reduce_scatter x4, waiting for transfers between devices, per_device(): lax.psum_scatter(gram_of(ortho_list[3]), 'ns', scatter_dimension=0, tiled...  85.3 us
    dot_general x16, matrix products, per_device(): jnp.dot(orthogonal, mixer_low, preferred_element_type=jnp.float32)  81.4 us
    reduce_scatter x4, waiting for transfers between devices, per_device(): lax.psum_scatter(gram_of(ortho_list[1]), 'ns', scatter_dimension=0, tiled...  69.4 us
    all_gather x1, waiting for transfers between devices, per_device(): lax.all_gather(own_piece.astype(jnp.bfloat16), 'dp', axis=0, tiled=True)  65.4 us
    all_gather x4, waiting for transfers between devices, per_device(): lax.all_gather(gram_parts[1].astype(jnp.bfloat16), 'ns', axis=0, tiled=True)  56.8 us
  transfers between devices with their start and end apart: 40, of which 32 were waited for; matrix products, arithmetic and copies ran while one was open for 20% of the time, Pallas kernels for 0%

commit v1 on v0

v1 whole, which is shorter than its diff:
```python
import functools
import math

import jax
import jax.numpy as jnp
from jax import lax
from jax.experimental import pallas as pl
from jax.experimental.pallas import tpu as pltpu
from jax.sharding import PartitionSpec as P

D = 768
HD = 64
FF = 3072
ITERS = 4
STEP = 10


NS_A = 3.4445
NS_B = -4.775
NS_C = 2.0315
MUON_RATE = 0.8
MUON_DECAY = 0.5
MUON_SHRINK = 0.01
ADAM_RATE = 0.5
BETA_ONE = 0.9
BETA_TWO = 0.95
MASKED = -1e30


def split_vectors(vectors):
    widths = [D, D, 3 * D, HD, HD, HD, D, D, D, FF, D]
    pieces = []
    start = 0
    for width in widths:
        pieces.append(vectors[start : start + width])
        start = start + width
    return pieces


def owner_slots(owners_row, capacity):
    image_total = owners_row.shape[0]
    ordering = jnp.arange(image_total, dtype=jnp.int32)
    earlier = (owners_row[None, :] == owners_row[:, None]) & (ordering[None, :] < ordering[:, None])
    same_before = jnp.sum(earlier.astype(jnp.int32), axis=1)
    return owners_row * capacity + same_before


def xor_pairs(count, bit):
    return [(index, index ^ (1 << bit)) for index in range(count)]


def swap(value, axis, bit):
    return lax.ppermute(value, axis, xor_pairs(lax.axis_size(axis), bit))


def bit_of(axis, bit):
    return (lax.axis_index(axis) >> bit) & 1


def bits_in(axis):
    return (lax.axis_size(axis) - 1).bit_length()


def add_low(first, second):
    return (first.astype(jnp.float32) + second.astype(jnp.float32)).astype(jnp.bfloat16)


def sum_rows(blocks):
    value = blocks
    for bit in range(bits_in("ns")):
        mine = bit_of("ns", bit)
        pairs = value.reshape(value.shape[0] // 2, 2, *value.shape[1:])
        keep = lax.dynamic_index_in_dim(pairs, mine, 1, keepdims=False)
        send = lax.dynamic_index_in_dim(pairs, 1 - mine, 1, keepdims=False)
        value = add_low(keep, swap(send, "ns", bit))
    value = value[0]
    halved = min(2, bits_in("dp"))
    for bit in range(halved):
        mine = bit_of("dp", bit)
        pairs = value.reshape(2, value.shape[0] // 2, D)
        keep = lax.dynamic_index_in_dim(pairs, mine, 0, keepdims=False)
        send = lax.dynamic_index_in_dim(pairs, 1 - mine, 0, keepdims=False)
        value = add_low(keep, swap(send, "dp", bit))
    for bit in range(halved, bits_in("dp")):
        value = add_low(value, swap(value, "dp", bit))
    for bit in reversed(range(halved)):
        mine = bit_of("dp", bit)
        other = swap(value, "dp", bit)
        low_half = jnp.where(mine == 0, value, other)
        high_half = jnp.where(mine == 0, other, value)
        value = jnp.concatenate([low_half, high_half], axis=0)
    return value


def sum_everywhere(value):
    for axis in ("ns", "dp"):
        for bit in range(bits_in(axis)):
            value = value + swap(value, axis, bit)
    return value


def sum_gram(gram):
    gram = gram + swap(gram, "ns", 0)
    count = bits_in("ns")
    if count == 1:
        return gram
    mine = bit_of("ns", 0)
    half = lax.dynamic_index_in_dim(gram.reshape(2, D // 2, D), mine, 0, keepdims=False)
    for bit in range(1, count):
        half = half + swap(half, "ns", bit)
    other = swap(half, "ns", 0)
    low_half = jnp.where(mine == 0, half, other)
    high_half = jnp.where(mine == 0, other, half)
    return jnp.concatenate([low_half, high_half], axis=0)


def split_low(value):
    high = lax.reduce_precision(value, 8, 7)
    return high.astype(jnp.bfloat16), (value - high).astype(jnp.bfloat16)


def dot32(first, second):
    return jnp.dot(first, second, preferred_element_type=jnp.float32)


def orthogonalise(moment_low, gram_raw):
    scale = 1.0 / (jnp.sqrt(jnp.trace(gram_raw)) + 1e-07)
    gram = gram_raw * (scale * scale)
    rows = moment_low
    for iteration in range(ITERS):
        gram_high, gram_rest = split_low(gram)
        mixer = (NS_B * gram + NS_C * dot32(gram_high, gram_high)).astype(jnp.bfloat16)
        renewed = NS_A * rows.astype(jnp.float32) + dot32(rows, mixer)
        if iteration == 0:
            renewed = renewed * scale
        if iteration == ITERS - 1:
            return renewed
        rows = renewed.astype(jnp.bfloat16)
        middle = NS_A * gram + dot32(gram_high, mixer) + dot32(gram_rest, mixer)
        middle_high, middle_rest = split_low(middle)
        gram = NS_A * middle + dot32(mixer, middle_high) + dot32(mixer, middle_rest)


LOW = jnp.bfloat16
F32 = jnp.float32
HEADS = D // HD
BIG = 576
SMALL = 64
TILE = 256
VMEM_LIMIT = 60 * 1024 * 1024


def mm(first, second, first_dim=1, second_dim=0):
    return lax.dot_general(
        first,
        second,
        (((first_dim,), (second_dim,)), ((), ())),
        preferred_element_type=F32,
    )


def split_value(value):
    high = value.astype(LOW)
    return high, (value - high.astype(F32)).astype(LOW)


def normalise(values):
    row_mean = jnp.mean(values, axis=-1, keepdims=True)
    centred = values - row_mean
    scale = lax.rsqrt(jnp.mean(centred * centred, axis=-1, keepdims=True) + 1e-06)
    return centred * scale, scale


def norm_back(unit, scale, unit_grad):
    return scale * (
        unit_grad
        - jnp.mean(unit_grad, axis=-1, keepdims=True)
        - unit * jnp.mean(unit_grad * unit, axis=-1, keepdims=True)
    )


def column_sum(values):
    return jnp.sum(values, axis=0, keepdims=True)


def params(**extra):
    return pltpu.CompilerParams(vmem_limit_bytes=VMEM_LIMIT, **extra)


def whole(shape):
    return pl.BlockSpec(shape, lambda *_: (0,) * len(shape))


def rows_of(width, tile=TILE):
    return pl.BlockSpec((tile, width), lambda i, *_: (i, 0))


def lanes_of(height, tile=TILE):
    return pl.BlockSpec((height, tile), lambda i, *_: (0, i))


def shape_of(shape, dtype):
    return jax.ShapeDtypeStruct(shape, dtype)


def project_kernel(x_ref, w_ref, g_ref, b_ref, bias_ref, gq_ref, bq_ref, gk_ref,
                   h_ref, qkv_ref, unit_ref, scale_ref):
    unit, _ = normalise(x_ref[...].astype(F32))
    h_low = (unit * g_ref[...] + b_ref[...]).astype(LOW)
    h_ref[...] = h_low
    for part in range(3):
        rows = pl.ds(part * D, D)
        value = mm(w_ref[rows, :], h_low, 1, 1) + bias_ref[rows, :]
        if part == 2:
            qkv_ref[2] = value.astype(LOW)
            continue
        heads = value.reshape(HEADS, HD, value.shape[1])
        centred = heads - jnp.mean(heads, axis=1, keepdims=True)
        scale = lax.rsqrt(jnp.mean(centred * centred, axis=1, keepdims=True) + 1e-06)
        unit_heads = centred * scale
        scale_ref[part] = scale
        unit_ref[part] = unit_heads.reshape(D, -1).astype(LOW)
        if part == 0:
            result = unit_heads * gq_ref[...][None] + bq_ref[...][None]
            result = result.astype(LOW) * LOW(0.125)
        else:
            result = (unit_heads * gk_ref[...][None]).astype(LOW)
        qkv_ref[part] = result.reshape(D, -1)


def project(patches, w_qkv, gain_one, bias_one, bias_qkv, gain_query, bias_query, gain_key):
    slots = patches.shape[0]
    return pl.pallas_call(
        project_kernel,
        grid=(slots // TILE,),
        in_specs=[rows_of(D), whole((3 * D, D)), whole((1, D)), whole((1, D)),
                  whole((3 * D, 1)), whole((HD, 1)), whole((HD, 1)), whole((HD, 1))],
        out_specs=[rows_of(D),
                   pl.BlockSpec((3, D, TILE), lambda i: (0, 0, i)),
                   pl.BlockSpec((2, D, TILE), lambda i: (0, 0, i)),
                   pl.BlockSpec((2, HEADS, 1, TILE), lambda i: (0, 0, 0, i))],
        out_shape=[shape_of((slots, D), LOW), shape_of((3, D, slots), LOW),
                   shape_of((2, D, slots), LOW), shape_of((2, HEADS, 1, slots), F32)],
        compiler_params=params(),
        name="project",
    )(patches, w_qkv, gain_one[None], bias_one[None], bias_qkv[:, None],
      gain_query[:, None], bias_query[:, None], gain_key[:, None])


def used_slots(counts_ref):
    total = counts_ref[0]
    for k in range(1, counts_ref.shape[0]):
        total = total + counts_ref[k]
    return total


def pair_mask(tile_start, used, has_big):
    same = (has_big & (tile_start + SMALL < BIG)) | (tile_start >= used)
    row_half = lax.broadcasted_iota(jnp.int32, (128, 128), 0) // SMALL
    column_half = lax.broadcasted_iota(jnp.int32, (128, 128), 1) // SMALL
    return (row_half == column_half) | same


def soft_columns(scores):
    peak = jnp.max(scores, axis=0, keepdims=True)
    exponent = jnp.exp(scores - peak)
    total = jnp.sum(exponent, axis=0, keepdims=True)
    return exponent.astype(LOW), total, peak + jnp.log(total)


def attend_kernel(group, counts_ref, qkv_ref, out_ref, log_ref):
    used = used_slots(counts_ref)
    has_big = counts_ref[0] == BIG
    slots = out_ref.shape[1]

    def head_rows(index):
        return pl.ds(index * HD, HD)

    for tile in range(slots // 128):
        span = pl.ds(tile * 128, 128)
        mask = pair_mask(tile * 128, used, has_big)
        for index in range(group):
            q = qkv_ref[0, head_rows(index), span]
            k = qkv_ref[1, head_rows(index), span]
            v = qkv_ref[2, head_rows(index), span]
            scores = jnp.where(mask, mm(k, q, 0, 0), MASKED)
            weights, total, log_total = soft_columns(scores)
            out_ref[head_rows(index), span] = (mm(v, weights) / total).astype(LOW)
            log_ref[index, :, span] = log_total

    @pl.when(has_big)
    def _():
        for index in range(group):
            k = qkv_ref[1, head_rows(index), 0:640]
            v = qkv_ref[2, head_rows(index), 0:640]
            for start, width in ((0, 256), (256, 256), (512, 128)):
                span = pl.ds(start, width)
                q = qkv_ref[0, head_rows(index), span]
                scores = mm(k, q, 0, 0)[:BIG]
                weights, total, log_total = soft_columns(scores)
                weights = jnp.concatenate([weights, jnp.zeros((640 - BIG, width), LOW)], axis=0)
                result = mm(v, weights) / total
                if width == 128:
                    lane = lax.broadcasted_iota(jnp.int32, (1, width), 1)
                    inside = lane < BIG - start
                    result = jnp.where(inside, result, out_ref[head_rows(index), span].astype(F32))
                    log_total = jnp.where(inside, log_total, log_ref[index, :, span])
                out_ref[head_rows(index), span] = result.astype(LOW)
                log_ref[index, :, span] = log_total

    for first in range(0, slots - 128, 256):

        @pl.when((used >= first) & (used < first + 256) & (used < slots - 128))
        def _():
            for index in range(group):
                k = qkv_ref[1, head_rows(index), first:slots]
                v = qkv_ref[2, head_rows(index), first:slots]

                def columns(chunk, carry):
                    span = pl.ds(pl.multiple_of(chunk * 256, 256), 256)
                    q = qkv_ref[0, head_rows(index), span]
                    scores = mm(k, q, 0, 0)
                    key_slot = first + lax.broadcasted_iota(jnp.int32, (256, 256), 0)
                    top = jnp.where(key_slot >= used, scores[:256], MASKED)
                    if slots - first > 256:
                        top = jnp.concatenate([top, scores[256:]], axis=0)
                    weights, total, log_total = soft_columns(top)
                    slot = chunk * 256 + lax.broadcasted_iota(jnp.int32, (1, 256), 1)
                    inside = slot >= used
                    result = mm(v, weights) / total
                    old = out_ref[head_rows(index), span].astype(F32)
                    out_ref[head_rows(index), span] = jnp.where(inside, result, old).astype(LOW)
                    log_ref[index, :, span] = jnp.where(inside, log_total, log_ref[index, :, span])
                    return carry

                lax.fori_loop(first // 256, slots // 256, columns, 0)


def attend(counts, qkv, group=2):
    slots = qkv.shape[2]
    return pl.pallas_call(
        functools.partial(attend_kernel, group),
        grid_spec=pltpu.PrefetchScalarGridSpec(
            num_scalar_prefetch=1,
            grid=(HEADS // group,),
            in_specs=[pl.BlockSpec((3, group * HD, slots), lambda h, c: (0, h, 0))],
            out_specs=[pl.BlockSpec((group * HD, slots), lambda h, c: (h, 0)),
                       pl.BlockSpec((group, 1, slots), lambda h, c: (h, 0, 0))],
        ),
        out_shape=[shape_of((D, slots), LOW), shape_of((HEADS, 1, slots), F32)],
        compiler_params=params(),
        name="attend",
    )(counts, qkv)


def attend_back_kernel(group, counts_ref, qkv_ref, attn_ref, log_ref, grad_ref, unit_ref,
                       scale_ref, gq_ref, gk_ref,
                       dqkv_ref, bias_ref, gain_q_ref, bias_q_ref, gain_k_ref, dq_s, dk_s, dv_s):
    used = used_slots(counts_ref)
    has_big = counts_ref[0] == BIG
    slots = attn_ref.shape[1]

    @pl.when(pl.program_id(0) == 0)
    def _():
        gain_q_ref[...] = jnp.zeros_like(gain_q_ref)
        bias_q_ref[...] = jnp.zeros_like(bias_q_ref)
        gain_k_ref[...] = jnp.zeros_like(gain_k_ref)

    def head_rows(index):
        return pl.ds(index * HD, HD)

    def delta_of(index, span):
        return column_sum(
            grad_ref[head_rows(index), span].astype(F32)
            * attn_ref[head_rows(index), span].astype(F32)
        )

    for tile in range(slots // 128):
        span = pl.ds(tile * 128, 128)
        mask = pair_mask(tile * 128, used, has_big)
        for index in range(group):
            rows = head_rows(index)
            q, k, v = (qkv_ref[part, rows, span] for part in range(3))
            grad = grad_ref[rows, span]
            scores = mm(k, q, 0, 0)
            probs = jnp.exp(jnp.where(mask, scores - log_ref[index, :, span], MASKED))
            score_low = (probs * (mm(v, grad, 0, 0) - delta_of(index, span))).astype(LOW)
            dv_s[rows, span] = mm(grad, probs.astype(LOW), 1, 1)
            dk_s[rows, span] = mm(q, score_low, 1, 1)
            dq_s[rows, span] = mm(k, score_low)

    @pl.when(has_big)
    def _():
        for index in range(group):
            rows = head_rows(index)
            wide = pl.ds(0, 640)
            q, k, v = (qkv_ref[part, rows, wide] for part in range(3))
            dk = jnp.zeros((HD, 640), F32)
            dv = jnp.zeros((HD, 640), F32)
            for start, width in ((0, 256), (256, 256), (512, 128)):
                span = pl.ds(start, width)
                q_part = qkv_ref[0, rows, span]
                grad = grad_ref[rows, span]
                scores = mm(k, q_part, 0, 0)[:BIG]
                probs = jnp.exp(scores - log_ref[index, :, span])
                if width == 128:
                    lane = lax.broadcasted_iota(jnp.int32, (1, width), 1)
                    probs = jnp.where(lane < BIG - start, probs, 0.0)
                score_low = (
                    probs * (mm(v, grad, 0, 0)[:BIG] - delta_of(index, span))
                ).astype(LOW)
                blank = jnp.zeros((640 - BIG, width), LOW)
                score_low = jnp.concatenate([score_low, blank], axis=0)
                probs_low = jnp.concatenate([probs.astype(LOW), blank], axis=0)
                dv = dv + mm(grad, probs_low, 1, 1)
                dk = dk + mm(q_part, score_low, 1, 1)
                dq = mm(k, score_low)
                if width == 128:
                    dq = jnp.where(lane < BIG - start, dq, dq_s[rows, span])
                dq_s[rows, span] = dq
            inside = lax.broadcasted_iota(jnp.int32, (1, 640), 1) < BIG
            dk_s[rows, wide] = jnp.where(inside, dk, dk_s[rows, wide])
            dv_s[rows, wide] = jnp.where(inside, dv, dv_s[rows, wide])

    for index in range(group):
        rows = head_rows(index)
        for part, store, gain_ref in ((0, dq_s, gq_ref), (1, dk_s, gk_ref)):
            unit = unit_ref[part, rows, :].astype(F32)
            grad = store[rows, :]
            if part == 0:
                grad = grad * 0.125
                bias_q_ref[...] += jnp.sum(grad, axis=1, keepdims=True)
                gain_q_ref[...] += jnp.sum(grad * unit, axis=1, keepdims=True)
            else:
                gain_k_ref[...] += jnp.sum(grad * unit, axis=1, keepdims=True)
            unit_grad = grad * gain_ref[...]
            result = scale_ref[part, index] * (
                unit_grad
                - jnp.mean(unit_grad, axis=0, keepdims=True)
                - unit * jnp.mean(unit_grad * unit, axis=0, keepdims=True)
            )
            result = result.astype(LOW)
            dqkv_ref[part, rows, :] = result
            bias_ref[part, rows, :] = jnp.sum(result.astype(F32), axis=1, keepdims=True)
        result = dv_s[rows, :].astype(LOW)
        dqkv_ref[2, rows, :] = result
        bias_ref[2, rows, :] = jnp.sum(result.astype(F32), axis=1, keepdims=True)


def attend_back(counts, qkv, attn, log_total, attn_grad, unit, scale, gain_query, gain_key, group=2):
    slots = qkv.shape[2]
    head_block = pl.BlockSpec((group * HD, slots), lambda h, c: (h, 0))
    column = pl.BlockSpec((HD, 1), lambda h, c: (0, 0))
    return pl.pallas_call(
        functools.partial(attend_back_kernel, group),
        grid_spec=pltpu.PrefetchScalarGridSpec(
            num_scalar_prefetch=1,
            grid=(HEADS // group,),
            in_specs=[pl.BlockSpec((3, group * HD, slots), lambda h, c: (0, h, 0)),
                      head_block,
                      pl.BlockSpec((group, 1, slots), lambda h, c: (h, 0, 0)),
                      head_block,
                      pl.BlockSpec((2, group * HD, slots), lambda h, c: (0, h, 0)),
                      pl.BlockSpec((2, group, 1, slots), lambda h, c: (0, h, 0, 0)),
                      column, column],
            out_specs=[pl.BlockSpec((3, group * HD, slots), lambda h, c: (0, h, 0)),
                       pl.BlockSpec((3, group * HD, 1), lambda h, c: (0, h, 0)),
                       column, column, column],
            scratch_shapes=[pltpu.VMEM((group * HD, slots), F32)] * 3,
        ),
        out_shape=[shape_of((3, D, slots), LOW), shape_of((3, D, 1), F32),
                   shape_of((HD, 1), F32), shape_of((HD, 1), F32), shape_of((HD, 1), F32)],
        compiler_params=params(),
        name="attend_back",
    )(counts, qkv, attn, log_total, attn_grad, unit, scale, gain_query[:, None], gain_key[:, None])


def segment_picker(counts_ref, first, width):
    images = counts_ref.shape[0]
    slot = first + lax.broadcasted_iota(jnp.int32, (images, width), 1)
    image = lax.broadcasted_iota(jnp.int32, (images, width), 0)
    start = jnp.int32(0)
    picked = jnp.zeros((images, width), jnp.bool_)
    for k in range(images):
        end = start + counts_ref[k]
        picked = picked | ((image == k) & (slot >= start) & (slot < end))
        start = end
    return picked.astype(F32), start


def image_sizes(counts_ref):
    images = counts_ref.shape[0]
    image = lax.broadcasted_iota(jnp.int32, (images, 1), 0)
    sizes = jnp.zeros((images, 1), F32)
    for k in range(images):
        sizes = jnp.where(image == k, jnp.maximum(counts_ref[k], 1).astype(F32), sizes)
    return sizes


def middle_kernel(counts_ref, x_ref, attn_ref, w_ref, bias_ref, g_ref, b_ref, cot_ref, image_ref,
                  x2_ref, h_ref, dy_ref, mix_ref):
    x2 = x_ref[...].astype(F32) + mm(attn_ref[...], w_ref[...], 0, 1) + bias_ref[...]
    x2_ref[...] = x2
    unit, _ = normalise(x2)
    h_ref[...] = (unit * g_ref[...] + b_ref[...]).astype(LOW)
    tile = x_ref.shape[0]
    first = pl.program_id(0) * tile
    picker, used = segment_picker(counts_ref, first, tile)
    picker = picker.astype(LOW)
    image_grad = image_ref[...].astype(F32) / image_sizes(counts_ref)
    dy = jnp.zeros(x2.shape, F32)
    rest = image_grad
    for _ in range(3):
        high, rest = split_value32(rest)
        dy = dy + mm(picker, high, 0, 0)
    slot = first + lax.broadcasted_iota(jnp.int32, (tile, 1), 0)
    dy = dy + jnp.where(slot < used, cot_ref[...].astype(F32), 0.0)
    dy_ref[...] = dy
    mix_ref[...] = dy.astype(LOW)


def split_value32(value):
    high = value.astype(LOW)
    return high, value - high.astype(F32)


def middle(counts, patches, attn, w_out, bias_out, gain_two, bias_two, patch_cot, image_cot):
    slots = patches.shape[0]
    images = counts.shape[0]
    return pl.pallas_call(
        middle_kernel,
        grid_spec=pltpu.PrefetchScalarGridSpec(
            num_scalar_prefetch=1,
            grid=(slots // TILE,),
            in_specs=[rows_of(D), lanes_of(D), whole((D, D)), whole((1, D)), whole((1, D)),
                      whole((1, D)), rows_of(D), whole((images, D))],
            out_specs=[rows_of(D)] * 4,
        ),
        out_shape=[shape_of((slots, D), F32), shape_of((slots, D), LOW),
                   shape_of((slots, D), F32), shape_of((slots, D), LOW)],
        compiler_params=params(),
        name="middle",
    )(counts, patches, attn, w_out, bias_out[None], gain_two[None], bias_two[None], patch_cot, image_cot)


def feed_kernel(x2_ref, h_ref, mix_ref, up_ref, down_ref, bias_ref, bias_down_ref,
                y_ref, dh_ref, grad_up_ref, grad_down_ref, bias_grad_ref):
    first = pl.program_id(0) == 0

    @pl.when(first)
    def _():
        y_ref[...] = x2_ref[...] + bias_down_ref[...]
        dh_ref[...] = jnp.zeros_like(dh_ref)

    up, down = up_ref[...], down_ref[...]
    slots = h_ref.shape[0]
    grad_up = jnp.zeros(up.shape, F32)
    grad_down = jnp.zeros(up.shape, F32)
    bias_grad = jnp.zeros((1, up.shape[0]), F32)
    for start in range(0, slots, TILE):
        span = pl.ds(start, TILE)
        h, mix = h_ref[span, :], mix_ref[span, :]
        u = mm(h, up, 1, 1) + bias_ref[...]
        gate = 0.5 * (1.0 + lax.erf(u * (0.5**0.5)))
        slope = gate + u * (jnp.exp(-0.5 * u * u) * ((0.5 / math.pi) ** 0.5))
        hidden = (u * gate).astype(LOW)
        pre = (mm(mix, down, 1, 1) * slope).astype(LOW)
        y_ref[span, :] += mm(hidden, down)
        dh_ref[span, :] += mm(pre, up)
        grad_up = grad_up + mm(pre, h, 0, 0)
        grad_down = grad_down + mm(hidden, mix, 0, 0)
        bias_grad = bias_grad + column_sum(pre.astype(F32))
    grad_up_ref[...] = grad_up.astype(LOW)
    grad_down_ref[...] = grad_down.astype(LOW)
    bias_grad_ref[...] = bias_grad


def feed(x2, h2, mix, w_up, w_down, bias_up, bias_down, block=256):
    slots = x2.shape[0]
    units = w_up.shape[0]
    return pl.pallas_call(
        feed_kernel,
        grid=(units // block,),
        in_specs=[whole((slots, D)), whole((slots, D)), whole((slots, D)),
                  rows_of(D, block), rows_of(D, block),
                  pl.BlockSpec((1, block), lambda i: (0, i)), whole((1, D))],
        out_specs=[whole((slots, D)), whole((slots, D)), rows_of(D, block), rows_of(D, block),
                   pl.BlockSpec((1, block), lambda i: (0, i))],
        out_shape=[shape_of((slots, D), F32), shape_of((slots, D), F32),
                   shape_of((units, D), LOW), shape_of((units, D), LOW),
                   shape_of((1, units), F32)],
        compiler_params=params(),
        name="feed",
    )(x2, h2, mix, w_up, w_down, bias_up[None], bias_down[None])


def after_kernel(counts_ref, y_ref, x2_ref, dh_ref, dy_ref, attn_ref, w_ref, g_ref,
                 out_ref, pooled_ref, dx2_ref, dattn_ref, grad_out_ref,
                 gain_ref, bias_ref, out_bias_ref, down_bias_ref, pool_s, grad_s):
    step = pl.program_id(0)

    @pl.when(step == 0)
    def _():
        pool_s[...] = jnp.zeros_like(pool_s)
        grad_s[...] = jnp.zeros_like(grad_s)
        for ref in (gain_ref, bias_ref, out_bias_ref, down_bias_ref):
            ref[...] = jnp.zeros_like(ref)

    y = y_ref[...]
    tile = y.shape[0]
    out_ref[...] = y.astype(LOW)
    picker, _ = segment_picker(counts_ref, step * tile, tile)
    picker = picker.astype(LOW)
    rest = y
    pooled = pool_s[...]
    for _ in range(3):
        high, rest = split_value32(rest)
        pooled = pooled + mm(picker, high)
    pool_s[...] = pooled
    pooled_ref[...] = (pooled / image_sizes(counts_ref)).astype(LOW)
    unit, scale = normalise(x2_ref[...])
    dh = dh_ref[...]
    gain_ref[...] += column_sum(dh * unit)
    bias_ref[...] += column_sum(dh)
    dy = dy_ref[...]
    down_bias_ref[...] += column_sum(dy.astype(LOW).astype(F32))
    dx2 = dy + norm_back(unit, scale, dh * g_ref[...])
    dx2_ref[...] = dx2
    da = dx2.astype(LOW)
    out_bias_ref[...] += column_sum(da.astype(F32))
    dattn_ref[...] = mm(w_ref[...], da, 0, 1).astype(LOW)
    grad = grad_s[...] + mm(da, attn_ref[...], 0, 1)
    grad_s[...] = grad
    grad_out_ref[...] = grad.astype(LOW)


def after(counts, y, x2, dh2, dy, attn, w_out, gain_two):
    slots = y.shape[0]
    images = counts.shape[0]
    line = whole((1, D))
    return pl.pallas_call(
        after_kernel,
        grid_spec=pltpu.PrefetchScalarGridSpec(
            num_scalar_prefetch=1,
            grid=(slots // TILE,),
            in_specs=[rows_of(D), rows_of(D), rows_of(D), rows_of(D), lanes_of(D),
                      whole((D, D)), line],
            out_specs=[rows_of(D), whole((images, D)), rows_of(D), lanes_of(D), whole((D, D)),
                       line, line, line, line],
            scratch_shapes=[pltpu.VMEM((images, D), F32), pltpu.VMEM((D, D), F32)],
        ),
        out_shape=[shape_of((slots, D), LOW), shape_of((images, D), LOW),
                   shape_of((slots, D), F32), shape_of((D, slots), LOW), shape_of((D, D), LOW)]
        + [shape_of((1, D), F32)] * 4,
        compiler_params=params(),
        name="after",
    )(counts, y, x2, dh2, dy, attn, w_out, gain_two[None])


def first_back_kernel(x_ref, dqkv_ref, w_ref, g_ref, dx2_ref, out_ref, gain_ref, bias_ref):
    @pl.when(pl.program_id(0) == 0)
    def _():
        gain_ref[...] = jnp.zeros_like(gain_ref)
        bias_ref[...] = jnp.zeros_like(bias_ref)

    dh = mm(dqkv_ref[...], w_ref[...], 0, 0)
    unit, scale = normalise(x_ref[...].astype(F32))
    gain_ref[...] += column_sum(dh * unit)
    bias_ref[...] += column_sum(dh)
    out_ref[...] = dx2_ref[...] + norm_back(unit, scale, dh * g_ref[...])


def first_back(patches, dqkv, w_qkv, gain_one, dx2):
    slots = patches.shape[0]
    line = whole((1, D))
    return pl.pallas_call(
        first_back_kernel,
        grid=(slots // TILE,),
        in_specs=[rows_of(D), lanes_of(3 * D), whole((3 * D, D)), line, rows_of(D)],
        out_specs=[rows_of(D), line, line],
        out_shape=[shape_of((slots, D), F32), shape_of((1, D), F32), shape_of((1, D), F32)],
        compiler_params=params(),
        name="first_back",
    )(patches, dqkv, w_qkv, gain_one[None], dx2)


def per_device(
    patches,
    counts,
    owners,
    pooled_cot,
    patch_cot,
    master_qkv,
    master_out,
    master_up,
    master_down,
    mom_qkv,
    mom_out,
    mom_up,
    mom_down,
    vectors,
    vec_first,
    vec_second,
):
    dp_count = lax.axis_size("dp")
    ns_count = lax.axis_size("ns")
    slot_count = patches.shape[0]
    image_total = counts.shape[1]
    capacity = pooled_cot.shape[0] // dp_count
    w_qkv, w_out, w_up, w_down = (
        lax.all_gather(master_qkv.astype(jnp.bfloat16), "ns", axis=0, tiled=True),
        lax.all_gather(master_out.astype(jnp.bfloat16), "ns", axis=0, tiled=True),
        lax.all_gather(master_up.astype(jnp.bfloat16), "ns", axis=0, tiled=True),
        lax.all_gather(master_down.astype(jnp.bfloat16), "ns", axis=0, tiled=True),
    )
    (
        gain_one,
        bias_one,
        bias_qkv,
        gain_query,
        bias_query,
        gain_key,
        bias_out,
        gain_two,
        bias_two,
        bias_up,
        bias_down,
    ) = split_vectors(vectors)
    returned = lax.all_to_all(
        pooled_cot.reshape(dp_count, capacity, D), "dp", split_axis=0, concat_axis=0, tiled=True
    ).reshape(dp_count * capacity, D)
    targets = owner_slots(owners[0], capacity)
    routing = (
        jnp.arange(dp_count * capacity, dtype=jnp.int32)[:, None] == targets[None, :]
    ).astype(jnp.bfloat16)
    image_cot = dot32(routing.T, returned).astype(jnp.bfloat16)
    sizes = counts[0]
    first_low, qkv, unit, scale = project(
        patches, w_qkv, gain_one, bias_one, bias_qkv, gain_query, bias_query, gain_key
    )
    attn, log_total = attend(sizes, qkv)
    x2, second_low, row_grad, mixed_low = middle(
        sizes, patches, attn, w_out, bias_out, gain_two, bias_two, patch_cot, image_cot
    )
    y, second_grad, grad_up, grad_down, up_bias_grad = feed(
        x2, second_low, mixed_low, w_up, w_down, bias_up, bias_down
    )
    (
        out_patches,
        pooled,
        middle_grad,
        attn_grad,
        grad_out,
        gain_two_grad,
        bias_two_grad,
        out_bias_grad,
        down_bias_grad,
    ) = after(sizes, y, x2, second_grad, row_grad, attn, w_out, gain_two)
    outgoing = dot32(routing, pooled).astype(jnp.bfloat16).reshape(dp_count, capacity, D)
    arrived = lax.all_to_all(outgoing, "dp", split_axis=0, concat_axis=0, tiled=True)
    pooled_rows = arrived.reshape(dp_count * capacity, D)
    dqkv, qkv_bias_grad, gain_query_grad, bias_query_grad, gain_key_grad = attend_back(
        sizes, qkv, attn, log_total, attn_grad, unit, scale, gain_query, gain_key
    )
    dqkv = dqkv.reshape(3 * D, slot_count)
    grad_qkv = dot32(dqkv, first_low).astype(jnp.bfloat16)
    patch_grad, gain_one_grad, bias_one_grad = first_back(
        patches, dqkv, w_qkv, gain_one, middle_grad
    )
    vector_local = jnp.concatenate(
        [
            piece.reshape(-1)
            for piece in (
                gain_one_grad,
                bias_one_grad,
                qkv_bias_grad,
                gain_query_grad,
                bias_query_grad,
                gain_key_grad,
                out_bias_grad,
                gain_two_grad,
                bias_two_grad,
                up_bias_grad,
                down_bias_grad,
            )
        ]
    )
    gradients = (grad_qkv, grad_out, grad_up, grad_down)
    moments = (mom_qkv, mom_out, mom_up, mom_down)
    masters = (master_qkv, master_out, master_up, master_down)
    grad_parts, moment_parts, new_masters = [None] * 4, [None] * 4, [None] * 4
    for kind_index in (3, 2, 1, 0):
        gradient = gradients[kind_index].astype(jnp.bfloat16)
        length = gradient.shape[0] // ns_count
        total = sum_rows(gradient.reshape(ns_count, length, D)).astype(jnp.float32)
        moment = MUON_DECAY * moments[kind_index] + total
        moment_low = moment.astype(jnp.bfloat16)
        gram_raw = sum_gram(
            jnp.einsum("rd,re->de", moment_low, moment_low, preferred_element_type=jnp.float32)
        )
        ortho = orthogonalise(moment_low, gram_raw)
        step_scale = MUON_RATE * math.sqrt(max(1.0, length * ns_count / D))
        grad_parts[kind_index] = total
        moment_parts[kind_index] = moment
        new_masters[kind_index] = (
            masters[kind_index] * (1.0 - MUON_RATE * MUON_SHRINK) - step_scale * ortho
        )
    vector_size = vector_local.shape[0]
    padded = -(-vector_size // 1024) * 1024
    vector_grad = sum_everywhere(
        jnp.pad(vector_local, (0, padded - vector_size)).reshape(-1, 128)
    ).reshape(-1)[:vector_size]
    vector_first = BETA_ONE * vec_first + (1.0 - BETA_ONE) * vector_grad
    vector_second = BETA_TWO * vec_second + (1.0 - BETA_TWO) * vector_grad * vector_grad
    first_hat = vector_first / (1.0 - BETA_ONE**STEP)
    second_hat = vector_second / (1.0 - BETA_TWO**STEP)
    vector_new = vectors - ADAM_RATE * first_hat / (jnp.sqrt(second_hat) + 1e-08)
    return (
        out_patches,
        pooled_rows,
        patch_grad,
        grad_parts[0],
        grad_parts[1],
        grad_parts[2],
        grad_parts[3],
        moment_parts[0],
        moment_parts[1],
        moment_parts[2],
        moment_parts[3],
        new_masters[0],
        new_masters[1],
        new_masters[2],
        new_masters[3],
        new_masters[0].astype(jnp.bfloat16),
        new_masters[1].astype(jnp.bfloat16),
        new_masters[2].astype(jnp.bfloat16),
        new_masters[3].astype(jnp.bfloat16),
        vector_grad,
        vector_first,
        vector_second,
        vector_new,
    )


def solution(mesh):
    placed = (
        P(("dp", "ns"), None),
        P(("dp", "ns"), None),
        P(("dp", "ns"), None),
        P(("dp", "ns"), None),
        P(("dp", "ns"), None),
        P("ns", None),
        P("ns", None),
        P("ns", None),
        P("ns", None),
        P("ns", None),
        P("ns", None),
        P("ns", None),
        P("ns", None),
        P(),
        P(),
        P(),
    )
    return jax.shard_map(
        per_device,
        mesh=mesh,
        in_specs=placed,
        out_specs=(
            P(("dp", "ns"), None),
            P(("dp", "ns"), None),
            P(("dp", "ns"), None),
            P("ns", None),
            P("ns", None),
            P("ns", None),
            P("ns", None),
            P("ns", None),
            P("ns", None),
            P("ns", None),
            P("ns", None),
            P("ns", None),
            P("ns", None),
            P("ns", None),
            P("ns", None),
            P("ns", None),
            P("ns", None),
            P("ns", None),
            P("ns", None),
            P(),
            P(),
            P(),
            P(),
        ),
        check_vma=False,
    )
```

time: 1690 us -> 667 us (0.39)
  waiting for transfers between devices: 877 us -> 212 us
  matrix products: 424 us -> 136 us
  Pallas kernels: 0 us -> 146 us
  other arithmetic: 167 us -> 52.8 us
  local copies, waits for them, and re-layouts: 130 us -> 26.7 us
  starting transfers between devices: 15.1 us -> 65.1 us
  blocking collectives: 45.5 us -> 0 us
    reduce_scatter x17 -> x0, waiting for transfers between devices: 615 us -> none  [the longest x1 264 us: per_device(): lax.psum_scatter(spread, ('dp', 'ns'), scatter_dimension=0, tiled=True)]
    dot_general x62 -> x83, matrix products: 424 us -> 136 us  [the longest x79 127 us: dot32(): return jnp.dot(first, second, preferred_element_type=jnp.float32)]
    all_gather x17 -> x0, waiting for transfers between devices: 254 us -> none  [the longest x1 65.4 us: per_device(): lax.all_gather(own_piece.astype(jnp.bfloat16), 'dp', axis=0, tiled=True)]
    ppermute x0 -> x45, waiting for transfers between devices: none -> 151 us  [swap(): return lax.ppermute(value, axis, xor_pairs(lax.axis_size(axis), bit))]
    pallas_call x0 -> x7, Pallas kernels: none -> 146 us  [the longest x1 45.6 us: feed(): pl.pallas_call(feed_kernel, grid=(units // block,), in_specs=[whole((slot...]
    reduce_sum x22 -> x4, other arithmetic: 62.6 us -> 2.97 us  [orthogonalise(): scale = 1.0 / (jnp.sqrt(jnp.trace(gram_raw)) + 1e-07)]
    ppermute x0 -> x45, starting transfers between devices: none -> 53.5 us  [swap(): return lax.ppermute(value, axis, xor_pairs(lax.axis_size(axis), bit))]
    psum x2 -> x0, blocking collectives: 45.5 us -> none  [the longest x1 39.9 us: per_device(): vector_grad = lax.psum(vector_local, ('dp', 'ns'))]
  transfers between devices with their start and end apart: 40 -> 51, of which waited for: 32 -> 23; matrix products, arithmetic and copies ran while one was open for 20% -> 23% of each run, Pallas kernels for 0% -> 13%
where the time goes in v1:
time: 667 us; the launch traced here: 657 us
  waiting for transfers between devices  212 us (32%)
  Pallas kernels  146 us (22%)
  matrix products  136 us (20%)
  starting transfers between devices  65.1 us (10%)
  other arithmetic  52.8 us (8%)
  local copies, waits for them, and re-layouts  26.7 us (4%)
  between operations  18.4 us (3%)
    ppermute x45, waiting for transfers between devices, swap(): return lax.ppermute(value, axis, xor_pairs(lax.axis_size(axis), bit))  151 us
    dot_general x79, matrix products, dot32(): return jnp.dot(first, second, preferred_element_type=jnp.float32)  127 us
    ppermute x45, starting transfers between devices, swap(): return lax.ppermute(value, axis, xor_pairs(lax.axis_size(axis), bit))  53.5 us
    pallas_call x1, Pallas kernels, feed(): pl.pallas_call(feed_kernel, grid=(units // block,), in_specs=[whole((slot...  45.6 us
    all_gather x1, waiting for transfers between devices, per_device(): lax.all_gather(master_up.astype(jnp.bfloat16), 'ns', axis=0, tiled=True)  39.5 us
    pallas_call x1, Pallas kernels, attend(): pl.pallas_call(functools.partial(attend_kernel, group), grid_spec=pltpu.P...  29.9 us
    pallas_call x1, Pallas kernels, attend_back(): pl.pallas_call(functools.partial(attend_back_kernel, group), grid_spec=pl...  27.7 us
  transfers between devices with their start and end apart: 51, of which 23 were waited for; matrix products, arithmetic and copies ran while one was open for 23% of the time, Pallas kernels for 13%

profile of v1, /device:TPU:0, one launch (start us, length us, event | category | flops | bytes accessed | tf_op | source)
XLA Modules:
  0.0 656.9 jit_solution(7120627417499294554)
XLA Ops:
  15.5 7.3 %all-to-all-start = ((bf16[8,2,768]{2,1,0:T(2,128)(2,1)}), bf16[8,2,768]{2,1,0:T(2,128)(2,1)S(1)}, u32[]{:S(2)}, u32[]{:S(2)}) async-start(bf16[8,2,768]{2,1,0:T(2,128)(2,1)} %reshape.178), calls=%async_computation | async-start | bytes 49152 | tf_op jit(solution)/shard_map/all_to_all | solution.py:729
  31.6 12.1 %all-gather.5.cloned.1.call-done.w_ref = bf16[2304,768]{1,0:T(8,128)(2,1)} async-done(((bf16[576,768]{1,0:T(8,128)(2,1)}), bf16[2304,768]{1,0:T(8,128)(2,1)}) %all-gather.5.cloned.1.call-update) | async-done | bytes 3538960 | tf_op jit(solution)/shard_map/all_gather | solution.py:711
  43.7 10.7 %project.1 = (bf16[1024,768]{1,0:T(8,128)(2,1)}, bf16[3,768,1024]{2,1,0:T(8,128)(2,1)}, bf16[2,768,1024]{2,1,0:T(8,128)(2,1)}, f32[2,12,1,1024]{3,2,1,0:T(1,128)}) custom-call(bf16[1024,768]{1,0:T(8,128)(2,1)} %x_ref.5, bf16[2304,768]{1,0:T(8,128)(2,1)} %all-gather.5.cloned.1.call-done.w_ref, f32[1,768]{1,0:T(1,128)} %broadcast_in_dim.48.g_ref, ...), custom_call_target="tpu_custom_call" | custom-call | tf_op jit(solution)/shard_map/project/pallas_call | solution.py:233
  54.4 29.9 %attend.1 = (bf16[768,1024]{1,0:T(8,128)(2,1)}, f32[12,1,1024]{2,1,0:T(1,128)}) custom-call(s32[16]{0:T(128)} %bitcast.231, bf16[3,768,1024]{2,1,0:T(8,128)(2,1)} %get-tuple-element.55.qkv_ref), custom_call_target="tpu_custom_call" | custom-call | tf_op jit(solution)/shard_map/attend/pallas_call | solution.py:341
  84.3 9.0 %middle.1 = (f32[1024,768]{1,0:T(8,128)}, bf16[1024,768]{1,0:T(8,128)(2,1)}, f32[1024,768]{1,0:T(8,128)}, bf16[1024,768]{1,0:T(8,128)(2,1)}) custom-call(s32[16]{0:T(128)} %bitcast.232, bf16[1024,768]{1,0:T(8,128)(2,1)} %x_ref.5, bf16[768,1024]{1,0:T(8,128)(2,1)} %get-tuple-element.56.attn_ref, bf16[768,768]{1,0:T(8,128)(2,1)} %all-gather.7.cloned.1.call-done.w_ref, ...), custom_call_target="tpu_custom_call" | custom-call | tf_op jit(solution)/shard_map/middle/pallas_call | solution.py:530
  93.3 9.6 %all-gather.11.cloned.1.call-done.down_ref = bf16[3072,768]{1,0:T(8,128)(2,1)} async-done(((bf16[768,768]{1,0:T(8,128)(2,1)}), bf16[3072,768]{1,0:T(8,128)(2,1)}) %all-gather.11.cloned.1.call-update) | async-done | bytes 4718608 | tf_op jit(solution)/shard_map/all_gather | solution.py:714
  103.0 39.5 %all-gather.9.cloned.1.call-done.up_ref = bf16[3072,768]{1,0:T(8,128)(2,1)} async-done(((bf16[768,768]{1,0:T(8,128)(2,1)}), bf16[3072,768]{1,0:T(8,128)(2,1)}) %all-gather.9.cloned.1.call-update) | async-done | bytes 4718608 | tf_op jit(solution)/shard_map/all_gather | solution.py:713
  142.4 45.6 %feed.1 = (f32[1024,768]{1,0:T(8,128)}, f32[1024,768]{1,0:T(8,128)}, bf16[3072,768]{1,0:T(8,128)(2,1)}, bf16[3072,768]{1,0:T(8,128)(2,1)}, f32[1,3072]{1,0:T(1,128)}) custom-call(f32[1024,768]{1,0:T(8,128)} %get-tuple-element.57.x2_ref, bf16[1024,768]{1,0:T(8,128)(2,1)} %get-tuple-element.58.h_ref, bf16[1024,768]{1,0:T(8,128)(2,1)} %get-tuple-element.59.mix_ref, ...), custom_call_target="tpu_custom_call" | custom-call | tf_op jit(solution)/shard_map/feed/pallas_call | solution.py:581
  188.0 12.2 %after.1 = (bf16[1024,768]{1,0:T(8,128)(2,1)}, bf16[16,768]{1,0:T(8,128)(2,1)}, f32[1024,768]{1,0:T(8,128)}, bf16[768,1024]{1,0:T(8,128)(2,1)}, bf16[768,768]{1,...) custom-call(s32[16]{0:T(128)} %bitcast.233, ...), custom_call_target="tpu_custom_call" | custom-call | tf_op jit(solution)/shard_map/after/pallas_call | solution.py:641
  201.7 27.7 %attend_back.1 = (bf16[3,768,1024]{2,1,0:T(8,128)(2,1)}, f32[3,768,1]{2,1,0:T(8,128)}, f32[64,1]{1,0:T(8,128)}, f32[64,1]{1,0:T(8,128)}, f32[64,1]{1,0:T(8,128)}) custom-call(s32[16]{0:T(128)} %bitcast.234, bf16[3,768,1024]{2,1,0:T(8,128)(2,1)} %get-tuple-element.55.qkv_ref, bf16[768,1024]{1,0:T(8,128)(2,1)} %get-tuple-element.56.attn_ref, ...), custom_call_target="tpu_custom_call" | custom-call | tf_op jit(solution)/shard_map/attend_back/pallas_call | solution.py:454
  229.4 10.5 %first_back.1 = (f32[1024,768]{1,0:T(8,128)}, f32[1,768]{1,0:T(1,128)}, f32[1,768]{1,0:T(1,128)}) custom-call(bf16[1024,768]{1,0:T(8,128)(2,1)} %x_ref.5, bf16[2304,1024]{1,0:T(8,128)(2,1)} %bitcast.207, bf16[2304,768]{1,0:T(8,128)(2,1)} %all-gather.5.cloned.1.call-done.w_ref, f32[1,768]{1,0:T(1,128)} %broadcast_in_dim.48.g_ref, ...), custom_call_target="tpu_custom_call" | custom-call | tf_op jit(solution)/shard_map/first_back/pallas_call | solution.py:676
  246.9 5.4 convolution_convert_fusion
  255.9 14.6 %collective-permute-start.9 = (bf16[96,768]{1,0:T(8,128)(2,1)S(1)}, bf16[96,768]{1,0:T(8,128)(2,1)S(1)}, u32[]{:S(2)}, u32[]{:S(2)}) collective-permute-start(bf16[96,768]{1,0:T(8,128)(2,1)S(1)} %dynamic-slice_bitcast_fusion.14), channel_id=1, source_target_pairs={{0,4},{4,0},{8,12},{12,8},{16,20},{20,16},{24,28},{28,24},{1,5},{5... | collective-permute-start | bytes 442376 | tf_op jit(solution)/shard_map/ppermute | solution.py:53
  285.5 4.1 all-to-all-start.1
  305.4 4.5 collective-permute-done.13
  319.2 15.4 %collective-permute-done.1 = bf16[1,576,768]{2,1,0:T(8,128)(2,1)S(1)} collective-permute-done((bf16[1,576,768]{2,1,0:T(8,128)(2,1)S(1)}, bf16[1,576,768]{2,1,0:T(8,128)(2,1)S(1)}, u32[]{:S(2)}, u32[]{:S(2)}) %collective-permute-start.1) | collective-permute-done | bytes 884768 | tf_op jit(solution)/shard_map/ppermute | solution.py:53
  339.4 4.5 collective-permute-done.2
  346.3 5.1 collective-permute-done.3
  351.5 8.4 %collective-permute-done.15 = bf16[1,768,768]{2,1,0:T(8,128)(2,1)S(1)} collective-permute-done((bf16[1,768,768]{2,1,0:T(8,128)(2,1)S(1)}, bf16[1,768,768]{2,1,0:T(8,128)(2,1)S(1)}, u32[]{:S(2)}, u32[]{:S(2)}) %collective-permute-start.15) | collective-permute-done | bytes 1179680 | tf_op jit(solution)/shard_map/ppermute | solution.py:53
  363.4 20.2 %collective-permute-done.22 = bf16[1,768,768]{2,1,0:T(8,128)(2,1)S(1)} collective-permute-done((bf16[1,768,768]{2,1,0:T(8,128)(2,1)S(1)}, bf16[1,768,768]{2,1,0:T(8,128)(2,1)S(1)}, u32[]{:S(2)}, u32[]{:S(2)}) %collective-permute-start.22) | collective-permute-done | bytes 1179680 | tf_op jit(solution)/shard_map/ppermute | solution.py:53
  388.9 11.4 %collective-permute-done.23 = bf16[384,768]{1,0:T(8,128)(2,1)S(1)} collective-permute-done((bf16[384,768]{1,0:T(8,128)(2,1)S(1)}, bf16[384,768]{1,0:T(8,128)(2,1)S(1)}, u32[]{:S(2)}, u32[]{:S(2)}) %collective-permute-start.23) | collective-permute-done | bytes 589856 | tf_op jit(solution)/shard_map/ppermute | solution.py:53
  402.7 4.5 collective-permute-done.6
  411.2 10.1 %collective-permute-done.18 = bf16[192,768]{1,0:T(8,128)(2,1)S(1)} collective-permute-done((bf16[192,768]{1,0:T(8,128)(2,1)S(1)}, bf16[192,768]{1,0:T(8,128)(2,1)S(1)}, u32[]{:S(2)}, u32[]{:S(2)}) %collective-permute-start.18) | collective-permute-done | bytes 294944 | tf_op jit(solution)/shard_map/ppermute | solution.py:53
  426.0 5.1 collective-permute-done.19
  440.1 6.1 collective-permute-done.20
  446.5 7.3 %collective-permute-done.27 = bf16[384,768]{1,0:T(8,128)(2,1)S(1)} collective-permute-done((bf16[384,768]{1,0:T(8,128)(2,1)S(1)}, bf16[384,768]{1,0:T(8,128)(2,1)S(1)}, u32[]{:S(2)}, u32[]{:S(2)}) %collective-permute-start.27) | collective-permute-done | bytes 589856 | tf_op jit(solution)/shard_map/ppermute | solution.py:53
  485.6 24.4 %collective-permute-done.29 = f32[384,768]{1,0:T(8,128)S(1)} collective-permute-done((f32[384,768]{1,0:T(8,128)S(1)}, f32[384,768]{1,0:T(8,128)S(1)}, u32[]{:S(2)}, u32[]{:S(2)}) %collective-permute-start.29) | collective-permute-done | bytes 1179680 | tf_op jit(solution)/shard_map/ppermute | solution.py:53
  512.8 5.7 fusion.143
  558.4 7.8 %fusion.142 = (bf16[576,768]{1,0:T(8,128)(2,1)}, f32[576,768]{1,0:T(8,128)}) fusion(bf16[576,768]{1,0:T(8,128)(2,1)} %add_convert_fusion.22, f32[768,768]{1,0:T(8,128)} %add_add_fusion.18, f32[576,768]{1,0:T(8,128)} %param.21), kind=kOutput, calls=%fused_computation.321 | convolution fusion | flops 1592082432 | bytes 7667712 | tf_op jit(solution)/shard_map/dot_general | solution.py:123
  566.2 10.1 %collective-permute-done.35 = f32[384,768]{1,0:T(8,128)} collective-permute-done((f32[384,768]{1,0:T(8,128)}, f32[384,768]{1,0:T(8,128)}, u32[]{:S(2)}, u32[]{:S(2)}) %collective-permute-start.35) | collective-permute-done | bytes 1179680 | tf_op jit(solution)/shard_map/ppermute | solution.py:53
  634.3 7.2 %fusion.145 = (bf16[768,768]{1,0:T(8,128)(2,1)}, f32[768,768]{1,0:T(8,128)}) fusion(bf16[768,768]{1,0:T(8,128)(2,1)S(1)} %add_convert_fusion.1, f32[768,768]{1,0:T(8,128)} %add_add_fusion, f32[768,768]{1,0:T(8,128)S(1)} %copy-done.13), kind=kOutput, calls=%fused_computation.324 | convolution fusion | flops 1819607040 | bytes 9437184 | tf_op jit(solution)/shard_map/dot_general | solution.py:123
  641.5 8.6 %fusion.144 = (bf16[768,768]{1,0:T(8,128)(2,1)}, f32[768,768]{1,0:T(8,128)}) fusion(bf16[768,768]{1,0:T(8,128)(2,1)} %add_convert_fusion.7, f32[768,768]{1,0:T(8,128)} %add_add_fusion.6, f32[768,768]{1,0:T(8,128)} %param.23), kind=kOutput, calls=%fused_computation.323 | convolution fusion | flops 1819607040 | bytes 9437184 | tf_op jit(solution)/shard_map/dot_general | solution.py:123
  (381 shorter events, 233.9 us)
Async XLA Ops:
  7.2 36.5 %all-gather.5.cloned.1.call-start = ((), (), s32[]{:S(2)}) async-start(), calls=%async_computation.2 | async-start | bytes 4423680 | tf_op jit(solution)/shard_map/all_gather | solution.py:711
  9.9 74.4 %all-gather.7.cloned.1.call-start = ((), (), s32[]{:S(2)}) async-start(), calls=%async_computation.3 | async-start | bytes 1474560 | tf_op jit(solution)/shard_map/all_gather | solution.py:712
  10.7 92.2 %all-gather.11.cloned.1.call-start = ((), (), s32[]{:S(2)}) async-start(), calls=%async_computation.5 | async-start | bytes 5898240 | tf_op jit(solution)/shard_map/all_gather | solution.py:714
  12.0 130.4 %all-gather.9.cloned.1.call-start = ((), (), s32[]{:S(2)}) async-start(), calls=%async_computation.4 | async-start | bytes 5898240 | tf_op jit(solution)/shard_map/all_gather | solution.py:713
  15.5 15.3 %all-to-all-start = ((bf16[8,2,768]{2,1,0:T(2,128)(2,1)}), bf16[8,2,768]{2,1,0:T(2,128)(2,1)S(1)}, u32[]{:S(2)}, u32[]{:S(2)}) async-start(bf16[8,2,768]{2,1,0:T(2,128)(2,1)} %reshape.178), calls=%async_computation | async-start | bytes 49152 | tf_op jit(solution)/shard_map/all_to_all | solution.py:729
  201.4 44.9 %collective-permute-start.7 = (bf16[2,192,768]{2,1,0:T(8,128)(2,1)S(1)}, bf16[2,192,768]{2,1,0:T(8,128)(2,1)S(1)}, u32[]{:S(2)}, u32[]{:S(2)}) collective-permute-start(bf16[2,192,768]{2,1,0:T(8,128)(2,1)S(1)} %dynamic-slice_bitcast_fusion.9), channel_id=1, source_target_pairs={{0,1},{1,0},{2,3},{3,2},{4,5},{5,4},{6,7},{7,6},{8,9},{9,8},{10,11... | collective-permute-start | bytes 1769480 | tf_op jit(solution)/shard_map/ppermute | solution.py:53
  242.3 28.1 %collective-permute-start.40 = (f32[80,128]{1,0:T(8,128)S(1)}, f32[80,128]{1,0:T(8,128)S(1)}, u32[]{:S(2)}, u32[]{:S(2)}) collective-permute-start(f32[80,128]{1,0:T(8,128)S(1)} %pad_bitcast_fusion), channel_id=1, source_target_pairs={{0,1},{1,0},{2,3},{3,2},{4,5},{5,4},{6,7},{7,6},{8,9},{9,8},{10,11... | collective-permute-start | bytes 122888 | tf_op jit(solution)/shard_map/ppermute | solution.py:53
  246.0 68.0 %collective-permute-start.14 = (bf16[2,768,768]{2,1,0:T(8,128)(2,1)}, bf16[2,768,768]{2,1,0:T(8,128)(2,1)}, u32[]{:S(2)}, u32[]{:S(2)}) collective-permute-start(bf16[2,768,768]{2,1,0:T(8,128)(2,1)} %dynamic-slice_bitcast_fusion.1), channel_id=1, source_target_pairs={{0,1},{1,0},{2,3},{3,2},{4,5},{5,4},{6,7},{7,6},{8,9},{9,8},{10,11... | collective-permute-start | bytes 7077896 | tf_op jit(solution)/shard_map/ppermute | solution.py:53
  253.7 56.3 %collective-permute-start = (bf16[2,576,768]{2,1,0:T(8,128)(2,1)}, bf16[2,576,768]{2,1,0:T(8,128)(2,1)}, u32[]{:S(2)}, u32[]{:S(2)}) collective-permute-start(bf16[2,576,768]{2,1,0:T(8,128)(2,1)} %dynamic-slice_bitcast_fusion.2), channel_id=1, source_target_pairs={{0,1},{1,0},{2,3},{3,2},{4,5},{5,4},{6,7},{7,6},{8,9},{9,8},{10,11... | collective-permute-start | bytes 5308424 | tf_op jit(solution)/shard_map/ppermute | solution.py:53
  255.9 18.7 %collective-permute-start.9 = (bf16[96,768]{1,0:T(8,128)(2,1)S(1)}, bf16[96,768]{1,0:T(8,128)(2,1)S(1)}, u32[]{:S(2)}, u32[]{:S(2)}) collective-permute-start(bf16[96,768]{1,0:T(8,128)(2,1)S(1)} %dynamic-slice_bitcast_fusion.14), channel_id=1, source_target_pairs={{0,4},{4,0},{8,12},{12,8},{16,20},{20,16},{24,28},{28,24},{1,5},{5... | collective-permute-start | bytes 442376 | tf_op jit(solution)/shard_map/ppermute | solution.py:53
  297.9 38.5 %collective-permute-start.21 = (bf16[2,768,768]{2,1,0:T(8,128)(2,1)}, bf16[2,768,768]{2,1,0:T(8,128)(2,1)}, u32[]{:S(2)}, u32[]{:S(2)}) collective-permute-start(bf16[2,768,768]{2,1,0:T(8,128)(2,1)} %dynamic-slice_bitcast_fusion), channel_id=1, source_target_pairs={{0,1},{1,0},{2,3},{3,2},{4,5},{5,4},{6,7},{7,6},{8,9},{9,8},{10,11... | collective-permute-start | bytes 7077896 | tf_op jit(solution)/shard_map/ppermute | solution.py:53
  312.0 22.6 %collective-permute-start.1 = (bf16[1,576,768]{2,1,0:T(8,128)(2,1)S(1)}, bf16[1,576,768]{2,1,0:T(8,128)(2,1)S(1)}, u32[]{:S(2)}, u32[]{:S(2)}) collective-permute-start(bf16[1,576,768]{2,1,0:T(8,128)(2,1)S(1)} %constant_dynamic-slice_fusion.3), channel_id=1, source_target_pairs={{0,2},{1,3},{2,0},{3,1},{4,6},{5,7},{6,4},{7,5},{8,10},{9,11},{10,... | collective-permute-start | bytes 2654216 | tf_op jit(solution)/shard_map/ppermute | solution.py:53
  314.0 72.2 %collective-permute-start.31 = (f32[768,768]{1,0:T(8,128)S(1)}, f32[768,768]{1,0:T(8,128)S(1)}, u32[]{:S(2)}, u32[]{:S(2)}) collective-permute-start(f32[768,768]{1,0:T(8,128)S(1)} %fusion.111), channel_id=1, source_target_pairs={{0,1},{1,0},{2,3},{3,2},{4,5},{5,4},{6,7},{7,6},{8,9},{9,8},{10,11... | collective-permute-start | bytes 7077896 | tf_op jit(solution)/shard_map/ppermute | solution.py:53
  317.6 42.3 %collective-permute-start.15 = (bf16[1,768,768]{2,1,0:T(8,128)(2,1)S(1)}, bf16[1,768,768]{2,1,0:T(8,128)(2,1)S(1)}, u32[]{:S(2)}, u32[]{:S(2)}) collective-permute-start(bf16[1,768,768]{2,1,0:T(8,128)(2,1)S(1)} %constant_dynamic-slice_fusion.1), channel_id=1, source_target_pairs={{0,2},{1,3},{2,0},{3,1},{4,6},{5,7},{6,4},{7,5},{8,10},{9,11},{10,... | collective-permute-start | bytes 3538952 | tf_op jit(solution)/shard_map/ppermute | solution.py:53
  338.8 44.8 %collective-permute-start.22 = (bf16[1,768,768]{2,1,0:T(8,128)(2,1)S(1)}, bf16[1,768,768]{2,1,0:T(8,128)(2,1)S(1)}, u32[]{:S(2)}, u32[]{:S(2)}) collective-permute-start(bf16[1,768,768]{2,1,0:T(8,128)(2,1)S(1)} %constant_dynamic-slice_fusion), channel_id=1, source_target_pairs={{0,2},{1,3},{2,0},{3,1},{4,6},{5,7},{6,4},{7,5},{8,10},{9,11},{10,... | collective-permute-start | bytes 3538952 | tf_op jit(solution)/shard_map/ppermute | solution.py:53
  360.3 26.9 %collective-permute-start.16 = (bf16[384,768]{1,0:T(8,128)(2,1)S(1)}, bf16[384,768]{1,0:T(8,128)(2,1)S(1)}, u32[]{:S(2)}, u32[]{:S(2)}) collective-permute-start(bf16[384,768]{1,0:T(8,128)(2,1)S(1)} %dynamic-slice_bitcast_fusion.8), channel_id=1, source_target_pairs={{0,4},{4,0},{8,12},{12,8},{16,20},{20,16},{24,28},{28,24},{1,5},{5... | collective-permute-start | bytes 1769480 | tf_op jit(solution)/shard_map/ppermute | solution.py:53
  361.9 23.6 %collective-permute-start.5 = (bf16[144,768]{1,0:T(8,128)(2,1)S(1)}, bf16[144,768]{1,0:T(8,128)(2,1)S(1)}, u32[]{:S(2)}, u32[]{:S(2)}) collective-permute-start(bf16[144,768]{1,0:T(8,128)(2,1)S(1)} %add_convert_fusion.28), channel_id=1, source_target_pairs={{0,8},{4,12},{8,0},{12,4},{16,24},{20,28},{24,16},{28,20},{1,9},{5... | collective-permute-start | bytes 663560 | tf_op jit(solution)/shard_map/ppermute | solution.py:53
  383.9 16.3 %collective-permute-start.23 = (bf16[384,768]{1,0:T(8,128)(2,1)S(1)}, bf16[384,768]{1,0:T(8,128)(2,1)S(1)}, u32[]{:S(2)}, u32[]{:S(2)}) collective-permute-start(bf16[384,768]{1,0:T(8,128)(2,1)S(1)} %dynamic-slice_bitcast_fusion.7), channel_id=1, source_target_pairs={{0,4},{4,0},{8,12},{12,8},{16,20},{20,16},{24,28},{28,24},{1,5},{5... | collective-permute-start | bytes 1769480 | tf_op jit(solution)/shard_map/ppermute | solution.py:53
  385.5 21.6 %collective-permute-start.6 = (bf16[288,768]{1,0:T(8,128)(2,1)S(1)}, bf16[288,768]{1,0:T(8,128)(2,1)S(1)}, u32[]{:S(2)}, u32[]{:S(2)}) collective-permute-start(bf16[288,768]{1,0:T(8,128)(2,1)S(1)} %pad_maximum_fusion.6), channel_id=1, source_target_pairs={{0,4},{4,0},{8,12},{12,8},{16,20},{20,16},{24,28},{28,24},{1,5},{5... | collective-permute-start | bytes 1327112 | tf_op jit(solution)/shard_map/ppermute | solution.py:53
  386.6 52.8 %collective-permute-start.32 = (f32[384,768]{1,0:T(8,128)S(1)}, f32[384,768]{1,0:T(8,128)S(1)}, u32[]{:S(2)}, u32[]{:S(2)}) collective-permute-start(f32[384,768]{1,0:T(8,128)S(1)} %dynamic-slice_bitcast_fusion.5), channel_id=1, source_target_pairs={{0,2},{1,3},{2,0},{3,1},{4,6},{5,7},{6,4},{7,5},{8,10},{9,11},{10,... | collective-permute-start | bytes 3538952 | tf_op jit(solution)/shard_map/ppermute | solution.py:53
  402.1 19.3 %collective-permute-start.18 = (bf16[192,768]{1,0:T(8,128)(2,1)S(1)}, bf16[192,768]{1,0:T(8,128)(2,1)S(1)}, u32[]{:S(2)}, u32[]{:S(2)}) collective-permute-start(bf16[192,768]{1,0:T(8,128)(2,1)S(1)} %fusion.90), channel_id=1, source_target_pairs={{0,16},{4,20},{8,24},{12,28},{16,0},{20,4},{24,8},{28,12},{1,17},{... | collective-permute-start | bytes 884744 | tf_op jit(solution)/shard_map/ppermute | solution.py:53
  431.2 15.1 %collective-permute-start.20 = (bf16[384,768]{1,0:T(8,128)(2,1)S(1)}, bf16[384,768]{1,0:T(8,128)(2,1)S(1)}, u32[]{:S(2)}, u32[]{:S(2)}) collective-permute-start(bf16[384,768]{1,0:T(8,128)(2,1)S(1)} %pad_maximum_fusion.4), channel_id=1, source_target_pairs={{0,4},{4,0},{8,12},{12,8},{16,20},{20,16},{24,28},{28,24},{1,5},{5... | collective-permute-start | bytes 1769480 | tf_op jit(solution)/shard_map/ppermute | solution.py:53
  435.4 18.4 %collective-permute-start.27 = (bf16[384,768]{1,0:T(8,128)(2,1)S(1)}, bf16[384,768]{1,0:T(8,128)(2,1)S(1)}, u32[]{:S(2)}, u32[]{:S(2)}) collective-permute-start(bf16[384,768]{1,0:T(8,128)(2,1)S(1)} %pad_maximum_fusion.5), channel_id=1, source_target_pairs={{0,4},{4,0},{8,12},{12,8},{16,20},{20,16},{24,28},{28,24},{1,5},{5... | collective-permute-start | bytes 1769480 | tf_op jit(solution)/shard_map/ppermute | solution.py:53
  439.4 39.5 %collective-permute-start.28 = (f32[768,768]{1,0:T(8,128)}, f32[768,768]{1,0:T(8,128)}, u32[]{:S(2)}, u32[]{:S(2)}) collective-permute-start(f32[768,768]{1,0:T(8,128)} %fusion.106), channel_id=1, source_target_pairs={{0,1},{1,0},{2,3},{3,2},{4,5},{5,4},{6,7},{7,6},{8,9},{9,8},{10,11... | collective-permute-start | bytes 7077896 | tf_op jit(solution)/shard_map/ppermute | solution.py:53
  439.6 23.7 %collective-permute-start.33 = (f32[384,768]{1,0:T(8,128)S(1)}, f32[384,768]{1,0:T(8,128)S(1)}, u32[]{:S(2)}, u32[]{:S(2)}) collective-permute-start(f32[384,768]{1,0:T(8,128)S(1)} %fusion.225), channel_id=1, source_target_pairs={{0,1},{1,0},{2,3},{3,2},{4,5},{5,4},{6,7},{7,6},{8,9},{9,8},{10,11... | collective-permute-start | bytes 3538952 | tf_op jit(solution)/shard_map/ppermute | solution.py:53
  460.0 58.5 %collective-permute-start.37 = (f32[768,768]{1,0:T(8,128)}, f32[768,768]{1,0:T(8,128)}, u32[]{:S(2)}, u32[]{:S(2)}) collective-permute-start(f32[768,768]{1,0:T(8,128)} %fusion.91), channel_id=1, source_target_pairs={{0,1},{1,0},{2,3},{3,2},{4,5},{5,4},{6,7},{7,6},{8,9},{9,8},{10,11... | collective-permute-start | bytes 7077896 | tf_op jit(solution)/shard_map/ppermute | solution.py:53
  462.8 60.1 %collective-permute-start.34 = (f32[768,768]{1,0:T(8,128)}, f32[768,768]{1,0:T(8,128)}, u32[]{:S(2)}, u32[]{:S(2)}) collective-permute-start(f32[768,768]{1,0:T(8,128)} %fusion.94), channel_id=1, source_target_pairs={{0,1},{1,0},{2,3},{3,2},{4,5},{5,4},{6,7},{7,6},{8,9},{9,8},{10,11... | collective-permute-start | bytes 7077896 | tf_op jit(solution)/shard_map/ppermute | solution.py:53
  482.0 27.9 %collective-permute-start.29 = (f32[384,768]{1,0:T(8,128)S(1)}, f32[384,768]{1,0:T(8,128)S(1)}, u32[]{:S(2)}, u32[]{:S(2)}) collective-permute-start(f32[384,768]{1,0:T(8,128)S(1)} %dynamic-slice_bitcast_fusion.6), channel_id=1, source_target_pairs={{0,2},{1,3},{2,0},{3,1},{4,6},{5,7},{6,4},{7,5},{8,10},{9,11},{10,... | collective-permute-start | bytes 3538952 | tf_op jit(solution)/shard_map/ppermute | solution.py:53
  510.1 18.1 %collective-permute-start.30 = (f32[384,768]{1,0:T(8,128)S(1)}, f32[384,768]{1,0:T(8,128)}, u32[]{:S(2)}, u32[]{:S(2)}) collective-permute-start(f32[384,768]{1,0:T(8,128)S(1)} %fusion.226), channel_id=1, source_target_pairs={{0,1},{1,0},{2,3},{3,2},{4,5},{5,4},{6,7},{7,6},{8,9},{9,8},{10,11... | collective-permute-start | bytes 3538952 | tf_op jit(solution)/shard_map/ppermute | solution.py:53
  522.4 31.8 %collective-permute-start.38 = (f32[384,768]{1,0:T(8,128)}, f32[384,768]{1,0:T(8,128)}, u32[]{:S(2)}, u32[]{:S(2)}) collective-permute-start(f32[384,768]{1,0:T(8,128)} %dynamic-slice_bitcast_fusion.3), channel_id=1, source_target_pairs={{0,2},{1,3},{2,0},{3,1},{4,6},{5,7},{6,4},{7,5},{8,10},{9,11},{10,... | collective-permute-start | bytes 3538952 | tf_op jit(solution)/shard_map/ppermute | solution.py:53
  526.7 49.7 %collective-permute-start.35 = (f32[384,768]{1,0:T(8,128)}, f32[384,768]{1,0:T(8,128)}, u32[]{:S(2)}, u32[]{:S(2)}) collective-permute-start(f32[384,768]{1,0:T(8,128)} %dynamic-slice_bitcast_fusion.4), channel_id=1, source_target_pairs={{0,2},{1,3},{2,0},{3,1},{4,6},{5,7},{6,4},{7,5},{8,10},{9,11},{10,... | collective-permute-start | bytes 3538952 | tf_op jit(solution)/shard_map/ppermute | solution.py:53
  555.6 23.1 %collective-permute-start.39 = (f32[384,768]{1,0:T(8,128)S(1)}, f32[384,768]{1,0:T(8,128)}, u32[]{:S(2)}, u32[]{:S(2)}) collective-permute-start(f32[384,768]{1,0:T(8,128)S(1)} %fusion.223), channel_id=1, source_target_pairs={{0,1},{1,0},{2,3},{3,2},{4,5},{5,4},{6,7},{7,6},{8,9},{9,8},{10,11... | collective-permute-start | bytes 3538952 | tf_op jit(solution)/shard_map/ppermute | solution.py:53
  (70 other events, 738.9 us)
Sparse Core Ops, SparseCore 0:
  10.2 33.4 all-gather.4
  45.8 17.4 all-gather.6
  65.5 37.4 all-gather.10
  104.9 37.4 all-gather.8

commit v2 on v1

v2 whole, which is shorter than its diff:
```python
import functools
import math

import jax
import jax.numpy as jnp
from jax import lax
from jax.experimental import pallas as pl
from jax.experimental.pallas import tpu as pltpu
from jax.sharding import PartitionSpec as P

D = 768
HD = 64
FF = 3072
ITERS = 4
STEP = 10


NS_A = 3.4445
NS_B = -4.775
NS_C = 2.0315
MUON_RATE = 0.8
MUON_DECAY = 0.5
MUON_SHRINK = 0.01
ADAM_RATE = 0.5
BETA_ONE = 0.9
BETA_TWO = 0.95
MASKED = -1e30


def owner_slots(owners_row, capacity):
    image_total = owners_row.shape[0]
    ordering = jnp.arange(image_total, dtype=jnp.int32)
    earlier = (owners_row[None, :] == owners_row[:, None]) & (ordering[None, :] < ordering[:, None])
    same_before = jnp.sum(earlier.astype(jnp.int32), axis=1)
    return owners_row * capacity + same_before


def swap(value, axis, bit):
    count = lax.axis_size(axis)
    return lax.ppermute(value, axis, [(index, index ^ (1 << bit)) for index in range(count)])


def bit_of(axis, bit):
    return (lax.axis_index(axis) >> bit) & 1


def bits_in(axis):
    return (lax.axis_size(axis) - 1).bit_length()


def tie(values, earlier):
    return lax.optimization_barrier((values, earlier))


def add_low(first, second):
    return (first.astype(jnp.float32) + second.astype(jnp.float32)).astype(jnp.bfloat16)


def halves(value, axis, bit, dim=0):
    mine = bit_of(axis, bit)
    shape = value.shape
    pairs = value.reshape(*shape[:dim], 2, shape[dim] // 2, *shape[dim + 1 :])
    keep = lax.dynamic_index_in_dim(pairs, mine, dim, keepdims=False)
    send = lax.dynamic_index_in_dim(pairs, 1 - mine, dim, keepdims=False)
    return keep, send


def joined(value, other, axis, bit, dim=0):
    mine = bit_of(axis, bit)
    low_half = jnp.where(mine == 0, value, other)
    high_half = jnp.where(mine == 0, other, value)
    return jnp.concatenate([low_half, high_half], axis=dim)


class Chain:
    def __init__(self, steps):
        self.steps = steps
        self.result = None
        self.pending = next(steps)

    def advance(self, came):
        try:
            self.pending = self.steps.send(came)
        except StopIteration as stop:
            self.pending = None
            self.result = stop.value


def meet(*chains, also=()):
    live = [chain for chain in chains if chain.pending is not None]
    cames, also = lax.optimization_barrier((tuple(chain.pending for chain in live), also))
    for chain, came in zip(live, cames):
        chain.advance(came)
    return also


def finish(*chains):
    while any(chain.pending is not None for chain in chains):
        meet(*chains)


def rest_of_dp(value, dim, split):
    first = 1
    split = split and bits_in("dp") > 2
    if split:
        keep, send = halves(value, "dp", 1, dim)
        value = add_low(keep, (yield swap(send, "dp", 1)))
        first = 2
    for bit in range(first, bits_in("dp")):
        value = add_low(value, (yield swap(value, "dp", bit)))
    if split:
        value = joined(value, (yield swap(value, "dp", 1)), "dp", 1, dim)
    other = yield swap(value, "dp", 0)
    return value, other


def sum_up(kept, sent):
    value = add_low(kept, (yield swap(sent, "ns", 1)))
    keep, send = halves(value, "dp", 0)
    return add_low(keep, (yield swap(send, "dp", 0)))


def sum_down(kept, sent):
    keep, send = halves(jnp.stack([kept, sent]), "dp", 0, 1)
    value = add_low(keep, (yield swap(send, "dp", 0)))
    return add_low(value[0], (yield swap(value[1], "ns", 1)))


def sum_blocks(value, split):
    for bit in range(bits_in("ns")):
        mine = bit_of("ns", bit)
        pairs = value.reshape(value.shape[0] // 2, 2, *value.shape[1:])
        keep = lax.dynamic_index_in_dim(pairs, mine, 1, keepdims=False)
        send = lax.dynamic_index_in_dim(pairs, 1 - mine, 1, keepdims=False)
        value = add_low(keep, (yield swap(send, "ns", bit)))
    keep, send = halves(value[0], "dp", 0)
    value = add_low(keep, (yield swap(send, "dp", 0)))
    return (yield from rest_of_dp(value, 0, split))


def sum_vector(value):
    for axis in ("ns", "dp"):
        count = lax.axis_size(axis)
        for bit in range(0, bits_in(axis), 2):
            masks = [1 << bit]
            if bit + 1 < bits_in(axis):
                masks += [2 << bit, 3 << bit]
            came = yield tuple(
                lax.ppermute(value, axis, [(index, index ^ mask) for index in range(count)])
                for mask in masks
            )
            value = value + came[0]
            if len(came) == 3:
                value = value + (came[1] + came[2])
    return value


def sum_gram(gram):
    gram = gram + (yield swap(gram, "ns", 0))
    keep, _ = halves(gram, "ns", 0)
    for bit in range(1, bits_in("ns")):
        keep = keep + (yield swap(keep, "ns", bit))
    other = yield swap(keep, "ns", 0)
    return (keep[None], 0), (other[None], 0)


def by_distance(table):
    place = lax.axis_index("ns")
    return [
        lax.dynamic_index_in_dim(table, place ^ distance, 0, keepdims=True)
        for distance in range(table.shape[0])
    ]


def dot32(first, second):
    return jnp.dot(first, second, preferred_element_type=jnp.float32)


LOW = jnp.bfloat16
F32 = jnp.float32
HEADS = D // HD
BIG = 576
SMALL = 64
TILE = 256
MIB = 1024 * 1024
COST_SCALE = 1e9


def mm(first, second, first_dim=1, second_dim=0):
    return lax.dot_general(
        first,
        second,
        (((first_dim,), (second_dim,)), ((), ())),
        preferred_element_type=F32,
    )


def split_value(value):
    high = value.astype(LOW)
    return high, (value - high.astype(F32)).astype(LOW)


def normalise(values):
    row_mean = jnp.mean(values, axis=-1, keepdims=True)
    centred = values - row_mean
    scale = lax.rsqrt(jnp.mean(centred * centred, axis=-1, keepdims=True) + 1e-06)
    return centred * scale, scale


def norm_back(unit, scale, unit_grad):
    return scale * (
        unit_grad
        - jnp.mean(unit_grad, axis=-1, keepdims=True)
        - unit * jnp.mean(unit_grad * unit, axis=-1, keepdims=True)
    )


def column_sum(values):
    return jnp.sum(values, axis=0, keepdims=True)


def params(mebibytes):
    return pltpu.CompilerParams(vmem_limit_bytes=mebibytes * MIB)


def cost(micros, nbytes):
    return pl.CostEstimate(flops=int(micros * COST_SCALE), bytes_accessed=int(nbytes * COST_SCALE * 1e-9), transcendentals=0)


def whole(shape):
    return pl.BlockSpec(shape, lambda *_: (0,) * len(shape))


def once(shape):
    return pl.BlockSpec(shape, lambda *_: (0,) * len(shape), pipeline_mode=pl.Buffered(1))


def rows_of(width, tile=TILE):
    return pl.BlockSpec((tile, width), lambda i, *_: (i, 0))


def lanes_of(height, tile=TILE):
    return pl.BlockSpec((height, tile), lambda i, *_: (0, i))


STARTS = {}
WIDTHS = dict(gain_one=D, bias_one=D, bias_qkv=3 * D, gain_query=HD, bias_query=HD, gain_key=HD,
              bias_out=D, gain_two=D, bias_two=D, bias_up=FF, bias_down=D)
for part_name, part_width in WIDTHS.items():
    STARTS[part_name] = sum(WIDTHS[other] for other in STARTS)


def vector_row(ref, name):
    start = STARTS[name]
    return ref[:, start : start + WIDTHS[name]]


def to_column(row):
    return jnp.broadcast_to(row, (8, row.shape[1])).T[:, :1]


def to_row(column):
    return jnp.broadcast_to(column, (column.shape[0], 128)).T[:1]


def qkv_part(block):
    return pl.BlockSpec(
        (block.shape[0] - out_rows(block), D), lambda *_: (0, 0), pipeline_mode=pl.Buffered(1)
    )


def out_part(block):
    return pl.BlockSpec((out_rows(block), D), lambda *_: (3, 0), pipeline_mode=pl.Buffered(1))


def out_rows(block):
    return block.shape[0] // 4


def place_blocks(place_ref, refs, store):
    rows = refs[0].shape[0]
    for distance, ref in enumerate(refs):
        start = pl.multiple_of((place_ref[0] ^ distance) * rows, rows)
        store[pl.ds(start, rows), :] = ref[...]


def shape_of(shape, dtype):
    return jax.ShapeDtypeStruct(shape, dtype)


def project_kernel(place_ref, x_ref, w0, w1, w2, w3, vec_ref,
                   h_ref, qkv_ref, unit_ref, scale_ref, w_s, col_s):
    @pl.when(pl.program_id(0) == 0)
    def _():
        place_blocks(place_ref, (w0, w1, w2, w3), w_s)
        start = STARTS["bias_qkv"]
        row = vec_ref[:, start : start + 3 * D + 256]
        col_s[...] = to_column(row)

    unit, _ = normalise(x_ref[...].astype(F32))
    h_low = (unit * vector_row(vec_ref, "gain_one") + vector_row(vec_ref, "bias_one")).astype(LOW)
    h_ref[...] = h_low
    gain_q = col_s[pl.ds(3 * D, HD), :]
    bias_q = col_s[pl.ds(3 * D + HD, HD), :]
    gain_k = col_s[pl.ds(3 * D + 2 * HD, HD), :]
    for part in range(3):
        rows = pl.ds(part * D, D)
        value = mm(w_s[rows, :], h_low, 1, 1) + col_s[rows, :]
        if part == 2:
            qkv_ref[2] = value.astype(LOW)
            continue
        heads = value.reshape(HEADS, HD, value.shape[1])
        centred = heads - jnp.mean(heads, axis=1, keepdims=True)
        scale = lax.rsqrt(jnp.mean(centred * centred, axis=1, keepdims=True) + 1e-06)
        unit_heads = centred * scale
        scale_ref[part] = scale
        unit_ref[part] = unit_heads.reshape(D, -1).astype(LOW)
        if part == 0:
            result = unit_heads * gain_q[None] + bias_q[None]
            result = result.astype(LOW) * LOW(0.125)
        else:
            result = (unit_heads * gain_k[None]).astype(LOW)
        qkv_ref[part] = result.reshape(D, -1)


def project(place, patches, w_blocks, vectors):
    slots = patches.shape[0]
    return pl.pallas_call(
        project_kernel,
        grid_spec=pltpu.PrefetchScalarGridSpec(
            num_scalar_prefetch=1,
            grid=(slots // TILE,),
            in_specs=[rows_of(D)] + [qkv_part(w_blocks[0])] * 4 + [once(vectors.shape)],
            out_specs=[rows_of(D),
                       pl.BlockSpec((3, D, TILE), lambda i, p: (0, 0, i)),
                       pl.BlockSpec((2, D, TILE), lambda i, p: (0, 0, i)),
                       pl.BlockSpec((2, HEADS, 1, TILE), lambda i, p: (0, 0, 0, i))],
            scratch_shapes=[pltpu.VMEM((3 * D, D), LOW), pltpu.VMEM((3 * D + 256, 1), F32)],
        ),
        out_shape=[shape_of((slots, D), LOW), shape_of((3, D, slots), LOW),
                   shape_of((2, D, slots), LOW), shape_of((2, HEADS, 1, slots), F32)],
        compiler_params=params(24),
        cost_estimate=cost(10, 16e6),
        name="project",
    )(place, patches, *w_blocks, vectors)


def used_slots(counts_ref):
    total = counts_ref[0]
    for k in range(1, counts_ref.shape[0]):
        total = total + counts_ref[k]
    return total


def pair_mask(tile_start, used, has_big):
    same = (has_big & (tile_start + SMALL < BIG)) | (tile_start >= used)
    row_half = lax.broadcasted_iota(jnp.int32, (128, 128), 0) // SMALL
    column_half = lax.broadcasted_iota(jnp.int32, (128, 128), 1) // SMALL
    return (row_half == column_half) | same


def soft_columns(scores):
    peak = jnp.max(scores, axis=0, keepdims=True)
    exponent = jnp.exp(scores - peak)
    total = jnp.sum(exponent, axis=0, keepdims=True)
    return exponent.astype(LOW), total, peak + jnp.log(total)


def pair_mask_row(slots, used, has_big):
    row_half = lax.broadcasted_iota(jnp.int32, (128, slots), 0) // SMALL
    slot = lax.broadcasted_iota(jnp.int32, (128, slots), 1)
    column_half = slot // SMALL % 2
    start = slot // 128 * 128
    same = (has_big & (start + SMALL < BIG)) | (start >= used)
    return (row_half == column_half) | same


def attend_kernel(group, counts_ref, qkv_ref, out_ref, log_ref):
    used = used_slots(counts_ref)
    has_big = counts_ref[0] == BIG
    slots = out_ref.shape[1]
    heads = [pl.ds(index * HD, HD) for index in range(group)]

    def narrow(first, last):
        tiles = [slice(start, start + 128) for start in range(first, last, 128)]
        mask = pair_mask_row(slots, used, has_big)[:, first:last]
        span = slice(first, last)
        all_scores = []
        for rows in heads:
            all_scores.append(jnp.concatenate(
                [mm(qkv_ref[1, rows, tile], qkv_ref[0, rows, tile], 0, 0) for tile in tiles], axis=1
            ))
        for index, rows in enumerate(heads):
            scores = jnp.where(mask, all_scores[index], MASKED)
            weights, total, log_total = soft_columns(scores)
            result = jnp.concatenate(
                [mm(qkv_ref[2, rows, tile], weights[:, tile.start - first : tile.stop - first])
                 for tile in tiles], axis=1
            )
            out_ref[rows, span] = (result / total).astype(LOW)
            log_ref[index, :, span] = log_total

    @pl.when(jnp.logical_not(has_big))
    def _():
        narrow(0, 512)

    narrow(512, slots)

    @pl.when(has_big)
    def _():
        for start, width in ((0, 256), (256, 256), (512, 128)):
            span = pl.ds(start, width)
            all_scores = [
                mm(qkv_ref[1, rows, 0:640], qkv_ref[0, rows, span], 0, 0)[:BIG] for rows in heads
            ]
            for index, rows in enumerate(heads):
                weights, total, log_total = soft_columns(all_scores[index])
                weights = jnp.concatenate([weights, jnp.zeros((640 - BIG, width), LOW)], axis=0)
                result = mm(qkv_ref[2, rows, 0:640], weights) / total
                if width == 128:
                    lane = lax.broadcasted_iota(jnp.int32, (1, width), 1)
                    inside = lane < BIG - start
                    result = jnp.where(inside, result, out_ref[rows, span].astype(F32))
                    log_total = jnp.where(inside, log_total, log_ref[index, :, span])
                out_ref[rows, span] = result.astype(LOW)
                log_ref[index, :, span] = log_total

    for first in range(0, slots - 128, 256):

        @pl.when((used >= first) & (used < first + 256) & (used < slots - 128))
        def _():
            def columns(chunk, carry):
                span = pl.ds(pl.multiple_of(chunk * 256, 256), 256)
                slot = chunk * 256 + lax.broadcasted_iota(jnp.int32, (1, 256), 1)
                inside = slot >= used
                key_slot = first + lax.broadcasted_iota(jnp.int32, (256, 256), 0)
                all_scores = [
                    mm(qkv_ref[1, rows, first:slots], qkv_ref[0, rows, span], 0, 0)
                    for rows in heads
                ]
                for index, rows in enumerate(heads):
                    scores = all_scores[index]
                    top = jnp.where(key_slot >= used, scores[:256], MASKED)
                    if slots - first > 256:
                        top = jnp.concatenate([top, scores[256:]], axis=0)
                    weights, total, log_total = soft_columns(top)
                    result = mm(qkv_ref[2, rows, first:slots], weights) / total
                    old = out_ref[rows, span].astype(F32)
                    out_ref[rows, span] = jnp.where(inside, result, old).astype(LOW)
                    log_ref[index, :, span] = jnp.where(inside, log_total, log_ref[index, :, span])
                return carry

            lax.fori_loop(first // 256, slots // 256, columns, 0)


def attend(counts, qkv, group=2):
    slots = qkv.shape[2]
    return pl.pallas_call(
        functools.partial(attend_kernel, group),
        grid_spec=pltpu.PrefetchScalarGridSpec(
            num_scalar_prefetch=1,
            grid=(HEADS // group,),
            in_specs=[pl.BlockSpec((3, group * HD, slots), lambda h, c: (0, h, 0))],
            out_specs=[pl.BlockSpec((group * HD, slots), lambda h, c: (h, 0)),
                       pl.BlockSpec((group, 1, slots), lambda h, c: (h, 0, 0))],
        ),
        out_shape=[shape_of((D, slots), LOW), shape_of((HEADS, 1, slots), F32)],
        compiler_params=params(16),
        cost_estimate=cost(28, 7000000.0),
        name="attend",
    )(counts, qkv)


def attend_back_kernel(group, counts_ref, qkv_ref, attn_ref, log_ref, grad_ref, unit_ref,
                       scale_ref, vec_ref, _, dqkv_ref, bias_ref, gains_ref, dq_s, dk_s, dv_s):
    used = used_slots(counts_ref)
    has_big = counts_ref[0] == BIG
    slots = attn_ref.shape[1]
    start = STARTS["gain_query"]
    columns = to_column(vec_ref[:, start : start + 256])
    gain_q, gain_k = columns[:HD], columns[2 * HD : 3 * HD]

    @pl.when(pl.program_id(0) == 0)
    def _():
        gains_ref[...] = jnp.zeros_like(gains_ref)

    def head_rows(index):
        return pl.ds(index * HD, HD)

    def delta_of(index, span):
        return column_sum(
            grad_ref[head_rows(index), span].astype(F32)
            * attn_ref[head_rows(index), span].astype(F32)
        )

    def narrow(first, last):
        tiles = [slice(start, start + 128) for start in range(first, last, 128)]
        mask = pair_mask_row(slots, used, has_big)[:, first:last]
        span = slice(first, last)

        def wide(product):
            return jnp.concatenate([product(tile) for tile in tiles], axis=1)

        def inner(tile):
            return slice(tile.start - first, tile.stop - first)

        all_scores, all_grads = [], []
        for index in range(group):
            rows = head_rows(index)
            all_scores.append(wide(
                lambda tile: mm(qkv_ref[1, rows, tile], qkv_ref[0, rows, tile], 0, 0)))
            all_grads.append(wide(
                lambda tile: mm(qkv_ref[2, rows, tile], grad_ref[rows, tile], 0, 0)))
        for index in range(group):
            rows = head_rows(index)
            scores = all_scores[index] - log_ref[index, :, span]
            probs = jnp.exp(jnp.where(mask, scores, MASKED))
            score_low = (probs * (all_grads[index] - delta_of(index, span))).astype(LOW)
            probs_low = probs.astype(LOW)
            dv_s[rows, span] = wide(
                lambda tile: mm(grad_ref[rows, tile], probs_low[:, inner(tile)], 1, 1))
            dk_s[rows, span] = wide(
                lambda tile: mm(qkv_ref[0, rows, tile], score_low[:, inner(tile)], 1, 1))
            dq_s[rows, span] = wide(
                lambda tile: mm(qkv_ref[1, rows, tile], score_low[:, inner(tile)]))

    @pl.when(jnp.logical_not(has_big))
    def _():
        narrow(0, 512)

    @pl.when(used > 512)
    def _():
        narrow(512, slots)

    @pl.when(used <= 512)
    def _():
        for store in (dq_s, dk_s, dv_s):
            store[:, 512:slots] = jnp.zeros((store.shape[0], slots - 512), F32)

    @pl.when(has_big)
    def _():
        wide = pl.ds(0, 640)
        dk = [jnp.zeros((HD, 640), F32)] * group
        dv = [jnp.zeros((HD, 640), F32)] * group
        for start, width in ((0, 256), (256, 256), (512, 128)):
            span = pl.ds(start, width)
            lane = lax.broadcasted_iota(jnp.int32, (1, width), 1)
            all_scores, all_grads = [], []
            for index in range(group):
                rows = head_rows(index)
                all_scores.append(mm(qkv_ref[1, rows, wide], qkv_ref[0, rows, span], 0, 0)[:BIG])
                all_grads.append(mm(qkv_ref[2, rows, wide], grad_ref[rows, span], 0, 0)[:BIG])
            for index in range(group):
                rows = head_rows(index)
                probs = jnp.exp(all_scores[index] - log_ref[index, :, span])
                if width == 128:
                    probs = jnp.where(lane < BIG - start, probs, 0.0)
                score_low = (probs * (all_grads[index] - delta_of(index, span))).astype(LOW)
                blank = jnp.zeros((640 - BIG, width), LOW)
                score_low = jnp.concatenate([score_low, blank], axis=0)
                probs_low = jnp.concatenate([probs.astype(LOW), blank], axis=0)
                dv[index] = dv[index] + mm(grad_ref[rows, span], probs_low, 1, 1)
                dk[index] = dk[index] + mm(qkv_ref[0, rows, span], score_low, 1, 1)
                dq = mm(qkv_ref[1, rows, wide], score_low)
                if width == 128:
                    dq = jnp.where(lane < BIG - start, dq, dq_s[rows, span])
                dq_s[rows, span] = dq
        inside = lax.broadcasted_iota(jnp.int32, (1, 640), 1) < BIG
        for index in range(group):
            rows = head_rows(index)
            dk_s[rows, wide] = jnp.where(inside, dk[index], dk_s[rows, wide])
            dv_s[rows, wide] = jnp.where(inside, dv[index], dv_s[rows, wide])

    sums = [jnp.zeros((HD, 1), F32)] * 3
    biases = [[], [], []]
    for index in range(group):
        rows = head_rows(index)
        for part, store, gain in ((0, dq_s, gain_q), (1, dk_s, gain_k)):
            unit = unit_ref[part, rows, :].astype(F32)
            grad = store[rows, :]
            if part == 0:
                grad = grad * 0.125
                sums[0] = sums[0] + jnp.sum(grad * unit, axis=1, keepdims=True)
                sums[1] = sums[1] + jnp.sum(grad, axis=1, keepdims=True)
            else:
                sums[2] = sums[2] + jnp.sum(grad * unit, axis=1, keepdims=True)
            unit_grad = grad * gain
            result = scale_ref[part, index] * (
                unit_grad
                - jnp.mean(unit_grad, axis=0, keepdims=True)
                - unit * jnp.mean(unit_grad * unit, axis=0, keepdims=True)
            )
            result = result.astype(LOW)
            dqkv_ref[part, rows, :] = result
            biases[part].append(jnp.sum(result.astype(F32), axis=1, keepdims=True))
        result = dv_s[rows, :].astype(LOW)
        dqkv_ref[2, rows, :] = result
        biases[2].append(jnp.sum(result.astype(F32), axis=1, keepdims=True))
    for part in range(3):
        bias_ref[part] = to_row(jnp.concatenate(biases[part], axis=0))
    blank = jnp.zeros((HD, 1), F32)
    gains_ref[:, 0:128] += to_row(jnp.concatenate(sums[:2], axis=0))
    gains_ref[:, 128:256] += to_row(jnp.concatenate([sums[2], blank], axis=0))


def attend_back(counts, qkv, attn, log_total, attn_grad, unit, scale, vectors, earlier, half,
                group=2):
    slots = qkv.shape[2]
    steps = HEADS // group // 2
    first = half * steps
    head_block = pl.BlockSpec((group * HD, slots), lambda h, c: (h + first, 0))
    dqkv_block = pl.BlockSpec((3, group * HD, slots), lambda h, c: (0, h + first, 0))
    held = pl.BlockSpec(memory_space=pl.ANY)
    extra = [vectors if earlier is None else earlier]
    return pl.pallas_call(
        functools.partial(attend_back_kernel, group),
        grid_spec=pltpu.PrefetchScalarGridSpec(
            num_scalar_prefetch=1,
            grid=(steps,),
            in_specs=[dqkv_block,
                      head_block,
                      pl.BlockSpec((group, 1, slots), lambda h, c: (h + first, 0, 0)),
                      head_block,
                      pl.BlockSpec((2, group * HD, slots), lambda h, c: (0, h + first, 0)),
                      pl.BlockSpec((2, group, 1, slots), lambda h, c: (0, h + first, 0, 0)),
                      whole(vectors.shape), held],
            out_specs=[dqkv_block,
                       pl.BlockSpec((3, 1, group * HD), lambda h, c: (0, 0, h)),
                       whole((1, 256))],
            scratch_shapes=[pltpu.VMEM((group * HD, slots), F32)] * 3,
        ),
        out_shape=[shape_of((3, D, slots), LOW), shape_of((3, 1, D // 2), F32),
                   shape_of((1, 256), F32)],
        input_output_aliases={} if earlier is None else {8: 0},
        compiler_params=params(20),
        cost_estimate=cost(14, 8e6),
        name="attend_back",
    )(counts, qkv, attn, log_total, attn_grad, unit, scale, vectors, *extra)


def segment_picker(counts_ref, first, width):
    images = counts_ref.shape[0]
    slot = first + lax.broadcasted_iota(jnp.int32, (images, width), 1)
    image = lax.broadcasted_iota(jnp.int32, (images, width), 0)
    start = jnp.int32(0)
    picked = jnp.zeros((images, width), jnp.bool_)
    for k in range(images):
        end = start + counts_ref[k]
        picked = picked | ((image == k) & (slot >= start) & (slot < end))
        start = end
    return picked.astype(F32), start


def image_sizes(counts_ref):
    images = counts_ref.shape[0]
    image = lax.broadcasted_iota(jnp.int32, (images, 1), 0)
    sizes = jnp.zeros((images, 1), F32)
    for k in range(images):
        sizes = jnp.where(image == k, jnp.maximum(counts_ref[k], 1).astype(F32), sizes)
    return sizes


def middle_kernel(counts_ref, place_ref, x_ref, attn_ref, w0, w1, w2, w3, vec_ref, cot_ref,
                  image_ref, x2_ref, h_ref, dy_ref, mix_ref, w_s):
    @pl.when(pl.program_id(0) == 0)
    def _():
        place_blocks(place_ref, (w0, w1, w2, w3), w_s)

    x2 = x_ref[...].astype(F32) + mm(attn_ref[...], w_s[...], 0, 1) + vector_row(vec_ref, "bias_out")
    x2_ref[...] = x2
    unit, _ = normalise(x2)
    h_ref[...] = (
        unit * vector_row(vec_ref, "gain_two") + vector_row(vec_ref, "bias_two")
    ).astype(LOW)
    tile = x_ref.shape[0]
    first = pl.program_id(0) * tile
    picker, used = segment_picker(counts_ref, first, tile)
    picker = picker.astype(LOW)
    image_grad = image_ref[...].astype(F32) / image_sizes(counts_ref)
    dy = jnp.zeros(x2.shape, F32)
    rest = image_grad
    for _ in range(3):
        high, rest = split_value32(rest)
        dy = dy + mm(picker, high, 0, 0)
    slot = first + lax.broadcasted_iota(jnp.int32, (tile, 1), 0)
    dy = dy + jnp.where(slot < used, cot_ref[...].astype(F32), 0.0)
    dy_ref[...] = dy
    mix_ref[...] = dy.astype(LOW)


def split_value32(value):
    high = value.astype(LOW)
    return high, value - high.astype(F32)


def middle(counts, place, patches, attn, w_blocks, vectors, patch_cot, image_cot):
    slots = patches.shape[0]
    images = counts.shape[0]
    return pl.pallas_call(
        middle_kernel,
        grid_spec=pltpu.PrefetchScalarGridSpec(
            num_scalar_prefetch=2,
            grid=(slots // TILE,),
            in_specs=[rows_of(D), lanes_of(D)] + [out_part(w_blocks[0])] * 4
            + [whole(vectors.shape), rows_of(D), whole((images, D))],
            out_specs=[rows_of(D)] * 4,
            scratch_shapes=[pltpu.VMEM((D, D), LOW)],
        ),
        out_shape=[shape_of((slots, D), F32), shape_of((slots, D), LOW),
                   shape_of((slots, D), F32), shape_of((slots, D), LOW)],
        compiler_params=params(20),
        cost_estimate=cost(9, 20e6),
        name="middle",
    )(counts, place, patches, attn, *w_blocks, vectors, patch_cot, image_cot)


def feed_kernel(distances, start_y, y_in_ref, dh_in_ref, h_ref, mix_ref, up_a, down_a, up_b,
                down_b, bias_ref, vec_ref,
                y_ref, dh_ref, grad_a, grad_b, bias_grad_a, bias_grad_b):
    @pl.when(pl.program_id(0) == 0)
    def _():
        if start_y:
            y_ref[...] = y_in_ref[...] + vector_row(vec_ref, "bias_down")
            dh_ref[...] = jnp.zeros_like(dh_ref)
        else:
            y_ref[...] = y_in_ref[...]
            dh_ref[...] = dh_in_ref[...]

    slots = h_ref.shape[0]
    for distance, up_ref, down_ref, grad_ref, bias_grad_ref in (
        (distances[0], up_a, down_a, grad_a, bias_grad_a),
        (distances[1], up_b, down_b, grad_b, bias_grad_b),
    ):
        up, down = up_ref[...], down_ref[...]
        h, mix = h_ref[...], mix_ref[...]
        u = mm(up, h, 1, 1) + to_column(bias_ref[distance : distance + 1])
        back = mm(down, mix, 1, 1)
        gate = 0.5 * (1.0 + lax.erf(u * (0.5**0.5)))
        slope = gate + u * (jnp.exp(-0.5 * u * u) * ((0.5 / math.pi) ** 0.5))
        hidden = (u * gate).astype(LOW)
        pre = (back * slope).astype(LOW)
        y_ref[...] += mm(hidden, down, 0, 0)
        dh_ref[...] += mm(pre, up, 0, 0)
        grad_up = mm(pre, h)
        grad_down = mm(hidden, mix)
        bias_grad = to_row(jnp.sum(pre.astype(F32), axis=1, keepdims=True))
        grad_ref[0] = grad_up.astype(LOW)
        grad_ref[1] = grad_down.astype(LOW)
        bias_grad_ref[...] = bias_grad


def feed(distances, y, dh2, h2, mix, pair_a, pair_b, bias_table, vectors, block=256):
    slots = y.shape[0]
    units = pair_a.shape[1]
    start_y = dh2 is None
    if start_y:
        dh2 = y
    up = pl.BlockSpec((None, block, D), lambda i: (0, i, 0))
    down = pl.BlockSpec((None, block, D), lambda i: (1, i, 0))
    bias = pl.BlockSpec((1, block), lambda i: (0, i))
    both = pl.BlockSpec((2, block, D), lambda i: (0, i, 0))
    dh_spec = pl.BlockSpec((8, D), lambda i: (0, 0)) if start_y else once((slots, D))
    return pl.pallas_call(
        functools.partial(feed_kernel, distances, start_y),
        grid=(units // block,),
        in_specs=[once((slots, D)), dh_spec, once((slots, D)), once((slots, D)),
                  up, down, up, down, pl.BlockSpec((bias_table.shape[0], block), lambda i: (0, i)),
                  whole(vectors.shape)],
        out_specs=[once((slots, D)), once((slots, D)), both, both, bias, bias],
        out_shape=[shape_of((slots, D), F32), shape_of((slots, D), F32),
                   shape_of((2, units, D), LOW), shape_of((2, units, D), LOW),
                   shape_of((1, units), F32), shape_of((1, units), F32)],
        compiler_params=params(26),
        cost_estimate=cost(24, 25e6),
        name="feed",
    )(y, dh2, h2, mix, pair_a, pair_a, pair_b, pair_b, bias_table, vectors)


def after_kernel(counts_ref, place_ref, y_ref, x2_ref, dh_ref, dy_ref, attn_ref, w0, w1, w2, w3,
                 vec_ref, out_ref, pooled_ref, dx2_ref, dattn_ref, grad_out_ref, sums_ref,
                 pool_s, grad_s, w_s):
    step = pl.program_id(0)

    @pl.when(step == 0)
    def _():
        pool_s[...] = jnp.zeros_like(pool_s)
        grad_s[...] = jnp.zeros_like(grad_s)
        sums_ref[...] = jnp.zeros_like(sums_ref)
        place_blocks(place_ref, (w0, w1, w2, w3), w_s)

    y = y_ref[...]
    tile = y.shape[0]
    out_ref[...] = y.astype(LOW)
    picker, _ = segment_picker(counts_ref, step * tile, tile)
    picker = picker.astype(LOW)
    rest = y
    pooled = pool_s[...]
    for _ in range(3):
        high, rest = split_value32(rest)
        pooled = pooled + mm(picker, high)
    pool_s[...] = pooled
    pooled_ref[...] = (pooled / image_sizes(counts_ref)).astype(LOW)
    unit, scale = normalise(x2_ref[...])
    dh = dh_ref[...]
    sums_ref[0:1] += column_sum(dh * unit)
    sums_ref[1:2] += column_sum(dh)
    dy = dy_ref[...]
    sums_ref[3:4] += column_sum(dy.astype(LOW).astype(F32))
    dx2 = dy + norm_back(unit, scale, dh * vector_row(vec_ref, "gain_two"))
    dx2_ref[...] = dx2
    da = dx2.astype(LOW)
    sums_ref[2:3] += column_sum(da.astype(F32))
    dattn_ref[...] = mm(w_s[...], da, 0, 1).astype(LOW)
    grad = grad_s[...] + mm(da, attn_ref[...], 0, 1)
    grad_s[...] = grad
    grad_out_ref[...] = grad.astype(LOW)


def after(counts, place, y, x2, dh2, dy, attn, w_blocks, vectors):
    slots = y.shape[0]
    images = counts.shape[0]
    return pl.pallas_call(
        after_kernel,
        grid_spec=pltpu.PrefetchScalarGridSpec(
            num_scalar_prefetch=2,
            grid=(slots // TILE,),
            in_specs=[rows_of(D), rows_of(D), rows_of(D), rows_of(D), lanes_of(D)]
            + [out_part(w_blocks[0])] * 4 + [whole(vectors.shape)],
            out_specs=[rows_of(D), whole((images, D)), rows_of(D), lanes_of(D), whole((D, D)),
                       whole((8, D))],
            scratch_shapes=[pltpu.VMEM((images, D), F32), pltpu.VMEM((D, D), F32),
                            pltpu.VMEM((D, D), LOW)],
        ),
        out_shape=[shape_of((slots, D), LOW), shape_of((images, D), LOW),
                   shape_of((slots, D), F32), shape_of((D, slots), LOW), shape_of((D, D), LOW),
                   shape_of((8, D), F32)],
        compiler_params=params(28),
        cost_estimate=cost(12, 25e6),
        name="after",
    )(counts, place, y, x2, dh2, dy, attn, *w_blocks, vectors)


def first_back_kernel(place_ref, x_ref, dqkv_ref, w0, w1, w2, w3, vec_ref, dx2_ref,
                      out_ref, sums_ref, w_s):
    @pl.when(pl.program_id(0) == 0)
    def _():
        sums_ref[...] = jnp.zeros_like(sums_ref)
        place_blocks(place_ref, (w0, w1, w2, w3), w_s)

    dh = mm(dqkv_ref[...], w_s[...], 0, 0)
    unit, scale = normalise(x_ref[...].astype(F32))
    sums_ref[0:1] += column_sum(dh * unit)
    sums_ref[1:2] += column_sum(dh)
    out_ref[...] = dx2_ref[...] + norm_back(unit, scale, dh * vector_row(vec_ref, "gain_one"))


def first_back(place, patches, dqkv, w_blocks, vectors, dx2):
    slots = patches.shape[0]
    return pl.pallas_call(
        first_back_kernel,
        grid_spec=pltpu.PrefetchScalarGridSpec(
            num_scalar_prefetch=1,
            grid=(slots // TILE,),
            in_specs=[rows_of(D), lanes_of(3 * D)] + [qkv_part(w_blocks[0])] * 4
            + [whole(vectors.shape), rows_of(D)],
            out_specs=[rows_of(D), whole((8, D))],
            scratch_shapes=[pltpu.VMEM((3 * D, D), LOW)],
        ),
        out_shape=[shape_of((slots, D), F32), shape_of((8, D), F32)],
        compiler_params=params(22),
        cost_estimate=cost(10, 17e6),
        name="first_back",
    )(place, patches, dqkv, *w_blocks, vectors, dx2)


SIDE = 256
GRID_BLOCKS = [(i, j) for i in range(D // SIDE) for j in range(i, D // SIDE)]


def moment_kernel(half_ref, own_ref, other_ref, mom_ref, grad_ref, moment_ref, gram_ref):
    rows = own_ref.shape[0]
    for ref, place in ((own_ref, half_ref[0]), (other_ref, 1 - half_ref[0])):
        span = pl.ds(pl.multiple_of(place * rows, rows), rows)
        grad = ref[...].astype(F32)
        grad_ref[span, :] = grad
        moment_ref[span, :] = MUON_DECAY * mom_ref[span, :] + grad
    moment_low = moment_ref[...].astype(LOW)
    for index, (i, j) in enumerate(GRID_BLOCKS):
        gram_ref[index] = mm(
            moment_low[:, i * SIDE : (i + 1) * SIDE], moment_low[:, j * SIDE : (j + 1) * SIDE], 0, 0
        )


def one_of(stack, index):
    return pl.BlockSpec(
        (None,) + stack.shape[1:],
        lambda i: (index,) + (0,) * (stack.ndim - 1),
        pipeline_mode=pl.Buffered(1),
    )


def moment_and_gram(half, own, other, mom):
    rows = mom.shape[0]
    blocks = len(GRID_BLOCKS)
    out_shape = [shape_of((rows, D), F32), shape_of((rows, D), F32),
                 shape_of((blocks, SIDE, SIDE), F32)]
    (own, own_index), (other, other_index) = own, other
    return pl.pallas_call(
        moment_kernel,
        grid=(1,),
        in_specs=[pl.BlockSpec(memory_space=pltpu.SMEM), one_of(own, own_index),
                  one_of(other, other_index), once((rows, D))],
        out_specs=[once(leaf.shape) for leaf in out_shape],
        out_shape=out_shape,
        compiler_params=params(16),
        cost_estimate=cost(4, rows * D * 14 + blocks * SIDE * SIDE * 4),
        name="moment",
    )(half, own, other, mom)


def muon_kernel(step_scale, half_ref, own_ref, other_ref, moment_ref, master_ref,
                new_ref, copy_ref, gram_s, low_s, rest_s, mix_s, rows_s, gram_ref):
    count = own_ref.shape[0]
    for index in range(count):
        gram_ref[half_ref[0] * count + index] = own_ref[index]
        gram_ref[(1 - half_ref[0]) * count + index] = other_ref[index]
    spans = [slice(i * SIDE, (i + 1) * SIDE) for i in range(D // SIDE)]

    def put(refs, i, j, blocks):
        for ref, block in zip(refs, blocks):
            ref[spans[i], spans[j]] = block
            if i != j:
                ref[spans[j], spans[i]] = block.T

    total = jnp.zeros((1, 1), F32)
    row = lax.broadcasted_iota(jnp.int32, (SIDE, SIDE), 0)
    column = lax.broadcasted_iota(jnp.int32, (SIDE, SIDE), 1)
    for index, (i, j) in enumerate(GRID_BLOCKS):
        if i == j:
            kept = jnp.where(row == column, gram_ref[index], 0.0)
            total = total + jnp.sum(jnp.sum(kept, axis=0, keepdims=True), axis=1, keepdims=True)
    scale = 1.0 / (jnp.sqrt(total) + 1e-07)
    square = scale * scale
    for index, (i, j) in enumerate(GRID_BLOCKS):
        block = gram_ref[index] * square
        put((gram_s,), i, j, (block,))
        put((low_s, rest_s), i, j, split_value(block))
    rows_s[...] = moment_ref[...].astype(LOW)
    for iteration in range(ITERS):
        careful = iteration == 0
        for i, j in GRID_BLOCKS:
            squared = mm(low_s[spans[i], :], low_s[:, spans[j]])
            put((mix_s,), i, j, ((NS_B * gram_s[spans[i], spans[j]] + NS_C * squared).astype(LOW),))
        if iteration == ITERS - 1:
            break
        middle_blocks = []
        for i in range(D // SIDE):
            for j in range(0 if careful else i, D // SIDE):
                block = NS_A * gram_s[spans[i], spans[j]] + mm(low_s[spans[i], :], mix_s[:, spans[j]])
                if careful:
                    block = block + mm(rest_s[spans[i], :], mix_s[:, spans[j]])
                middle_blocks.append((i, j, block))
        for i, j, block in middle_blocks:
            gram_s[spans[i], spans[j]] = block
            if careful:
                low_s[spans[i], spans[j]], rest_s[spans[i], spans[j]] = split_value(block)
            else:
                put((low_s,), i, j, (block.astype(LOW),))
        renewed = NS_A * rows_s[...].astype(F32) + mm(rows_s[...], mix_s[...])
        if careful:
            renewed = renewed * scale
        rows_s[...] = renewed.astype(LOW)
        gram_blocks = []
        for i, j in GRID_BLOCKS:
            block = NS_A * gram_s[spans[i], spans[j]] + mm(mix_s[spans[i], :], low_s[:, spans[j]])
            if careful:
                block = block + mm(mix_s[spans[i], :], rest_s[:, spans[j]])
            gram_blocks.append((i, j, block))
        for i, j, block in gram_blocks:
            gram_s[spans[i], spans[j]] = block
            put((low_s,), i, j, (block.astype(LOW),))
    renewed = NS_A * rows_s[...].astype(F32) + mm(rows_s[...], mix_s[...])
    new = master_ref[...] * (1.0 - MUON_RATE * MUON_SHRINK) - step_scale * renewed
    new_ref[...] = new
    copy_ref[...] = new.astype(LOW)


def muon(half, own, other, moment, master, step_scale):
    rows = moment.shape[0]
    (own, own_index), (other, other_index) = own, other
    out_shape = [shape_of((rows, D), F32), shape_of((rows, D), LOW)]
    return pl.pallas_call(
        functools.partial(muon_kernel, step_scale),
        grid=(1,),
        in_specs=[pl.BlockSpec(memory_space=pltpu.SMEM), one_of(own, own_index),
                  one_of(other, other_index), once((rows, D)), once((rows, D))],
        out_specs=[once(leaf.shape) for leaf in out_shape],
        out_shape=out_shape,
        scratch_shapes=[pltpu.VMEM((D, D), F32), pltpu.VMEM((D, D), LOW), pltpu.VMEM((D, D), LOW),
                        pltpu.VMEM((D, D), LOW), pltpu.VMEM((rows, D), LOW),
                        pltpu.VMEM((len(GRID_BLOCKS), SIDE, SIDE), F32)],
        compiler_params=params(30),
        cost_estimate=cost(18, rows * D * 14),
        name="muon",
    )(half, own, other, moment, master)


def per_device(
    patches,
    counts,
    owners,
    pooled_cot,
    patch_cot,
    master_qkv,
    master_out,
    master_up,
    master_down,
    mom_qkv,
    mom_out,
    mom_up,
    mom_down,
    vectors,
    vec_first,
    vec_second,
):
    dp_count = lax.axis_size("dp")
    ns_count = lax.axis_size("ns")
    slot_count = patches.shape[0]
    image_total = counts.shape[1]
    capacity = pooled_cot.shape[0] // dp_count
    low = jnp.bfloat16
    place = lax.axis_index("ns").astype(jnp.int32).reshape(1)
    half_dp = bit_of("dp", 0).astype(jnp.int32).reshape(1)
    half_ns = bit_of("ns", 0).astype(jnp.int32).reshape(1)

    own_first = jnp.concatenate([master_qkv, master_out]).astype(low)
    w_first = (own_first, swap(own_first, "ns", 0), swap(own_first, "ns", 1))
    row = vectors.reshape(1, -1)
    bias_start = STARTS["bias_up"]
    bias_table = jnp.concatenate(
        by_distance(vectors[bias_start : bias_start + FF].reshape(ns_count, -1)), axis=0
    )
    returned = lax.all_to_all(
        pooled_cot.reshape(dp_count, capacity, D), "dp", split_axis=0, concat_axis=0, tiled=True
    ).reshape(dp_count * capacity, D)
    targets = owner_slots(owners[0], capacity)
    routing = (
        jnp.arange(dp_count * capacity, dtype=jnp.int32)[:, None] == targets[None, :]
    ).astype(low)
    image_cot = dot32(routing.T, returned).astype(low)
    sizes = counts[0]
    own_pair = jnp.stack([master_up, master_down]).astype(low)
    far_first, (own_pair, image_cot) = tie(w_first[2], (own_pair, image_cot))
    w_first = (w_first[0], w_first[1], far_first, swap(far_first, "ns", 0))
    own_pair, _ = tie(own_pair, far_first)
    near_pair, next_pair, far_pair = own_pair, swap(own_pair, "ns", 0), swap(own_pair, "ns", 1)
    first_low, qkv, unit, scale = project(place, patches, w_first, row)
    attn, log_total = attend(sizes, qkv)
    attn, far_pair = tie(attn, far_pair)
    pairs = (near_pair, next_pair, far_pair, swap(far_pair, "ns", 0))
    x2, second_low, row_grad, mixed_low = middle(
        sizes, place, patches, attn, w_first, row, patch_cot, image_cot
    )
    y, second_grad, grad_3, grad_1, bias_3, bias_1 = feed(
        (3, 1), x2, None, second_low, mixed_low, pairs[3], pairs[1], bias_table, row
    )
    came_3, came_1 = swap(grad_3, "ns", 0), swap(grad_1, "ns", 0)
    y, second_grad, grad_2, grad_0, bias_2, bias_0 = feed(
        (2, 0), y, second_grad, second_low, mixed_low, pairs[2], pairs[0], bias_table, row
    )
    sent, kept = add_low(grad_2, came_3), add_low(grad_0, came_1)
    up, down = Chain(sum_up(kept[0], sent[0])), Chain(sum_down(kept[1], sent[1]))
    y, (sent, kept) = tie(y, (sent, kept))
    out_patches, pooled, middle_grad, attn_grad, grad_out, sums_two = after(
        sizes, place, y, x2, second_grad, row_grad, attn, w_first, row
    )
    out = Chain(sum_blocks(grad_out.reshape(ns_count, -1, D), False))
    dqkv, bias_a, gains_a = attend_back(
        sizes, qkv, attn, log_total, attn_grad, unit, scale, row, None, 0
    )
    dqkv = meet(up, down, out, also=dqkv)
    dqkv, bias_b, gains_b = attend_back(
        sizes, qkv, attn, log_total, attn_grad, unit, scale, row, dqkv, 1
    )
    outgoing = dot32(routing, pooled).astype(low).reshape(dp_count, capacity, D)
    dqkv = meet(up, down, out, also=dqkv.reshape(3 * D, slot_count))
    pair = Chain(rest_of_dp(jnp.stack([up.result, down.result]), 1, True))
    grad_qkv = dot32(dqkv, first_low).astype(low)
    three = Chain(sum_blocks(grad_qkv.reshape(ns_count, -1, D), True))
    meet(three)
    middle_grad = meet(pair, out, also=middle_grad)
    patch_grad, sums_one = first_back(place, patches, dqkv, w_first, row, middle_grad)
    sums_one, patch_grad = meet(three, also=(sums_one, patch_grad))
    gains = gains_a + gains_b
    up_bias_grad = by_distance(jnp.concatenate([bias_0, bias_1, bias_2, bias_3], axis=0))
    vector_local = jnp.concatenate(
        [
            sums_one[0:1],
            sums_one[1:2],
            jnp.concatenate([bias_a, bias_b], axis=2).reshape(1, 3 * D),
            gains[:, : 3 * HD],
            sums_two[2:3],
            sums_two[0:1],
            sums_two[1:2],
            *up_bias_grad,
            sums_two[3:4],
        ],
        axis=1,
    )
    vector_size = vector_local.shape[1]
    padded = -(-vector_size // 1024) * 1024
    vector = Chain(sum_vector(
        jnp.pad(vector_local, ((0, 0), (0, padded - vector_size))).reshape(-1, 128)
    ))
    moments = (mom_qkv, mom_out, mom_up, mom_down)
    masters = (master_qkv, master_out, master_up, master_down)
    grad_parts, moment_parts = [None] * 4, [None] * 4
    new_masters, copies = [None] * 4, [None] * 4

    def momentum(kind, own, other):
        grad_parts[kind], moment_parts[kind], gram = moment_and_gram(
            half_dp, own, other, moments[kind]
        )
        return Chain(sum_gram(gram))

    def iterate(kind, halves_of_gram):
        rows = moments[kind].shape[0] * ns_count
        step_scale = MUON_RATE * math.sqrt(max(1.0, rows / D))
        new_masters[kind], copies[kind] = muon(
            half_ns, *halves_of_gram, moment_parts[kind], masters[kind], step_scale
        )

    meet(pair, out, vector)
    meet(three)
    meet(pair, out, vector)
    outgoing = meet(three, out, also=outgoing)
    finish(out)
    gram_out = momentum(1, *((half[None], 0) for half in out.result))
    arrived = lax.all_to_all(outgoing, "dp", split_axis=0, concat_axis=0, tiled=True)
    pooled_rows = arrived.reshape(dp_count * capacity, D)
    pooled_rows = meet(three, gram_out, vector, also=pooled_rows)
    finish(vector)
    finish(pair)
    gram_up = momentum(2, *((half, 0) for half in pair.result))
    gram_down = momentum(3, *((half, 1) for half in pair.result))
    meet(three, gram_out)
    meet(gram_up)
    finish(three)
    gram_three = momentum(0, *((half[None], 0) for half in three.result))
    meet(gram_down, gram_out)
    finish(gram_out)
    iterate(1, gram_out.result)
    new_masters[1] = meet(gram_up, gram_three, also=new_masters[1])
    finish(gram_up)
    iterate(2, gram_up.result)
    new_masters[2] = meet(gram_down, also=new_masters[2])
    finish(gram_down)
    iterate(3, gram_down.result)
    new_masters[3] = meet(gram_three, also=new_masters[3])
    finish(gram_three)
    iterate(0, gram_three.result)
    vector_grad = vector.result.reshape(-1)[:vector_size]
    vector_first = BETA_ONE * vec_first + (1.0 - BETA_ONE) * vector_grad
    vector_second = BETA_TWO * vec_second + (1.0 - BETA_TWO) * vector_grad * vector_grad
    first_hat = vector_first / (1.0 - BETA_ONE**STEP)
    second_hat = vector_second / (1.0 - BETA_TWO**STEP)
    vector_new = vectors - ADAM_RATE * first_hat / (jnp.sqrt(second_hat) + 1e-08)
    return (
        out_patches,
        pooled_rows,
        patch_grad,
        grad_parts[0],
        grad_parts[1],
        grad_parts[2],
        grad_parts[3],
        moment_parts[0],
        moment_parts[1],
        moment_parts[2],
        moment_parts[3],
        new_masters[0],
        new_masters[1],
        new_masters[2],
        new_masters[3],
        *copies,
        vector_grad,
        vector_first,
        vector_second,
        vector_new,
    )


def solution(mesh):
    placed = (
        P(("dp", "ns"), None),
        P(("dp", "ns"), None),
        P(("dp", "ns"), None),
        P(("dp", "ns"), None),
        P(("dp", "ns"), None),
        P("ns", None),
        P("ns", None),
        P("ns", None),
        P("ns", None),
        P("ns", None),
        P("ns", None),
        P("ns", None),
        P("ns", None),
        P(),
        P(),
        P(),
    )
    return jax.shard_map(
        per_device,
        mesh=mesh,
        in_specs=placed,
        out_specs=(
            P(("dp", "ns"), None),
            P(("dp", "ns"), None),
            P(("dp", "ns"), None),
            P("ns", None),
            P("ns", None),
            P("ns", None),
            P("ns", None),
            P("ns", None),
            P("ns", None),
            P("ns", None),
            P("ns", None),
            P("ns", None),
            P("ns", None),
            P("ns", None),
            P("ns", None),
            P("ns", None),
            P("ns", None),
            P("ns", None),
            P("ns", None),
            P(),
            P(),
            P(),
            P(),
        ),
        check_vma=False,
    )
```

time: 667 us -> 442 us (0.66)
  matrix products: 136 us -> 5.7 us
  waiting for transfers between devices: 212 us -> 133 us
  Pallas kernels: 146 us -> 177 us
  other arithmetic: 52.8 us -> 29.1 us
  between operations: 18.4 us -> 1.93 us
  starting transfers between devices: 65.1 us -> 57.4 us
    dot_general x79 -> x3, matrix products: 127 us -> 5.7 us  [dot32(): return jnp.dot(first, second, preferred_element_type=jnp.float32)]
    all_gather x4 -> x0, waiting for transfers between devices: 61.2 us -> none  [the longest x1 39.5 us: per_device(): lax.all_gather(master_up.astype(jnp.bfloat16), 'ns', axis=0, tiled=True)]
    pallas_call x3 -> x12, Pallas kernels: 66.7 us -> 124 us  [the longest x4 54.3 us: muon(): pl.pallas_call(functools.partial(muon_kernel, step_scale), grid=(1,), in_...]
    ppermute x45 -> x48, waiting for transfers between devices: 151 us -> 114 us  [the longest x41 114 us: swap(): lax.ppermute(value, axis, [(index, index ^ 1 << bit) for index in range(c...]
    all_to_all x1, waiting for transfers between devices: 0.01 us -> 16.4 us  [per_device(): lax.all_to_all(outgoing, 'dp', split_axis=0, concat_axis=0, tiled=True)]
    unnamed x102 -> x142, local copies, waits for them, and re-layouts: 3.4 us -> 19.5 us
    add x15 -> x11, other arithmetic: 21 us -> 5.32 us  [the longest x4 2.86 us: sum_gram(): gram = gram + (yield swap(gram, 'ns', 0))]
    pallas_call x1 -> x2, Pallas kernels: 27.7 us -> 13.9 us  [attend_back(): pl.pallas_call(functools.partial(attend_back_kernel, group), grid_spec=pl...]
  transfers between devices with their start and end apart: 51 -> 50, of which waited for: 23 -> 23; matrix products, arithmetic and copies ran while one was open for 23% -> 8% of each run, Pallas kernels for 13% -> 33%
where the time goes in v2:
time: 442 us; the launch traced here: 434 us
  Pallas kernels  177 us (40%)
  waiting for transfers between devices  133 us (30%)
  starting transfers between devices  57.4 us (13%)
  local copies, waits for them, and re-layouts  29.8 us (7%)
  other arithmetic  29.1 us (7%)
  matrix products  5.7 us (1%)
    ppermute x41, waiting for transfers between devices, swap(): lax.ppermute(value, axis, [(index, index ^ 1 << bit) for index in range(c...  114 us
    pallas_call x4, Pallas kernels, muon(): pl.pallas_call(functools.partial(muon_kernel, step_scale), grid=(1,), in_...  54.3 us
    ppermute x41, starting transfers between devices, swap(): lax.ppermute(value, axis, [(index, index ^ 1 << bit) for index in range(c...  38.9 us
    pallas_call x2, Pallas kernels, feed(): pl.pallas_call(functools.partial(feed_kernel, distances, start_y), grid=(...  38.5 us
    pallas_call x1, Pallas kernels, attend(): pl.pallas_call(functools.partial(attend_kernel, group), grid_spec=pltpu.P...  24.1 us
    unnamed x142, local copies, waits for them, and re-layouts  19.5 us
    all_to_all x1, waiting for transfers between devices, per_device(): lax.all_to_all(outgoing, 'dp', split_axis=0, concat_axis=0, tiled=True)  16.4 us
    convert_element_type x18, other arithmetic, add_low(): (first.astype(jnp.float32) + second.astype(jnp.float32)).astype(jnp.bfloa...  16.2 us
  transfers between devices with their start and end apart: 50, of which 23 were waited for; matrix products, arithmetic and copies ran while one was open for 8% of the time, Pallas kernels for 33%

profile of v2, /device:TPU:0, one launch (start us, length us, event | category | flops | bytes accessed | tf_op | source)
XLA Modules:
  0.0 433.8 jit_solution(11807943385256229754)
XLA Ops:
  6.9 5.8 %all-to-all-start = ((bf16[8,2,768]{2,1,0:T(2,128)(2,1)}), bf16[8,2,768]{2,1,0:T(2,128)(2,1)}, u32[]{:S(2)}, u32[]{:S(2)}) async-start(bf16[8,2,768]{2,1,0:T(2,128)(2,1)} %reshape.148), calls=%async_computation | async-start | bytes 49152 | tf_op jit(solution)/shard_map/all_to_all | solution.py:1043
  22.3 9.3 %collective-permute-done.1.w2 = bf16[768,768]{1,0:T(8,128)(2,1)} collective-permute-done((bf16[768,768]{1,0:T(8,128)(2,1)S(1)}, bf16[768,768]{1,0:T(8,128)(2,1)}, u32[]{:S(2)}, u32[]{:S(2)}) %collective-permute-start.1) | collective-permute-done | bytes 1179680 | tf_op jit(solution)/shard_map/ppermute | solution.py:40
  36.9 10.3 %project.1 = (bf16[1024,768]{1,0:T(8,128)(2,1)S(1)}, bf16[3,768,1024]{2,1,0:T(8,128)(2,1)S(1)}, bf16[2,768,1024]{2,1,0:T(8,128)(2,1)S(1)}, f32[2,12,1,1024]{3,2,1,0:T(1,128)S(1)}) custom-call(s32[1]{0:T(128)} %bitcast.1.place_ref, bf16[1024,768]{1,0:T(8,128)(2,1)S(1)} %copy-done.17, bf16[768,768]{1,0:T(8,128)(2,1)S(1)} %pad_maximum_fusion.2.w0, ...), custom_call_target="tpu_custom_call" | custom-call | flops 10000000000 | bytes 16000000 | tf_op jit(solution)/shard_map/project/pallas_call | solution.py:328
  47.3 24.1 %attend.1 = (bf16[768,1024]{1,0:T(8,128)(2,1)S(1)}, f32[12,1,1024]{2,1,0:T(1,128)S(1)}) custom-call(s32[16]{0:T(128)S(1)} %bitcast.149, bf16[3,768,1024]{2,1,0:T(8,128)(2,1)S(1)} %get-tuple-element.129.qkv_ref), custom_call_target="tpu_custom_call" | custom-call | flops 28000000000 | bytes 7000000 | tf_op jit(solution)/shard_map/attend/pallas_call | solution.py:458
  73.2 12.4 %collective-permute-done.3.up_a.down_a = bf16[2,768,768]{2,1,0:T(8,128)(2,1)} collective-permute-done((bf16[2,768,768]{2,1,0:T(8,128)(2,1)}, bf16[2,768,768]{2,1,0:T(8,128)(2,1)}, u32[]{:S(2)}, u32[]{:S(2)}) %collective-permute-start.3) | collective-permute-done | bytes 2359328 | tf_op jit(solution)/shard_map/ppermute | solution.py:40
  93.6 6.3 %middle.1 = (f32[1024,768]{1,0:T(8,128)S(1)}, bf16[1024,768]{1,0:T(8,128)(2,1)S(1)}, f32[1024,768]{1,0:T(8,128)S(1)}, bf16[1024,768]{1,0:T(8,128)(2,1)S(1)}) custom-call(s32[16]{0:T(128)S(1)} %bitcast.150, s32[1]{0:T(128)} %bitcast.1.place_ref, bf16[1024,768]{1,0:T(8,128)(2,1)S(1)} %copy-done.18, bf16[768,1024]{1,0:T(8,128)(2,1)S(1)} %copy-done.38, ...), custom_call_target="tpu_custom_call" | custom-call | flops 8999999488 | bytes 20000000 | tf_op jit(solution)/shard_map/middle/pallas_call | solution.py:699
  101.7 19.6 %feed.2 = (f32[1024,768]{1,0:T(8,128)S(1)}, f32[1024,768]{1,0:T(8,128)S(1)}, bf16[2,768,768]{2,1,0:T(8,128)(2,1)S(1)}, bf16[2,768,768]{2,1,0:T(8,128)(2,1)S(1)},...) custom-call(f32[1024,768]{1,0:T(8,128)S(1)} %get-tuple-element.135.y_in_ref.dh_in_ref.x2_ref, ...), custom_call_target="tpu_custom_call" | custom-call | flops 24000000000 | bytes 25000000 | tf_op jit(solution)/shard_map/feed/pallas_call | solution.py:763
  122.0 18.9 %feed.3 = (f32[1024,768]{1,0:T(8,128)S(1)}, f32[1024,768]{1,0:T(8,128)S(1)}, bf16[2,768,768]{2,1,0:T(8,128)(2,1)S(1)}, bf16[2,768,768]{2,1,0:T(8,128)(2,1)S(1)},...) custom-call(f32[1024,768]{1,0:T(8,128)S(1)} %get-tuple-element.139.y_in_ref, f32[1024,768]{1,0:T(8,128)S(1)} %get-tuple-element.140.dh_in_ref, ...), custom_call_target="tpu_custom_call" | custom-call | flops 24000000000 | bytes 25000000 | tf_op jit(solution)/shard_map/feed/pallas_call | solution.py:763
  141.6 3.8 add_convert_fusion
  153.7 8.9 %after.1 = (bf16[1024,768]{1,0:T(8,128)(2,1)}, bf16[16,768]{1,0:T(8,128)(2,1)S(1)}, f32[1024,768]{1,0:T(8,128)S(1)}, bf16[768,1024]{1,0:T(8,128)(2,1)S(1)}, bf16...) custom-call(s32[16]{0:T(128)S(1)} %bitcast.151, s32[1]{0:T(128)} %bitcast.1.place_ref, f32[1024,768]{1,0:T(8,128)S(1)} %copy-done.30, ...), custom_call_target="tpu_custom_call" | custom-call | flops 12000000000 | bytes 25000000 | tf_op jit(solution)/shard_map/after/pallas_call | solution.py:822
  166.8 6.9 %attend_back.2 = (bf16[3,768,1024]{2,1,0:T(8,128)(2,1)S(1)}, f32[3,1,384]{2,1,0:T(1,128)S(1)}, f32[1,256]{1,0:T(1,128)S(1)}) custom-call(s32[16]{0:T(128)S(1)} %bitcast.152, bf16[3,768,1024]{2,1,0:T(8,128)(2,1)S(1)} %bitcast.157, bf16[768,1024]{1,0:T(8,128)(2,1)S(1)} %copy-done.39, f32[12,1,1024]{2,1,0:T(1,128)S(1)} %copy-done.43, ...), custom_call_target="tpu_custom_call" | custom-call | flops 14000000000 | bytes 8000000 | tf_op jit(solution)/shard_map/attend_back/pallas_call | solution.py:615
  177.6 13.6 %collective-permute-done.8 = bf16[768,768]{1,0:T(8,128)(2,1)S(1)} collective-permute-done((bf16[768,768]{1,0:T(8,128)(2,1)S(1)}, bf16[768,768]{1,0:T(8,128)(2,1)S(1)}, u32[]{:S(2)}, u32[]{:S(2)}) %collective-permute-start.8) | collective-permute-done | bytes 1179680 | tf_op jit(solution)/shard_map/ppermute | solution.py:40
  196.1 7.1 %attend_back.3 = (bf16[3,768,1024]{2,1,0:T(8,128)(2,1)S(1)}, f32[3,1,384]{2,1,0:T(1,128)S(1)}, f32[1,256]{1,0:T(1,128)S(1)}) custom-call(s32[16]{0:T(128)S(1)} %bitcast.153, bf16[3,768,1024]{2,1,0:T(8,128)(2,1)S(1)} %bitcast.159, bf16[768,1024]{1,0:T(8,128)(2,1)S(1)} %copy-done.39, f32[12,1,1024]{2,1,0:T(1,128)S(1)} %copy-done.43, ...), custom_call_target="tpu_custom_call", output_to_operand_aliasing={{0}: (8, {})} | custom-call | flops 14000000000 | bytes 8000000 | tf_op jit(solution)/shard_map/attend_back/pallas_call | solution.py:615
  203.2 9.0 %collective-permute-done.12 = bf16[384,768]{1,0:T(8,128)(2,1)S(1)} collective-permute-done((bf16[384,768]{1,0:T(8,128)(2,1)S(1)}, bf16[384,768]{1,0:T(8,128)(2,1)S(1)}, u32[]{:S(2)}, u32[]{:S(2)}) %collective-permute-start.12) | collective-permute-done | bytes 589856 | tf_op jit(solution)/shard_map/ppermute | solution.py:40
  212.2 4.0 convolution_convert_fusion
  221.0 3.9 collective-permute-done.17
  224.9 7.8 %collective-permute-done.16 = bf16[2,192,768]{2,1,0:T(8,128)(2,1)S(1)} collective-permute-done((bf16[2,192,768]{2,1,0:T(8,128)(2,1)S(1)}, bf16[2,192,768]{2,1,0:T(8,128)(2,1)S(1)}, u32[]{:S(2)}, u32[]{:S(2)}) %collective-permute-start.16) | collective-permute-done | bytes 589856 | tf_op jit(solution)/shard_map/ppermute | solution.py:40
  241.9 9.1 %first_back.1 = (f32[1024,768]{1,0:T(8,128)}, f32[8,768]{1,0:T(8,128)S(1)}) custom-call(s32[1]{0:T(128)} %bitcast.1.place_ref, bf16[1024,768]{1,0:T(8,128)(2,1)S(1)} %copy-done.19, bf16[2304,1024]{1,0:T(8,128)(2,1)S(1)} %bitcast.155, bf16[768,768]{1,0:T(8,128)(2,1)S(1)} %pad_maximum_fusion.2.w0, bf16[768,768]{1,0:T(8,128)(2,1)} %collective-permute-done.w1, ...), custom_call_target="tpu_custom_call" | custom-call | flops 10000000000 | bytes 17000000 | tf_op jit(solution)/shard_map/first_back/pallas_call | solution.py:859
  251.1 10.0 %collective-permute-done.15 = bf16[1,576,768]{2,1,0:T(8,128)(2,1)S(1)} collective-permute-done((bf16[1,576,768]{2,1,0:T(8,128)(2,1)S(1)}, bf16[1,576,768]{2,1,0:T(8,128)(2,1)S(1)}, u32[]{:S(2)}, u32[]{:S(2)}) %collective-permute-start.15) | collective-permute-done | bytes 884768 | tf_op jit(solution)/shard_map/ppermute | solution.py:40
  274.8 5.7 %collective-permute-done.18 = bf16[288,768]{1,0:T(8,128)(2,1)S(1)} collective-permute-done((bf16[288,768]{1,0:T(8,128)(2,1)S(1)}, bf16[288,768]{1,0:T(8,128)(2,1)S(1)}, u32[]{:S(2)}, u32[]{:S(2)}) %collective-permute-start.18) | collective-permute-done | bytes 442400 | tf_op jit(solution)/shard_map/ppermute | solution.py:40
  281.5 9.2 %collective-permute-done.26 = bf16[96,768]{1,0:T(8,128)(2,1)S(1)} collective-permute-done((bf16[96,768]{1,0:T(8,128)(2,1)S(1)}, bf16[96,768]{1,0:T(8,128)(2,1)S(1)}, u32[]{:S(2)}, u32[]{:S(2)}) %collective-permute-start.26) | collective-permute-done | bytes 147488 | tf_op jit(solution)/shard_map/ppermute | solution.py:40
  304.7 4.4 %all-to-all-start.1 = ((bf16[8,2,768]{2,1,0:T(2,128)(2,1)}), bf16[8,2,768]{2,1,0:T(2,128)(2,1)}, u32[]{:S(2)}, u32[]{:S(2)}) async-start(bf16[8,2,768]{2,1,0:T(2,128)(2,1)} %reshape.158), calls=%async_computation.1 | async-start | bytes 49152 | tf_op jit(solution)/shard_map/all_to_all | solution.py:1139
  313.4 16.4 %all-to-all-done.1 = bf16[8,2,768]{2,1,0:T(2,128)(2,1)} async-done(((bf16[8,2,768]{2,1,0:T(2,128)(2,1)}), bf16[8,2,768]{2,1,0:T(2,128)(2,1)}, u32[]{:S(2)}, u32[]{:S(2)}) %all-to-all-start.1) | async-done | bytes 24608 | tf_op jit(solution)/shard_map/all_to_all | solution.py:1139
  335.1 3.8 moment.6
  340.4 3.8 moment.7
  344.4 3.5 collective-permute-done.34
  347.9 4.8 %collective-permute-done.35 = f32[3,256,256]{2,1,0:T(8,128)S(1)} collective-permute-done((f32[3,256,256]{2,1,0:T(8,128)S(1)}, f32[3,256,256]{2,1,0:T(8,128)S(1)}, u32[]{:S(2)}, u32[]{:S(2)}) %collective-permute-start.35) | collective-permute-done | bytes 786464 | tf_op jit(solution)/shard_map/ppermute | solution.py:40
  355.7 8.0 %collective-permute-done.36 = bf16[288,768]{1,0:T(8,128)(2,1)S(1)} collective-permute-done((bf16[288,768]{1,0:T(8,128)(2,1)S(1)}, bf16[288,768]{1,0:T(8,128)(2,1)S(1)}, u32[]{:S(2)}, u32[]{:S(2)}) %collective-permute-start.36) | collective-permute-done | bytes 442400 | tf_op jit(solution)/shard_map/ppermute | solution.py:40
  365.9 10.9 %muon.4 = (f32[192,768]{1,0:T(8,128)}, bf16[192,768]{1,0:T(8,128)(2,1)}) custom-call(s32[1]{0:T(128)} %bitcast.47.half_ref, f32[1,3,256,256]{3,2,1,0:T(8,128)S(1)} %bitcast.129, f32[1,3,256,256]{3,2,1,0:T(8,128)S(1)} %bitcast.143, f32[192,768]{1,0:T(8,128)S(1)} %copy-done.25, f32[192,768]{1,0:T(8,128)S(1)} %copy-done.5), custom_call_target="tpu_custom_call" | custom-call | flops 17999998976 | bytes 2064384 | tf_op jit(solution)/shard_map/muon/pallas_call | solution.py:992
  379.3 15.1 %muon.5 = (f32[768,768]{1,0:T(8,128)}, bf16[768,768]{1,0:T(8,128)(2,1)}) custom-call(s32[1]{0:T(128)} %bitcast.47.half_ref, f32[1,3,256,256]{3,2,1,0:T(8,128)S(1)} %bitcast.131, f32[1,3,256,256]{3,2,1,0:T(8,128)S(1)} %bitcast.145, f32[768,768]{1,0:T(8,128)S(1)} %copy-done.22, f32[768,768]{1,0:T(8,128)S(1)} %copy-done), custom_call_target="tpu_custom_call" | custom-call | flops 17999998976 | bytes 8257536 | tf_op jit(solution)/shard_map/muon/pallas_call | solution.py:992
  399.7 14.9 %muon.6 = (f32[768,768]{1,0:T(8,128)}, bf16[768,768]{1,0:T(8,128)(2,1)}) custom-call(s32[1]{0:T(128)} %bitcast.47.half_ref, f32[1,3,256,256]{3,2,1,0:T(8,128)S(1)} %bitcast.132, f32[1,3,256,256]{3,2,1,0:T(8,128)S(1)} %bitcast.146, f32[768,768]{1,0:T(8,128)S(1)} %copy-done.23, f32[768,768]{1,0:T(8,128)S(1)} %copy-done.1), custom_call_target="tpu_custom_call" | custom-call | flops 17999998976 | bytes 8257536 | tf_op jit(solution)/shard_map/muon/pallas_call | solution.py:992
  420.2 13.4 %muon.7 = (f32[576,768]{1,0:T(8,128)}, bf16[576,768]{1,0:T(8,128)(2,1)}) custom-call(s32[1]{0:T(128)} %bitcast.47.half_ref, f32[1,3,256,256]{3,2,1,0:T(8,128)S(1)} %bitcast.130, f32[1,3,256,256]{3,2,1,0:T(8,128)S(1)} %bitcast.144, f32[576,768]{1,0:T(8,128)S(1)} %copy-done.24, f32[576,768]{1,0:T(8,128)S(1)} %copy-done.3), custom_call_target="tpu_custom_call" | custom-call | flops 17999998976 | bytes 6193152 | tf_op jit(solution)/shard_map/muon/pallas_call | solution.py:992
  (307 shorter events, 127.3 us)
Async XLA Ops:
  2.5 29.1 %collective-permute-start.1 = (bf16[768,768]{1,0:T(8,128)(2,1)S(1)}, bf16[768,768]{1,0:T(8,128)(2,1)}, u32[]{:S(2)}, u32[]{:S(2)}) collective-permute-start(bf16[768,768]{1,0:T(8,128)(2,1)S(1)} %pad_maximum_fusion.2.w0), channel_id=1, source_target_pairs={{0,2},{1,3},{2,0},{3,1},{4,6},{5,7},{6,4},{7,5},{8,10},{9,11},{10,... | collective-permute-start | bytes 3538952 | tf_op jit(solution)/shard_map/ppermute | solution.py:40
  5.5 28.0 %collective-permute-start = (bf16[768,768]{1,0:T(8,128)(2,1)S(1)}, bf16[768,768]{1,0:T(8,128)(2,1)}, u32[]{:S(2)}, u32[]{:S(2)}) collective-permute-start(bf16[768,768]{1,0:T(8,128)(2,1)S(1)} %pad_maximum_fusion.2.w0), channel_id=1, source_target_pairs={{0,1},{1,0},{2,3},{3,2},{4,5},{5,4},{6,7},{7,6},{8,9},{9,8},{10,11... | collective-permute-start | bytes 3538952 | tf_op jit(solution)/shard_map/ppermute | solution.py:40
  6.9 12.5 %all-to-all-start = ((bf16[8,2,768]{2,1,0:T(2,128)(2,1)}), bf16[8,2,768]{2,1,0:T(2,128)(2,1)}, u32[]{:S(2)}, u32[]{:S(2)}) async-start(bf16[8,2,768]{2,1,0:T(2,128)(2,1)} %reshape.148), calls=%async_computation | async-start | bytes 49152 | tf_op jit(solution)/shard_map/all_to_all | solution.py:1043
  31.6 54.0 %collective-permute-start.3 = (bf16[2,768,768]{2,1,0:T(8,128)(2,1)}, bf16[2,768,768]{2,1,0:T(8,128)(2,1)}, u32[]{:S(2)}, u32[]{:S(2)}) collective-permute-start(bf16[2,768,768]{2,1,0:T(8,128)(2,1)} %pad_maximum_fusion.up_b.down_b), channel_id=1, source_target_pairs={{0,2},{1,3},{2,0},{3,1},{4,6},{5,7},{6,4},{7,5},{8,10},{9,11},{10,... | collective-permute-start | bytes 7077896 | tf_op jit(solution)/shard_map/ppermute | solution.py:40
  33.3 68.3 %collective-permute-start.5 = (bf16[2,768,768]{2,1,0:T(8,128)(2,1)}, bf16[2,768,768]{2,1,0:T(8,128)(2,1)}, u32[]{:S(2)}, u32[]{:S(2)}) collective-permute-start(bf16[2,768,768]{2,1,0:T(8,128)(2,1)} %pad_maximum_fusion.up_b.down_b), channel_id=1, source_target_pairs={{0,1},{1,0},{2,3},{3,2},{4,5},{5,4},{6,7},{7,6},{8,9},{9,8},{10,11... | collective-permute-start | bytes 7077896 | tf_op jit(solution)/shard_map/ppermute | solution.py:40
  85.5 16.1 %collective-permute-start.4 = (bf16[2,768,768]{2,1,0:T(8,128)(2,1)}, bf16[2,768,768]{2,1,0:T(8,128)(2,1)}, u32[]{:S(2)}, u32[]{:S(2)}) collective-permute-start(bf16[2,768,768]{2,1,0:T(8,128)(2,1)} %collective-permute-done.3.up_a.down_a), channel_id=1, source_target_pairs={{0,1},{1,0},{2,3},{3,2},{4,5},{5,4},{6,7},{7,6},{8,9},{9,8},{10,11... | collective-permute-start | bytes 7077896 | tf_op jit(solution)/shard_map/ppermute | solution.py:40
  121.3 20.3 %collective-permute-start.7 = (bf16[2,768,768]{2,1,0:T(8,128)(2,1)S(1)}, bf16[2,768,768]{2,1,0:T(8,128)(2,1)}, u32[]{:S(2)}, u32[]{:S(2)}) collective-permute-start(bf16[2,768,768]{2,1,0:T(8,128)(2,1)S(1)} %get-tuple-element.145), channel_id=1, source_target_pairs={{0,1},{1,0},{2,3},{3,2},{4,5},{5,4},{6,7},{7,6},{8,9},{9,8},{10,11... | collective-permute-start | bytes 7077896 | tf_op jit(solution)/shard_map/ppermute | solution.py:40
  121.9 23.7 %collective-permute-start.6 = (bf16[2,768,768]{2,1,0:T(8,128)(2,1)S(1)}, bf16[2,768,768]{2,1,0:T(8,128)(2,1)}, u32[]{:S(2)}, u32[]{:S(2)}) collective-permute-start(bf16[2,768,768]{2,1,0:T(8,128)(2,1)S(1)} %get-tuple-element.143), channel_id=1, source_target_pairs={{0,1},{1,0},{2,3},{3,2},{4,5},{5,4},{6,7},{7,6},{8,9},{9,8},{10,11... | collective-permute-start | bytes 7077896 | tf_op jit(solution)/shard_map/ppermute | solution.py:40
  149.2 28.4 %collective-permute-start.9 = (bf16[2,384,768]{2,1,0:T(8,128)(2,1)S(1)}, bf16[2,384,768]{2,1,0:T(8,128)(2,1)S(1)}, u32[]{:S(2)}, u32[]{:S(2)}) collective-permute-start(bf16[2,384,768]{2,1,0:T(8,128)(2,1)S(1)} %dynamic-slice_bitcast_fusion.1), channel_id=1, source_target_pairs={{0,4},{4,0},{8,12},{12,8},{16,20},{20,16},{24,28},{28,24},{1,5},{5... | collective-permute-start | bytes 3538952 | tf_op jit(solution)/shard_map/ppermute | solution.py:40
  163.2 28.0 %collective-permute-start.8 = (bf16[768,768]{1,0:T(8,128)(2,1)S(1)}, bf16[768,768]{1,0:T(8,128)(2,1)S(1)}, u32[]{:S(2)}, u32[]{:S(2)}) collective-permute-start(bf16[768,768]{1,0:T(8,128)(2,1)S(1)} %get-tuple-element.238), channel_id=1, source_target_pairs={{0,2},{1,3},{2,0},{3,1},{4,6},{5,7},{6,4},{7,5},{8,10},{9,11},{10,... | collective-permute-start | bytes 3538952 | tf_op jit(solution)/shard_map/ppermute | solution.py:40
  193.5 18.7 %collective-permute-start.12 = (bf16[384,768]{1,0:T(8,128)(2,1)S(1)}, bf16[384,768]{1,0:T(8,128)(2,1)S(1)}, u32[]{:S(2)}, u32[]{:S(2)}) collective-permute-start(bf16[384,768]{1,0:T(8,128)(2,1)S(1)} %slice_bitcast_fusion.3), channel_id=1, source_target_pairs={{0,2},{1,3},{2,0},{3,1},{4,6},{5,7},{6,4},{7,5},{8,10},{9,11},{10,... | collective-permute-start | bytes 1769480 | tf_op jit(solution)/shard_map/ppermute | solution.py:40
  194.3 17.9 %collective-permute-start.11 = (bf16[384,768]{1,0:T(8,128)(2,1)S(1)}, bf16[384,768]{1,0:T(8,128)(2,1)S(1)}, u32[]{:S(2)}, u32[]{:S(2)}) collective-permute-start(bf16[384,768]{1,0:T(8,128)(2,1)S(1)} %dynamic-slice_bitcast_fusion.6), channel_id=1, source_target_pairs={{0,4},{4,0},{8,12},{12,8},{16,20},{20,16},{24,28},{28,24},{1,5},{5... | collective-permute-start | bytes 1769480 | tf_op jit(solution)/shard_map/ppermute | solution.py:40
  216.4 22.3 %collective-permute-start.14 = (bf16[2,576,768]{2,1,0:T(8,128)(2,1)S(1)}, bf16[2,576,768]{2,1,0:T(8,128)(2,1)S(1)}, u32[]{:S(2)}, u32[]{:S(2)}) collective-permute-start(bf16[2,576,768]{2,1,0:T(8,128)(2,1)S(1)} %dynamic-slice_bitcast_fusion), channel_id=1, source_target_pairs={{0,1},{1,0},{2,3},{3,2},{4,5},{5,4},{6,7},{7,6},{8,9},{9,8},{10,11... | collective-permute-start | bytes 5308424 | tf_op jit(solution)/shard_map/ppermute | solution.py:40
  216.9 15.8 %collective-permute-start.16 = (bf16[2,192,768]{2,1,0:T(8,128)(2,1)S(1)}, bf16[2,192,768]{2,1,0:T(8,128)(2,1)S(1)}, u32[]{:S(2)}, u32[]{:S(2)}) collective-permute-start(bf16[2,192,768]{2,1,0:T(8,128)(2,1)S(1)} %fusion.11), channel_id=1, source_target_pairs={{0,8},{4,12},{8,0},{12,4},{16,24},{20,28},{24,16},{28,20},{1,9},{5... | collective-permute-start | bytes 1769480 | tf_op jit(solution)/shard_map/ppermute | solution.py:40
  233.4 33.2 %collective-permute-start.21 = (bf16[96,768]{1,0:T(8,128)(2,1)}, bf16[96,768]{1,0:T(8,128)(2,1)}, u32[]{:S(2)}, u32[]{:S(2)}) collective-permute-start(bf16[96,768]{1,0:T(8,128)(2,1)} %fusion.13), channel_id=1, source_target_pairs={{0,8},{4,12},{8,0},{12,4},{16,24},{20,28},{24,16},{28,20},{1,9},{5... | collective-permute-start | bytes 442376 | tf_op jit(solution)/shard_map/ppermute | solution.py:40
  236.1 32.1 %collective-permute-start.20 = (bf16[2,192,768]{2,1,0:T(8,128)(2,1)}, bf16[2,192,768]{2,1,0:T(8,128)(2,1)}, u32[]{:S(2)}, u32[]{:S(2)}) collective-permute-start(bf16[2,192,768]{2,1,0:T(8,128)(2,1)} %fusion.3), channel_id=1, source_target_pairs={{0,16},{4,20},{8,24},{12,28},{16,0},{20,4},{24,8},{28,12},{1,17},{... | collective-permute-start | bytes 1769480 | tf_op jit(solution)/shard_map/ppermute | solution.py:40
  240.4 20.7 %collective-permute-start.15 = (bf16[1,576,768]{2,1,0:T(8,128)(2,1)S(1)}, bf16[1,576,768]{2,1,0:T(8,128)(2,1)S(1)}, u32[]{:S(2)}, u32[]{:S(2)}) collective-permute-start(bf16[1,576,768]{2,1,0:T(8,128)(2,1)S(1)} %constant_dynamic-slice_fusion.4), channel_id=1, source_target_pairs={{0,2},{1,3},{2,0},{3,1},{4,6},{5,7},{6,4},{7,5},{8,10},{9,11},{10,... | collective-permute-start | bytes 2654216 | tf_op jit(solution)/shard_map/ppermute | solution.py:40
  266.7 13.8 %collective-permute-start.18 = (bf16[288,768]{1,0:T(8,128)(2,1)S(1)}, bf16[288,768]{1,0:T(8,128)(2,1)S(1)}, u32[]{:S(2)}, u32[]{:S(2)}) collective-permute-start(bf16[288,768]{1,0:T(8,128)(2,1)S(1)} %dynamic-slice_bitcast_fusion.8), channel_id=1, source_target_pairs={{0,4},{4,0},{8,12},{12,8},{16,20},{20,16},{24,28},{28,24},{1,5},{5... | collective-permute-start | bytes 1327112 | tf_op jit(solution)/shard_map/ppermute | solution.py:40
  268.3 12.7 %collective-permute-start.27 = (f32[80,128]{1,0:T(8,128)S(1)}, f32[80,128]{1,0:T(8,128)S(1)}, u32[]{:S(2)}, u32[]{:S(2)}) collective-permute-start(f32[80,128]{1,0:T(8,128)S(1)} %add_add_fusion.1), channel_id=1, source_target_pairs={{0,4},{4,0},{8,12},{12,8},{16,20},{20,16},{24,28},{28,24},{1,5},{5... | collective-permute-start | bytes 122888 | tf_op jit(solution)/shard_map/ppermute | solution.py:149
  273.2 19.5 %collective-permute-start.25 = (bf16[2,192,768]{2,1,0:T(8,128)(2,1)S(1)}, bf16[2,192,768]{2,1,0:T(8,128)(2,1)S(1)}, u32[]{:S(2)}, u32[]{:S(2)}) collective-permute-start(bf16[2,192,768]{2,1,0:T(8,128)(2,1)S(1)} %add_convert_fusion.3), channel_id=1, source_target_pairs={{0,8},{4,12},{8,0},{12,4},{16,24},{20,28},{24,16},{28,20},{1,9},{5... | collective-permute-start | bytes 1769480 | tf_op jit(solution)/shard_map/ppermute | solution.py:40
  281.0 14.7 %collective-permute-start.19 = (bf16[144,768]{1,0:T(8,128)(2,1)S(1)}, bf16[144,768]{1,0:T(8,128)(2,1)S(1)}, u32[]{:S(2)}, u32[]{:S(2)}) collective-permute-start(bf16[144,768]{1,0:T(8,128)(2,1)S(1)} %dynamic-slice_bitcast_fusion.9), channel_id=1, source_target_pairs={{0,8},{4,12},{8,0},{12,4},{16,24},{20,28},{24,16},{28,20},{1,9},{5... | collective-permute-start | bytes 663560 | tf_op jit(solution)/shard_map/ppermute | solution.py:40
  300.7 30.4 %collective-permute-start.32 = (f32[6,256,256]{2,1,0:T(8,128)}, f32[6,256,256]{2,1,0:T(8,128)}, u32[]{:S(2)}, u32[]{:S(2)}) collective-permute-start(f32[6,256,256]{2,1,0:T(8,128)} %get-tuple-element.192), channel_id=1, source_target_pairs={{0,1},{1,0},{2,3},{3,2},{4,5},{5,4},{6,7},{7,6},{8,9},{9,8},{10,11... | collective-permute-start | bytes 4718600 | tf_op jit(solution)/shard_map/ppermute | solution.py:40
  301.1 30.1 %collective-permute-start.37 = (bf16[2,384,768]{2,1,0:T(8,128)(2,1)S(1)}, bf16[2,384,768]{2,1,0:T(8,128)(2,1)}, u32[]{:S(2)}, u32[]{:S(2)}) collective-permute-start(bf16[2,384,768]{2,1,0:T(8,128)(2,1)S(1)} %pad_maximum_fusion.3.own_ref), channel_id=1, source_target_pairs={{0,4},{4,0},{8,12},{12,8},{16,20},{20,16},{24,28},{28,24},{1,5},{5... | collective-permute-start | bytes 3538952 | tf_op jit(solution)/shard_map/ppermute | solution.py:40
  303.3 27.8 %collective-permute-start.31 = (bf16[144,768]{1,0:T(8,128)(2,1)}, bf16[144,768]{1,0:T(8,128)(2,1)}, u32[]{:S(2)}, u32[]{:S(2)}) collective-permute-start(bf16[144,768]{1,0:T(8,128)(2,1)} %fusion.12), channel_id=1, source_target_pairs={{0,16},{4,20},{8,24},{12,28},{16,0},{20,4},{24,8},{28,12},{1,17},{... | collective-permute-start | bytes 663560 | tf_op jit(solution)/shard_map/ppermute | solution.py:40
  304.7 25.1 %all-to-all-start.1 = ((bf16[8,2,768]{2,1,0:T(2,128)(2,1)}), bf16[8,2,768]{2,1,0:T(2,128)(2,1)}, u32[]{:S(2)}, u32[]{:S(2)}) async-start(bf16[8,2,768]{2,1,0:T(2,128)(2,1)} %reshape.158), calls=%async_computation.1 | async-start | bytes 49152 | tf_op jit(solution)/shard_map/all_to_all | solution.py:1139
  310.6 20.6 %collective-permute-start.33 = (f32[80,128]{1,0:T(8,128)}, f32[80,128]{1,0:T(8,128)}, u32[]{:S(2)}, u32[]{:S(2)}) collective-permute-start(f32[80,128]{1,0:T(8,128)} %add_add_fusion), channel_id=1, source_target_pairs={{0,16},{4,20},{8,24},{12,28},{16,0},{20,4},{24,8},{28,12},{1,17},{... | collective-permute-start | bytes 122888 | tf_op jit(solution)/shard_map/ppermute | solution.py:149
  333.5 19.1 %collective-permute-start.35 = (f32[3,256,256]{2,1,0:T(8,128)S(1)}, f32[3,256,256]{2,1,0:T(8,128)S(1)}, u32[]{:S(2)}, u32[]{:S(2)}) collective-permute-start(f32[3,256,256]{2,1,0:T(8,128)S(1)} %dynamic-slice_bitcast_fusion.5), channel_id=1, source_target_pairs={{0,2},{1,3},{2,0},{3,1},{4,6},{5,7},{6,4},{7,5},{8,10},{9,11},{10,... | collective-permute-start | bytes 2359304 | tf_op jit(solution)/shard_map/ppermute | solution.py:40
  338.9 15.6 %collective-permute-start.38 = (f32[6,256,256]{2,1,0:T(8,128)S(1)}, f32[6,256,256]{2,1,0:T(8,128)S(1)}, u32[]{:S(2)}, u32[]{:S(2)}) collective-permute-start(f32[6,256,256]{2,1,0:T(8,128)S(1)} %get-tuple-element.212), channel_id=1, source_target_pairs={{0,1},{1,0},{2,3},{3,2},{4,5},{5,4},{6,7},{7,6},{8,9},{9,8},{10,11... | collective-permute-start | bytes 4718600 | tf_op jit(solution)/shard_map/ppermute | solution.py:40
  344.1 21.7 %collective-permute-start.41 = (f32[6,256,256]{2,1,0:T(8,128)S(1)}, f32[6,256,256]{2,1,0:T(8,128)S(1)}, u32[]{:S(2)}, u32[]{:S(2)}) collective-permute-start(f32[6,256,256]{2,1,0:T(8,128)S(1)} %get-tuple-element.214), channel_id=1, source_target_pairs={{0,1},{1,0},{2,3},{3,2},{4,5},{5,4},{6,7},{7,6},{8,9},{9,8},{10,11... | collective-permute-start | bytes 4718600 | tf_op jit(solution)/shard_map/ppermute | solution.py:40
  354.8 21.9 %collective-permute-start.39 = (f32[3,256,256]{2,1,0:T(8,128)S(1)}, f32[3,256,256]{2,1,0:T(8,128)S(1)}, u32[]{:S(2)}, u32[]{:S(2)}) collective-permute-start(f32[3,256,256]{2,1,0:T(8,128)S(1)} %dynamic-slice_bitcast_fusion.4), channel_id=1, source_target_pairs={{0,2},{1,3},{2,0},{3,1},{4,6},{5,7},{6,4},{7,5},{8,10},{9,11},{10,... | collective-permute-start | bytes 2359304 | tf_op jit(solution)/shard_map/ppermute | solution.py:40
  377.7 19.5 %collective-permute-start.44 = (f32[3,256,256]{2,1,0:T(8,128)S(1)}, f32[3,256,256]{2,1,0:T(8,128)S(1)}, u32[]{:S(2)}, u32[]{:S(2)}) collective-permute-start(f32[3,256,256]{2,1,0:T(8,128)S(1)} %dynamic-slice_bitcast_fusion.2), channel_id=1, source_target_pairs={{0,2},{1,3},{2,0},{3,1},{4,6},{5,7},{6,4},{7,5},{8,10},{9,11},{10,... | collective-permute-start | bytes 2359304 | tf_op jit(solution)/shard_map/ppermute | solution.py:40
  397.7 20.0 %collective-permute-start.43 = (f32[3,256,256]{2,1,0:T(8,128)S(1)}, f32[3,256,256]{2,1,0:T(8,128)S(1)}, u32[]{:S(2)}, u32[]{:S(2)}) collective-permute-start(f32[3,256,256]{2,1,0:T(8,128)S(1)} %dynamic-slice_bitcast_fusion.3), channel_id=1, source_target_pairs={{0,2},{1,3},{2,0},{3,1},{4,6},{5,7},{6,4},{7,5},{8,10},{9,11},{10,... | collective-permute-start | bytes 2359304 | tf_op jit(solution)/shard_map/ppermute | solution.py:40
  (89 other events, 738.7 us)

commit v3 on v2

--- a/solution.py
+++ b/solution.py
@@ -35,9 +35,17 @@
     return owners_row * capacity + same_before
 
 
+def exchange(value, axis, mask):
+    count = lax.axis_size(axis)
+    return lax.ppermute(value, axis, [(index, index ^ mask) for index in range(count)])
+
+
 def swap(value, axis, bit):
-    count = lax.axis_size(axis)
-    return lax.ppermute(value, axis, [(index, index ^ (1 << bit)) for index in range(count)])
+    return exchange(value, axis, 1 << bit)
+
+
+def step(value, axis, bit):
+    return value, axis, (1 << bit,)
 
 
 def bit_of(axis, bit):
@@ -76,13 +84,14 @@
     def __init__(self, steps):
         self.steps = steps
         self.result = None
-        self.pending = next(steps)
+        self.advance(None)
 
     def advance(self, came):
         try:
-            self.pending = self.steps.send(came)
+            self.sent, axis, masks, *self.held = self.steps.send(came)
+            self.pending = tuple(exchange(self.sent, axis, mask) for mask in masks)
         except StopIteration as stop:
-            self.pending = None
+            self.sent = self.pending = None
             self.result = stop.value
 
 
@@ -90,7 +99,7 @@
     live = [chain for chain in chains if chain.pending is not None]
     cames, also = lax.optimization_barrier((tuple(chain.pending for chain in live), also))
     for chain, came in zip(live, cames):
-        chain.advance(came)
+        chain.advance(came if len(came) > 1 else came[0])
     return also
 
 
@@ -100,30 +109,46 @@
 
 
 def rest_of_dp(value, dim, split):
+    value = yield from rest_summed(value, dim, split)
+    other = yield step(value, "dp", 0)
+    return value, other
+
+
+def rest_summed(value, dim, split):
     first = 1
     split = split and bits_in("dp") > 2
     if split:
         keep, send = halves(value, "dp", 1, dim)
-        value = add_low(keep, (yield swap(send, "dp", 1)))
+        value = add_low(keep, (yield step(send, "dp", 1)))
         first = 2
     for bit in range(first, bits_in("dp")):
-        value = add_low(value, (yield swap(value, "dp", bit)))
+        value = add_low(value, (yield step(value, "dp", bit)))
     if split:
-        value = joined(value, (yield swap(value, "dp", 1)), "dp", 1, dim)
-    other = yield swap(value, "dp", 0)
-    return value, other
+        value = joined(value, (yield step(value, "dp", 1)), "dp", 1, dim)
+    return value
+
+
+def sum_pair(value):
+    value = yield from rest_summed(value, 1, True)
+    role = bit_of("dp", 0)
+    mine = lax.dynamic_index_in_dim(value, role, 0, keepdims=False)
+    theirs = lax.dynamic_index_in_dim(value, 1 - role, 0, keepdims=False)
+    first = yield (*step(theirs, "dp", 0), "first")
+    held = (mine, first)
+    second = yield (*step(tie(mine, first)[0], "dp", 0), held)
+    return value, first, second
 
 
 def sum_up(kept, sent):
-    value = add_low(kept, (yield swap(sent, "ns", 1)))
+    value = add_low(kept, (yield step(sent, "ns", 1)))
     keep, send = halves(value, "dp", 0)
-    return add_low(keep, (yield swap(send, "dp", 0)))
+    return add_low(keep, (yield step(send, "dp", 0)))
 
 
 def sum_down(kept, sent):
     keep, send = halves(jnp.stack([kept, sent]), "dp", 0, 1)
-    value = add_low(keep, (yield swap(send, "dp", 0)))
-    return add_low(value[0], (yield swap(value[1], "ns", 1)))
+    value = add_low(keep, (yield step(send, "dp", 0)))
+    return add_low(value[0], (yield step(value[1], "ns", 1)))
 
 
 def sum_blocks(value, split):
@@ -132,35 +157,32 @@
         pairs = value.reshape(value.shape[0] // 2, 2, *value.shape[1:])
         keep = lax.dynamic_index_in_dim(pairs, mine, 1, keepdims=False)
         send = lax.dynamic_index_in_dim(pairs, 1 - mine, 1, keepdims=False)
-        value = add_low(keep, (yield swap(send, "ns", bit)))
+        value = add_low(keep, (yield step(send, "ns", bit)))
     keep, send = halves(value[0], "dp", 0)
-    value = add_low(keep, (yield swap(send, "dp", 0)))
+    value = add_low(keep, (yield step(send, "dp", 0)))
     return (yield from rest_of_dp(value, 0, split))
 
 
 def sum_vector(value):
     for axis in ("ns", "dp"):
-        count = lax.axis_size(axis)
         for bit in range(0, bits_in(axis), 2):
             masks = [1 << bit]
             if bit + 1 < bits_in(axis):
                 masks += [2 << bit, 3 << bit]
-            came = yield tuple(
-                lax.ppermute(value, axis, [(index, index ^ mask) for index in range(count)])
-                for mask in masks
-            )
-            value = value + came[0]
-            if len(came) == 3:
-                value = value + (came[1] + came[2])
+            came = yield value, axis, masks
+            if len(masks) == 1:
+                value = value + came
+            else:
+                value = (value + came[0]) + (came[1] + came[2])
     return value
 
 
 def sum_gram(gram):
-    gram = gram + (yield swap(gram, "ns", 0))
+    gram = gram + (yield step(gram, "ns", 0))
     keep, _ = halves(gram, "ns", 0)
     for bit in range(1, bits_in("ns")):
-        keep = keep + (yield swap(keep, "ns", bit))
-    other = yield swap(keep, "ns", 0)
+        keep = keep + (yield step(keep, "ns", bit))
+    other = yield step(keep, "ns", 0)
     return (keep[None], 0), (other[None], 0)
 
 
@@ -632,8 +654,8 @@
         out_shape=[shape_of((3, D, slots), LOW), shape_of((3, 1, D // 2), F32),
                    shape_of((1, 256), F32)],
         input_output_aliases={} if earlier is None else {8: 0},
-        compiler_params=params(20),
-        cost_estimate=cost(14, 8e6),
+        compiler_params=params(60),
+        cost_estimate=cost(2.0, 8e6),
         name="attend_back",
     )(counts, qkv, attn, log_total, attn_grad, unit, scale, vectors, *extra)
 
@@ -834,8 +856,8 @@
         out_shape=[shape_of((slots, D), LOW), shape_of((images, D), LOW),
                    shape_of((slots, D), F32), shape_of((D, slots), LOW), shape_of((D, D), LOW),
                    shape_of((8, D), F32)],
-        compiler_params=params(28),
-        cost_estimate=cost(12, 25e6),
+        compiler_params=params(60),
+        cost_estimate=cost(4.0, 25e6),
         name="after",
     )(counts, place, y, x2, dh2, dy, attn, *w_blocks, vectors)
 
@@ -868,7 +890,7 @@
         ),
         out_shape=[shape_of((slots, D), F32), shape_of((8, D), F32)],
         compiler_params=params(22),
-        cost_estimate=cost(10, 17e6),
+        cost_estimate=cost(2.0, 17e6),
         name="first_back",
     )(place, patches, dqkv, *w_blocks, vectors, dx2)
 
@@ -889,6 +911,71 @@
         gram_ref[index] = mm(
             moment_low[:, i * SIDE : (i + 1) * SIDE], moment_low[:, j * SIDE : (j + 1) * SIDE], 0, 0
         )
+
+
+def role_kernel(half_ref, own_ref, other_ref, mom_ref, low_ref, gram_ref):
+    rows = own_ref.shape[0]
+    for ref, place in ((own_ref, half_ref[0]), (other_ref, 1 - half_ref[0])):
+        span = pl.ds(pl.multiple_of(place * rows, rows), rows)
+        low_ref[span, :] = (MUON_DECAY * mom_ref[span, :] + ref[...].astype(F32)).astype(LOW)
+    moment_low = low_ref[...]
+    for index, (i, j) in enumerate(GRID_BLOCKS):
+        gram_ref[index] = mm(
+            moment_low[:, i * SIDE : (i + 1) * SIDE], moment_low[:, j * SIDE : (j + 1) * SIDE], 0, 0
+        )
+
+
+def role_gram(half, own, other, mom):
+    rows = mom.shape[0]
+    blocks = len(GRID_BLOCKS)
+    out_shape = [shape_of((rows, D), LOW), shape_of((blocks, SIDE, SIDE), F32)]
+    return pl.pallas_call(
+        role_kernel,
+        grid=(1,),
+        in_specs=[pl.BlockSpec(memory_space=pltpu.SMEM), once(own.shape), once(other.shape),
+                  once((rows, D))],
+        out_specs=[once(leaf.shape) for leaf in out_shape],
+        out_shape=out_shape,
+        compiler_params=params(16),
+        cost_estimate=cost(0.5, rows * D * 8 + blocks * SIDE * SIDE * 4),
+        name="role_gram",
+    )(half, own, other, mom)
+
+
+def record_kernel(kind, half_ref, own_ref, first_ref, second_ref, mom_ref, grad_ref, moment_ref):
+    rows = own_ref.shape[0]
+
+    def put(ref, place):
+        span = pl.ds(pl.multiple_of(place * rows, rows), rows)
+        grad = ref[...].astype(F32)
+        grad_ref[span, :] = grad
+        moment_ref[span, :] = MUON_DECAY * mom_ref[span, :] + grad
+
+    put(own_ref, half_ref[0])
+
+    @pl.when(half_ref[0] == kind)
+    def _():
+        put(first_ref, 1 - half_ref[0])
+
+    @pl.when(half_ref[0] != kind)
+    def _():
+        put(second_ref, 1 - half_ref[0])
+
+
+def record(kind, half, own, first, second, mom):
+    rows = mom.shape[0]
+    out_shape = [shape_of((rows, D), F32), shape_of((rows, D), F32)]
+    return pl.pallas_call(
+        functools.partial(record_kernel, kind),
+        grid=(1,),
+        in_specs=[pl.BlockSpec(memory_space=pltpu.SMEM), one_of(own, kind), once(first.shape),
+                  once(second.shape), once((rows, D))],
+        out_specs=[once(leaf.shape) for leaf in out_shape],
+        out_shape=out_shape,
+        compiler_params=params(16),
+        cost_estimate=cost(0.5, rows * D * 14),
+        name="record",
+    )(half, own, first, second, mom)
 
 
 def one_of(stack, index):
@@ -913,13 +1000,13 @@
         out_specs=[once(leaf.shape) for leaf in out_shape],
         out_shape=out_shape,
         compiler_params=params(16),
-        cost_estimate=cost(4, rows * D * 14 + blocks * SIDE * SIDE * 4),
+        cost_estimate=cost(0.5, rows * D * 14 + blocks * SIDE * SIDE * 4),
         name="moment",
     )(half, own, other, mom)
 
 
-def muon_kernel(step_scale, half_ref, own_ref, other_ref, moment_ref, master_ref,
-                new_ref, copy_ref, gram_s, low_s, rest_s, mix_s, rows_s, gram_ref):
+def muon_kernel(step_scale, half_ref, own_ref, other_ref, moment_ref, *refs):
+    *refs, gram_s, low_s, rest_s, mix_s, rows_s, gram_ref = refs
     count = own_ref.shape[0]
     for index in range(count):
         gram_ref[half_ref[0] * count + index] = own_ref[index]
@@ -980,29 +1067,37 @@
             gram_s[spans[i], spans[j]] = block
             put((low_s,), i, j, (block.astype(LOW),))
     renewed = NS_A * rows_s[...].astype(F32) + mm(rows_s[...], mix_s[...])
+    if step_scale is None:
+        (ortho_ref,) = refs
+        ortho_ref[...] = renewed.astype(LOW)
+        return
+    master_ref, new_ref, copy_ref = refs
     new = master_ref[...] * (1.0 - MUON_RATE * MUON_SHRINK) - step_scale * renewed
     new_ref[...] = new
     copy_ref[...] = new.astype(LOW)
 
 
-def muon(half, own, other, moment, master, step_scale):
+def muon(half, own, other, moment, master=None, step_scale=None):
     rows = moment.shape[0]
     (own, own_index), (other, other_index) = own, other
     out_shape = [shape_of((rows, D), F32), shape_of((rows, D), LOW)]
+    masters = [master]
+    if master is None:
+        out_shape, masters = out_shape[1:], []
     return pl.pallas_call(
         functools.partial(muon_kernel, step_scale),
         grid=(1,),
         in_specs=[pl.BlockSpec(memory_space=pltpu.SMEM), one_of(own, own_index),
-                  one_of(other, other_index), once((rows, D)), once((rows, D))],
+                  one_of(other, other_index), once((rows, D))] + [once((rows, D))] * len(masters),
         out_specs=[once(leaf.shape) for leaf in out_shape],
         out_shape=out_shape,
         scratch_shapes=[pltpu.VMEM((D, D), F32), pltpu.VMEM((D, D), LOW), pltpu.VMEM((D, D), LOW),
                         pltpu.VMEM((D, D), LOW), pltpu.VMEM((rows, D), LOW),
                         pltpu.VMEM((len(GRID_BLOCKS), SIDE, SIDE), F32)],
         compiler_params=params(30),
-        cost_estimate=cost(18, rows * D * 14),
+        cost_estimate=cost(1.0, rows * D * 14),
         name="muon",
-    )(half, own, other, moment, master)
+    )(half, own, other, moment, *masters)
 
 
 def per_device(
@@ -1050,25 +1145,29 @@
     image_cot = dot32(routing.T, returned).astype(low)
     sizes = counts[0]
     own_pair = jnp.stack([master_up, master_down]).astype(low)
-    far_first, (own_pair, image_cot) = tie(w_first[2], (own_pair, image_cot))
+    role_mom = jnp.where(bit_of("dp", 0) == 0, mom_up, mom_down)
+    far_first, (own_pair, image_cot, role_mom) = tie(w_first[2], (own_pair, image_cot, role_mom))
     w_first = (w_first[0], w_first[1], far_first, swap(far_first, "ns", 0))
     own_pair, _ = tie(own_pair, far_first)
     near_pair, next_pair, far_pair = own_pair, swap(own_pair, "ns", 0), swap(own_pair, "ns", 1)
     first_low, qkv, unit, scale = project(place, patches, w_first, row)
     attn, log_total = attend(sizes, qkv)
-    attn, far_pair = tie(attn, far_pair)
-    pairs = (near_pair, next_pair, far_pair, swap(far_pair, "ns", 0))
     x2, second_low, row_grad, mixed_low = middle(
         sizes, place, patches, attn, w_first, row, patch_cot, image_cot
     )
-    y, second_grad, grad_3, grad_1, bias_3, bias_1 = feed(
-        (3, 1), x2, None, second_low, mixed_low, pairs[3], pairs[1], bias_table, row
-    )
-    came_3, came_1 = swap(grad_3, "ns", 0), swap(grad_1, "ns", 0)
-    y, second_grad, grad_2, grad_0, bias_2, bias_0 = feed(
-        (2, 0), y, second_grad, second_low, mixed_low, pairs[2], pairs[0], bias_table, row
-    )
-    sent, kept = add_low(grad_2, came_3), add_low(grad_0, came_1)
+    y, second_grad, grad_1, grad_0, bias_1, bias_0 = feed(
+        (1, 0), x2, None, second_low, mixed_low, next_pair, near_pair, bias_table, row
+    )
+    came_1 = swap(grad_1, "ns", 0)
+    y, far_pair = tie(y, far_pair)
+    far_next_pair = swap(far_pair, "ns", 0)
+    y, second_grad, grad_3, grad_2, bias_3, bias_2 = feed(
+        (3, 2), y, second_grad, second_low, mixed_low, far_next_pair, far_pair, bias_table, row
+    )
+    came_3 = swap(grad_3, "ns", 0)
+    kept = add_low(grad_0, came_1)
+    came_3, kept = tie(came_3, kept)
+    sent = add_low(grad_2, came_3)
     up, down = Chain(sum_up(kept[0], sent[0])), Chain(sum_down(kept[1], sent[1]))
     y, (sent, kept) = tie(y, (sent, kept))
     out_patches, pooled, middle_grad, attn_grad, grad_out, sums_two = after(
@@ -1084,7 +1183,7 @@
     )
     outgoing = dot32(routing, pooled).astype(low).reshape(dp_count, capacity, D)
     dqkv = meet(up, down, out, also=dqkv.reshape(3 * D, slot_count))
-    pair = Chain(rest_of_dp(jnp.stack([up.result, down.result]), 1, True))
+    pair = Chain(sum_pair(jnp.stack([up.result, down.result])))
     grad_qkv = dot32(dqkv, first_low).astype(low)
     three = Chain(sum_blocks(grad_qkv.reshape(ns_count, -1, D), True))
     meet(three)
@@ -1133,32 +1232,47 @@
     meet(pair, out, vector)
     meet(three)
     meet(pair, out, vector)
-    outgoing = meet(three, out, also=outgoing)
+    meet(three, also=pair.sent)
+    meet(out, vector, also=pair.sent)
     finish(out)
     gram_out = momentum(1, *((half[None], 0) for half in out.result))
+    while pair.held != ["first"]:
+        meet(pair)
+    meet(pair, three, also=gram_out.sent)
+    role_low, gram = role_gram(half_dp, *pair.held[0], role_mom)
+    gram_role = Chain(sum_gram(gram))
+    meet(three, also=gram_role.sent)
+    meet(gram_role, also=three.sent)
+    outgoing = meet(gram_out, pair, also=(gram_role.sent, outgoing))[1]
+    value, first, second = pair.result
+    for kind in (2, 3):
+        grad_parts[kind], moment_parts[kind] = record(
+            kind - 2, half_dp, value, first, second, moments[kind]
+        )
     arrived = lax.all_to_all(outgoing, "dp", split_axis=0, concat_axis=0, tiled=True)
     pooled_rows = arrived.reshape(dp_count * capacity, D)
-    pooled_rows = meet(three, gram_out, vector, also=pooled_rows)
-    finish(vector)
-    finish(pair)
-    gram_up = momentum(2, *((half, 0) for half in pair.result))
-    gram_down = momentum(3, *((half, 1) for half in pair.result))
-    meet(three, gram_out)
-    meet(gram_up)
+    grad_parts[2], grad_parts[3] = meet(three, also=(grad_parts[2], grad_parts[3]))
     finish(three)
     gram_three = momentum(0, *((half[None], 0) for half in three.result))
-    meet(gram_down, gram_out)
+    pooled_rows = meet(gram_role, also=(pooled_rows, gram_three.sent))[0]
+    meet(gram_three, also=gram_role.sent)
+    meet(gram_role, also=gram_three.sent)
+    finish(vector)
+    (ortho,) = muon(half_ns, *gram_role.result, role_low)
+    ortho_came = swap(ortho, "dp", 0)
+    meet(gram_out, also=ortho)
     finish(gram_out)
     iterate(1, gram_out.result)
-    new_masters[1] = meet(gram_up, gram_three, also=new_masters[1])
-    finish(gram_up)
-    iterate(2, gram_up.result)
-    new_masters[2] = meet(gram_down, also=new_masters[2])
-    finish(gram_down)
-    iterate(3, gram_down.result)
-    new_masters[3] = meet(gram_three, also=new_masters[3])
+    new_masters[1] = meet(gram_three, also=new_masters[1])
     finish(gram_three)
     iterate(0, gram_three.result)
+    ortho_came, new_masters[0] = tie(ortho_came, new_masters[0])
+    for kind in (2, 3):
+        rows = moments[kind].shape[0] * ns_count
+        step_scale = MUON_RATE * math.sqrt(max(1.0, rows / D))
+        chosen = jnp.where(bit_of("dp", 0) == kind - 2, ortho, ortho_came).astype(jnp.float32)
+        new_masters[kind] = masters[kind] * (1.0 - MUON_RATE * MUON_SHRINK) - step_scale * chosen
+        copies[kind] = new_masters[kind].astype(low)
     vector_grad = vector.result.reshape(-1)[:vector_size]
     vector_first = BETA_ONE * vec_first + (1.0 - BETA_ONE) * vector_grad
     vector_second = BETA_TWO * vec_second + (1.0 - BETA_TWO) * vector_grad * vector_grad

time: 442 us -> 408 us (0.923)
  waiting for transfers between devices: 133 us -> 102 us
  other arithmetic: 29.1 us -> 39.7 us
  Pallas kernels: 177 us -> 168 us
  local copies, waits for them, and re-layouts: 29.8 us -> 25.2 us
    pallas_call x4 -> x3, Pallas kernels: 54.3 us -> 38.9 us  [muon(): pl.pallas_call(functools.partial(muon_kernel, step_scale), grid=(1,), in_...]
    ppermute x48 -> x47, waiting for transfers between devices: 114 us -> 99.2 us  [exchange(): lax.ppermute(value, axis, [(index, index ^ mask) for index in range(count)])]
    all_to_all x1, waiting for transfers between devices: 16.4 us -> 3.24 us  [per_device(): lax.all_to_all(outgoing, 'dp', split_axis=0, concat_axis=0, tiled=True)]
    pallas_call x0 -> x3, Pallas kernels: none -> 7.8 us  [the longest x2 5.2 us: record(): pl.pallas_call(functools.partial(record_kernel, kind), grid=(1,), in_spec...]
    pallas_call x4 -> x2, Pallas kernels: 11.3 us -> 4.84 us  [moment_and_gram(): pl.pallas_call(moment_kernel, grid=(1,), in_specs=[pl.BlockSpec(memory_sp...]
    unnamed x142 -> x136, local copies, waits for them, and re-layouts: 19.5 us -> 13.4 us
    add x10 -> x8, other arithmetic: 4.75 us -> 9.89 us  [the longest x3 6.93 us: sum_gram(): gram = gram + (yield step(gram, 'ns', 0))]
    pallas_call x2, Pallas kernels: 13.9 us -> 18.4 us  [attend_back(): pl.pallas_call(functools.partial(attend_back_kernel, group), grid_spec=pl...]
  transfers between devices with their start and end apart: 50 -> 49, of which waited for: 23 -> 20; matrix products, arithmetic and copies ran while one was open for 8% -> 9% of each run, Pallas kernels for 33% -> 41%
where the time goes in v3:
time: 408 us; the launch traced here: 400 us
  Pallas kernels  168 us (41%)
  waiting for transfers between devices  102 us (25%)
  starting transfers between devices  55.9 us (14%)
  other arithmetic  39.7 us (10%)
  local copies, waits for them, and re-layouts  25.2 us (6%)
  matrix products  6.88 us (2%)
    ppermute x47, waiting for transfers between devices, exchange(): lax.ppermute(value, axis, [(index, index ^ mask) for index in range(count)])  99.2 us
    ppermute x47, starting transfers between devices, exchange(): lax.ppermute(value, axis, [(index, index ^ mask) for index in range(count)])  45.2 us
    pallas_call x3, Pallas kernels, muon(): pl.pallas_call(functools.partial(muon_kernel, step_scale), grid=(1,), in_...  38.9 us
    pallas_call x2, Pallas kernels, feed(): pl.pallas_call(functools.partial(feed_kernel, distances, start_y), grid=(...  36 us
    pallas_call x1, Pallas kernels, attend(): pl.pallas_call(functools.partial(attend_kernel, group), grid_spec=pltpu.P...  24.1 us
    pallas_call x2, Pallas kernels, attend_back(): pl.pallas_call(functools.partial(attend_back_kernel, group), grid_spec=pl...  18.4 us
    convert_element_type x18, other arithmetic, add_low(): (first.astype(jnp.float32) + second.astype(jnp.float32)).astype(jnp.bfloa...  16 us
    unnamed x136, local copies, waits for them, and re-layouts  13.4 us
  transfers between devices with their start and end apart: 49, of which 20 were waited for; matrix products, arithmetic and copies ran while one was open for 9% of the time, Pallas kernels for 41%

profile of v3, /device:TPU:0, one launch (start us, length us, event | category | flops | bytes accessed | tf_op | source)
XLA Modules:
  0.0 400.3 jit_solution(4458254856732548983)
XLA Ops:
  6.1 5.8 %all-to-all-start = ((bf16[8,2,768]{2,1,0:T(2,128)(2,1)}), bf16[8,2,768]{2,1,0:T(2,128)(2,1)S(1)}, u32[]{:S(2)}, u32[]{:S(2)}) async-start(bf16[8,2,768]{2,1,0:T(2,128)(2,1)} %reshape.145), calls=%async_computation | async-start | bytes 49152 | tf_op jit(solution)/shard_map/all_to_all | solution.py:1138
  19.5 12.0 %collective-permute-done.1.w2 = bf16[768,768]{1,0:T(8,128)(2,1)S(1)} collective-permute-done((bf16[768,768]{1,0:T(8,128)(2,1)S(1)}, bf16[768,768]{1,0:T(8,128)(2,1)S(1)}, u32[]{:S(2)}, u32[]{:S(2)}) %collective-permute-start.1) | collective-permute-done | bytes 1179680 | tf_op jit(solution)/shard_map/ppermute | solution.py:40
  35.9 10.0 %project.1 = (bf16[1024,768]{1,0:T(8,128)(2,1)S(1)}, bf16[3,768,1024]{2,1,0:T(8,128)(2,1)S(1)}, bf16[2,768,1024]{2,1,0:T(8,128)(2,1)S(1)}, f32[2,12,1,1024]{3,2,1,0:T(1,128)S(1)}) custom-call(s32[1]{0:T(128)} %bitcast.1.place_ref, bf16[1024,768]{1,0:T(8,128)(2,1)S(1)} %copy-done.26, bf16[768,768]{1,0:T(8,128)(2,1)S(1)} %pad_maximum_fusion.3.w0, ...), custom_call_target="tpu_custom_call" | custom-call | flops 10000000000 | bytes 16000000 | tf_op jit(solution)/shard_map/project/pallas_call | solution.py:350
  46.0 24.1 %attend.1 = (bf16[768,1024]{1,0:T(8,128)(2,1)S(1)}, f32[12,1,1024]{2,1,0:T(1,128)S(1)}) custom-call(s32[16]{0:T(128)S(1)} %bitcast.144, bf16[3,768,1024]{2,1,0:T(8,128)(2,1)S(1)} %get-tuple-element.133.qkv_ref), custom_call_target="tpu_custom_call" | custom-call | flops 28000000000 | bytes 7000000 | tf_op jit(solution)/shard_map/attend/pallas_call | solution.py:480
  70.7 6.8 %middle.1 = (f32[1024,768]{1,0:T(8,128)S(1)}, bf16[1024,768]{1,0:T(8,128)(2,1)S(1)}, f32[1024,768]{1,0:T(8,128)S(1)}, bf16[1024,768]{1,0:T(8,128)(2,1)S(1)}) custom-call(s32[16]{0:T(128)S(1)} %bitcast.145, s32[1]{0:T(128)} %bitcast.1.place_ref, bf16[1024,768]{1,0:T(8,128)(2,1)S(1)} %copy-done.27, bf16[768,1024]{1,0:T(8,128)(2,1)S(1)} %get-tuple-element.134.attn_ref, ...), custom_call_target="tpu_custom_call" | custom-call | flops 8999999488 | bytes 20000000 | tf_op jit(solution)/shard_map/middle/pallas_call | solution.py:721
  79.2 18.4 %feed.2 = (f32[1024,768]{1,0:T(8,128)S(1)}, f32[1024,768]{1,0:T(8,128)S(1)}, bf16[2,768,768]{2,1,0:T(8,128)(2,1)}, bf16[2,768,768]{2,1,0:T(8,128)(2,1)S(1)}, f32[1,768]{1,0:T(1,128)S(1)}, /*index=5*/f32[1,768]{1,0:T(1,128)S(1)}) custom-call(f32[1024,768]{1,0:T(8,128)S(1)} %get-tuple-element.136.y_in_ref.dh_in_ref.x2_ref, ...), custom_call_target="tpu_custom_call" | custom-call | flops 24000000000 | bytes 25000000 | tf_op jit(solution)/shard_map/feed/pallas_call | solution.py:785
  98.1 5.9 %collective-permute-done.5.up_a.down_a = bf16[2,768,768]{2,1,0:T(8,128)(2,1)S(1)} collective-permute-done((bf16[2,768,768]{2,1,0:T(8,128)(2,1)S(1)}, bf16[2,768,768]{2,1,0:T(8,128)(2,1)S(1)}, u32[]{:S(2)}, u32[]{:S(2)}) %collective-permute-start.5) | collective-permute-done | bytes 2359328 | tf_op jit(solution)/shard_map/ppermute | solution.py:40
  104.0 17.6 %feed.3 = (f32[1024,768]{1,0:T(8,128)S(1)}, f32[1024,768]{1,0:T(8,128)S(1)}, bf16[2,768,768]{2,1,0:T(8,128)(2,1)}, bf16[2,768,768]{2,1,0:T(8,128)(2,1)S(1)}, f32[1,768]{1,0:T(1,128)S(1)}, /*index=5*/f32[1,768]{1,0:T(1,128)S(1)}) custom-call(f32[1024,768]{1,0:T(8,128)S(1)} %get-tuple-element.142.y_in_ref, f32[1024,768]{1,0:T(8,128)S(1)} %get-tuple-element.143.dh_in_ref, ...), custom_call_target="tpu_custom_call" | custom-call | flops 24000000000 | bytes 25000000 | tf_op jit(solution)/shard_map/feed/pallas_call | solution.py:785
  138.6 12.0 %after.1 = (bf16[1024,768]{1,0:T(8,128)(2,1)}, bf16[16,768]{1,0:T(8,128)(2,1)}, f32[1024,768]{1,0:T(8,128)}, bf16[768,1024]{1,0:T(8,128)(2,1)}, bf16[768,768]{1,0:T(8,128)(2,1)}, /*index=5*/f32[8,768]{1,0:T(8,128)}) custom-call(s32[16]{0:T(128)} %bitcast.141, s32[1]{0:T(128)} %bitcast.1.place_ref, f32[1024,768]{1,0:T(8,128)} %copy-done.17, ...), custom_call_target="tpu_custom_call" | custom-call | flops 4000000000 | bytes 25000000 | tf_op jit(solution)/shard_map/after/pallas_call | solution.py:844
  151.8 9.1 %attend_back.2 = (bf16[3,768,1024]{2,1,0:T(8,128)(2,1)}, f32[3,1,384]{2,1,0:T(1,128)}, f32[1,256]{1,0:T(1,128)}) custom-call(s32[16]{0:T(128)} %bitcast.142, bf16[3,768,1024]{2,1,0:T(8,128)(2,1)} %copy-done, bf16[768,1024]{1,0:T(8,128)(2,1)} %copy-done.1, f32[12,1,1024]{2,1,0:T(1,128)} %copy-done.32, bf16[768,1024]{1,0:T(8,128)(2,1)} %get-tuple-element.158.grad_ref, ...), custom_call_target="tpu_custom_call" | custom-call | flops 2000000000 | bytes 8000000 | tf_op jit(solution)/shard_map/attend_back/pallas_call | solution.py:637
  160.9 3.6 collective-permute-done.9
  175.9 9.4 %attend_back.3 = (bf16[3,768,1024]{2,1,0:T(8,128)(2,1)}, f32[3,1,384]{2,1,0:T(1,128)}, f32[1,256]{1,0:T(1,128)}) custom-call(s32[16]{0:T(128)} %bitcast.143, bf16[3,768,1024]{2,1,0:T(8,128)(2,1)} %copy-done, bf16[768,1024]{1,0:T(8,128)(2,1)} %copy-done.1, f32[12,1,1024]{2,1,0:T(1,128)} %copy-done.32, ...), custom_call_target="tpu_custom_call", output_to_operand_aliasing={{0}: (8, {})} | custom-call | flops 2000000000 | bytes 8000000 | tf_op jit(solution)/shard_map/attend_back/pallas_call | solution.py:637
  185.2 4.1 %collective-permute-done.13 = bf16[1,192,768]{2,1,0:T(8,128)(2,1)S(1)} collective-permute-done((bf16[1,192,768]{2,1,0:T(8,128)(2,1)}, bf16[1,192,768]{2,1,0:T(8,128)(2,1)S(1)}, u32[]{:S(2)}, u32[]{:S(2)}) %collective-permute-start.13) | collective-permute-done | bytes 294944 | tf_op jit(solution)/shard_map/ppermute | solution.py:40
  189.4 6.6 %convolution_convert_fusion = bf16[2304,768]{1,0:T(8,128)(2,1)S(1)} fusion(bf16[2304,1024]{1,0:T(8,128)(2,1)} %bitcast.122, bf16[1024,768]{1,0:T(8,128)(2,1)S(1)} %copy-done.38), kind=kOutput, calls=%fused_computation | convolution fusion | flops 3625648128 | bytes 9830400 | tf_op jit(solution)/shard_map/dot_general | solution.py:198
  203.9 3.3 collective-permute-start.14
  210.3 10.1 %collective-permute-done.14 = bf16[2,192,768]{2,1,0:T(8,128)(2,1)S(1)} collective-permute-done((bf16[2,192,768]{2,1,0:T(8,128)(2,1)S(1)}, bf16[2,192,768]{2,1,0:T(8,128)(2,1)S(1)}, u32[]{:S(2)}, u32[]{:S(2)}) %collective-permute-start.14) | collective-permute-done | bytes 589856 | tf_op jit(solution)/shard_map/ppermute | solution.py:40
  225.1 9.2 %first_back.1 = (f32[1024,768]{1,0:T(8,128)}, f32[8,768]{1,0:T(8,128)S(1)}) custom-call(s32[1]{0:T(128)} %bitcast.1.place_ref, bf16[1024,768]{1,0:T(8,128)(2,1)S(1)} %copy-done.28, bf16[2304,1024]{1,0:T(8,128)(2,1)S(1)} %bitcast.125, bf16[768,768]{1,0:T(8,128)(2,1)S(1)} %copy-done.4, bf16[768,768]{1,0:T(8,128)(2,1)} %collective-permute-done.w1, ...), custom_call_target="tpu_custom_call" | custom-call | flops 2000000000 | bytes 17000000 | tf_op jit(solution)/shard_map/first_back/pallas_call | solution.py:881
  239.3 11.3 %collective-permute-done.16 = bf16[2,192,768]{2,1,0:T(8,128)(2,1)S(1)} collective-permute-done((bf16[2,192,768]{2,1,0:T(8,128)(2,1)S(1)}, bf16[2,192,768]{2,1,0:T(8,128)(2,1)S(1)}, u32[]{:S(2)}, u32[]{:S(2)}) %collective-permute-start.16) | collective-permute-done | bytes 589856 | tf_op jit(solution)/shard_map/ppermute | solution.py:40
  255.1 3.4 collective-permute-start.24
  258.9 13.2 %collective-permute-done.24 = bf16[96,768]{1,0:T(8,128)(2,1)S(1)} collective-permute-done((bf16[96,768]{1,0:T(8,128)(2,1)S(1)}, bf16[96,768]{1,0:T(8,128)(2,1)S(1)}, u32[]{:S(2)}, u32[]{:S(2)}) %collective-permute-start.24) | collective-permute-done | bytes 147488 | tf_op jit(solution)/shard_map/ppermute | solution.py:40
  280.4 9.5 %collective-permute-done.33 = f32[80,128]{1,0:T(8,128)S(1)} collective-permute-done((f32[80,128]{1,0:T(8,128)S(1)}, f32[80,128]{1,0:T(8,128)S(1)}, u32[]{:S(2)}, u32[]{:S(2)}) %collective-permute-start.33) | collective-permute-done | bytes 40992 | tf_op jit(solution)/shard_map/ppermute | solution.py:40
  298.3 4.3 %collective-permute-done.35 = bf16[144,768]{1,0:T(8,128)(2,1)S(1)} collective-permute-done((bf16[144,768]{1,0:T(8,128)(2,1)S(1)}, bf16[144,768]{1,0:T(8,128)(2,1)S(1)}, u32[]{:S(2)}, u32[]{:S(2)}) %collective-permute-start.35) | collective-permute-done | bytes 221216 | tf_op jit(solution)/shard_map/ppermute | solution.py:40
  309.9 3.3 collective-permute-done.38.second_ref
  324.6 4.8 %all-to-all-start.1 = ((bf16[8,2,768]{2,1,0:T(2,128)(2,1)}), bf16[8,2,768]{2,1,0:T(2,128)(2,1)S(1)}, u32[]{:S(2)}, u32[]{:S(2)}) async-start(bf16[8,2,768]{2,1,0:T(2,128)(2,1)} %reshape.157), calls=%async_computation.1 | async-start | bytes 49152 | tf_op jit(solution)/shard_map/all_to_all | solution.py:1252
  329.5 3.2 add.227
  332.7 3.2 all-to-all-done.1
  341.6 13.2 %muon.3 = bf16[768,768]{1,0:T(8,128)(2,1)S(1)} custom-call(s32[1]{0:T(128)} %bitcast.49.half_ref, f32[1,3,256,256]{3,2,1,0:T(8,128)S(1)} %bitcast.126, f32[1,3,256,256]{3,2,1,0:T(8,128)S(1)} %bitcast.138, bf16[768,768]{1,0:T(8,128)(2,1)S(1)} %get-tuple-element.229.moment_ref), custom_call_target="tpu_custom_call" | custom-call | flops 1000000000 | bytes 8257536 | tf_op jit(solution)/shard_map/muon/pallas_call | solution.py:1087
  354.8 3.5 collective-permute-done.44
  360.9 11.9 %muon.4 = (f32[192,768]{1,0:T(8,128)}, bf16[192,768]{1,0:T(8,128)(2,1)}) custom-call(s32[1]{0:T(128)} %bitcast.49.half_ref, f32[1,3,256,256]{3,2,1,0:T(8,128)S(1)} %bitcast.137, f32[1,3,256,256]{3,2,1,0:T(8,128)} %bitcast.57.other_ref, f32[192,768]{1,0:T(8,128)S(1)} %copy-done.36, f32[192,768]{1,0:T(8,128)S(1)} %copy-done.30), custom_call_target="tpu_custom_call" | custom-call | flops 1000000000 | bytes 2064384 | tf_op jit(solution)/shard_map/muon/pallas_call | solution.py:1087
  372.9 5.9 %collective-permute-done.43 = f32[3,256,256]{2,1,0:T(8,128)} collective-permute-done((f32[3,256,256]{2,1,0:T(8,128)}, f32[3,256,256]{2,1,0:T(8,128)}, u32[]{:S(2)}, u32[]{:S(2)}) %collective-permute-start.43) | collective-permute-done | bytes 786464 | tf_op jit(solution)/shard_map/ppermute | solution.py:40
  382.4 13.8 %muon.5 = (f32[576,768]{1,0:T(8,128)}, bf16[576,768]{1,0:T(8,128)(2,1)}) custom-call(s32[1]{0:T(128)} %bitcast.49.half_ref, f32[1,3,256,256]{3,2,1,0:T(8,128)S(1)} %bitcast.127, f32[1,3,256,256]{3,2,1,0:T(8,128)S(1)} %bitcast.139, f32[576,768]{1,0:T(8,128)S(1)} %copy-done.23, f32[576,768]{1,0:T(8,128)S(1)} %copy-done.10), custom_call_target="tpu_custom_call" | custom-call | flops 1000000000 | bytes 6193152 | tf_op jit(solution)/shard_map/muon/pallas_call | solution.py:1087
  396.2 3.8 fusion.25
  (298 shorter events, 121.9 us)
Async XLA Ops:
  2.5 29.0 %collective-permute-start.1 = (bf16[768,768]{1,0:T(8,128)(2,1)S(1)}, bf16[768,768]{1,0:T(8,128)(2,1)S(1)}, u32[]{:S(2)}, u32[]{:S(2)}) collective-permute-start(bf16[768,768]{1,0:T(8,128)(2,1)S(1)} %pad_maximum_fusion.3.w0), channel_id=1, source_target_pairs={{0,2},{1,3},{2,0},{3,1},{4,6},{5,7},{6,4},{7,5},{8,10},{9,11},{10,... | collective-permute-start | bytes 3538952 | tf_op jit(solution)/shard_map/ppermute | solution.py:40
  5.5 28.4 %collective-permute-start = (bf16[768,768]{1,0:T(8,128)(2,1)S(1)}, bf16[768,768]{1,0:T(8,128)(2,1)}, u32[]{:S(2)}, u32[]{:S(2)}) collective-permute-start(bf16[768,768]{1,0:T(8,128)(2,1)S(1)} %pad_maximum_fusion.3.w0), channel_id=1, source_target_pairs={{0,1},{1,0},{2,3},{3,2},{4,5},{5,4},{6,7},{7,6},{8,9},{9,8},{10,11... | collective-permute-start | bytes 3538952 | tf_op jit(solution)/shard_map/ppermute | solution.py:40
  31.6 47.6 %collective-permute-start.3 = (bf16[2,768,768]{2,1,0:T(8,128)(2,1)}, bf16[2,768,768]{2,1,0:T(8,128)(2,1)S(1)}, u32[]{:S(2)}, u32[]{:S(2)}) collective-permute-start(bf16[2,768,768]{2,1,0:T(8,128)(2,1)} %pad_maximum_fusion.up_b.down_b), channel_id=1, source_target_pairs={{0,1},{1,0},{2,3},{3,2},{4,5},{5,4},{6,7},{7,6},{8,9},{9,8},{10,11... | collective-permute-start | bytes 7077896 | tf_op jit(solution)/shard_map/ppermute | solution.py:40
  32.2 65.4 %collective-permute-start.4 = (bf16[2,768,768]{2,1,0:T(8,128)(2,1)}, bf16[2,768,768]{2,1,0:T(8,128)(2,1)S(1)}, u32[]{:S(2)}, u32[]{:S(2)}) collective-permute-start(bf16[2,768,768]{2,1,0:T(8,128)(2,1)} %pad_maximum_fusion.up_b.down_b), channel_id=1, source_target_pairs={{0,2},{1,3},{2,0},{3,1},{4,6},{5,7},{6,4},{7,5},{8,10},{9,11},{10,... | collective-permute-start | bytes 7077896 | tf_op jit(solution)/shard_map/ppermute | solution.py:40
  97.7 28.8 %collective-permute-start.7 = (bf16[2,768,768]{2,1,0:T(8,128)(2,1)}, bf16[2,768,768]{2,1,0:T(8,128)(2,1)}, u32[]{:S(2)}, u32[]{:S(2)}) collective-permute-start(bf16[2,768,768]{2,1,0:T(8,128)(2,1)} %get-tuple-element.149), channel_id=1, source_target_pairs={{0,1},{1,0},{2,3},{3,2},{4,5},{5,4},{6,7},{7,6},{8,9},{9,8},{10,11... | collective-permute-start | bytes 7077896 | tf_op jit(solution)/shard_map/ppermute | solution.py:40
  136.1 28.4 %collective-permute-start.9 = (bf16[2,384,768]{2,1,0:T(8,128)(2,1)}, bf16[2,384,768]{2,1,0:T(8,128)(2,1)}, u32[]{:S(2)}, u32[]{:S(2)}) collective-permute-start(bf16[2,384,768]{2,1,0:T(8,128)(2,1)} %dynamic-slice_bitcast_fusion.1), channel_id=1, source_target_pairs={{0,4},{4,0},{8,12},{12,8},{16,20},{20,16},{24,28},{28,24},{1,5},{5... | collective-permute-start | bytes 3538952 | tf_op jit(solution)/shard_map/ppermute | solution.py:40
  137.9 28.0 %collective-permute-start.8 = (bf16[768,768]{1,0:T(8,128)(2,1)}, bf16[768,768]{1,0:T(8,128)(2,1)}, u32[]{:S(2)}, u32[]{:S(2)}) collective-permute-start(bf16[768,768]{1,0:T(8,128)(2,1)} %get-tuple-element.252), channel_id=1, source_target_pairs={{0,2},{1,3},{2,0},{3,1},{4,6},{5,7},{6,4},{7,5},{8,10},{9,11},{10,... | collective-permute-start | bytes 3538952 | tf_op jit(solution)/shard_map/ppermute | solution.py:40
  168.6 20.8 %collective-permute-start.12 = (bf16[384,768]{1,0:T(8,128)(2,1)}, bf16[384,768]{1,0:T(8,128)(2,1)}, u32[]{:S(2)}, u32[]{:S(2)}) collective-permute-start(bf16[384,768]{1,0:T(8,128)(2,1)} %slice_bitcast_fusion.2), channel_id=1, source_target_pairs={{0,2},{1,3},{2,0},{3,1},{4,6},{5,7},{6,4},{7,5},{8,10},{9,11},{10,... | collective-permute-start | bytes 1769480 | tf_op jit(solution)/shard_map/ppermute | solution.py:40
  171.7 17.6 %collective-permute-start.11 = (bf16[384,768]{1,0:T(8,128)(2,1)}, bf16[384,768]{1,0:T(8,128)(2,1)}, u32[]{:S(2)}, u32[]{:S(2)}) collective-permute-start(bf16[384,768]{1,0:T(8,128)(2,1)} %dynamic-slice_bitcast_fusion.5), channel_id=1, source_target_pairs={{0,4},{4,0},{8,12},{12,8},{16,20},{20,16},{24,28},{28,24},{1,5},{5... | collective-permute-start | bytes 1769480 | tf_op jit(solution)/shard_map/ppermute | solution.py:40
  175.8 13.6 %collective-permute-start.13 = (bf16[1,192,768]{2,1,0:T(8,128)(2,1)}, bf16[1,192,768]{2,1,0:T(8,128)(2,1)S(1)}, u32[]{:S(2)}, u32[]{:S(2)}) collective-permute-start(bf16[1,192,768]{2,1,0:T(8,128)(2,1)} %constant_dynamic-slice_fusion.5), channel_id=1, source_target_pairs={{0,2},{1,3},{2,0},{3,1},{4,6},{5,7},{6,4},{7,5},{8,10},{9,11},{10,... | collective-permute-start | bytes 884744 | tf_op jit(solution)/shard_map/ppermute | solution.py:40
  203.9 16.5 %collective-permute-start.14 = (bf16[2,192,768]{2,1,0:T(8,128)(2,1)S(1)}, bf16[2,192,768]{2,1,0:T(8,128)(2,1)S(1)}, u32[]{:S(2)}, u32[]{:S(2)}) collective-permute-start(bf16[2,192,768]{2,1,0:T(8,128)(2,1)S(1)} %fusion.9), channel_id=1, source_target_pairs={{0,8},{4,12},{8,0},{12,4},{16,24},{20,28},{24,16},{28,20},{1,9},{5... | collective-permute-start | bytes 1769480 | tf_op jit(solution)/shard_map/ppermute | solution.py:40
  209.4 24.9 %collective-permute-start.19 = (bf16[1,576,768]{2,1,0:T(8,128)(2,1)S(1)}, bf16[1,576,768]{2,1,0:T(8,128)(2,1)S(1)}, u32[]{:S(2)}, u32[]{:S(2)}) collective-permute-start(bf16[1,576,768]{2,1,0:T(8,128)(2,1)S(1)} %constant_dynamic-slice_fusion.4), channel_id=1, source_target_pairs={{0,2},{1,3},{2,0},{3,1},{4,6},{5,7},{6,4},{7,5},{8,10},{9,11},{10,... | collective-permute-start | bytes 2654216 | tf_op jit(solution)/shard_map/ppermute | solution.py:40
  220.4 18.3 %collective-permute-start.17 = (bf16[96,768]{1,0:T(8,128)(2,1)S(1)}, bf16[96,768]{1,0:T(8,128)(2,1)S(1)}, u32[]{:S(2)}, u32[]{:S(2)}) collective-permute-start(bf16[96,768]{1,0:T(8,128)(2,1)S(1)} %fusion.17), channel_id=1, source_target_pairs={{0,8},{4,12},{8,0},{12,4},{16,24},{20,28},{24,16},{28,20},{1,9},{5... | collective-permute-start | bytes 442376 | tf_op jit(solution)/shard_map/ppermute | solution.py:40
  222.4 28.2 %collective-permute-start.16 = (bf16[2,192,768]{2,1,0:T(8,128)(2,1)S(1)}, bf16[2,192,768]{2,1,0:T(8,128)(2,1)S(1)}, u32[]{:S(2)}, u32[]{:S(2)}) collective-permute-start(bf16[2,192,768]{2,1,0:T(8,128)(2,1)S(1)} %fusion.3), channel_id=1, source_target_pairs={{0,16},{4,20},{8,24},{12,28},{16,0},{20,4},{24,8},{28,12},{1,17},{... | collective-permute-start | bytes 1769480 | tf_op jit(solution)/shard_map/ppermute | solution.py:40
  235.4 15.2 %collective-permute-start.20 = (f32[80,128]{1,0:T(8,128)S(1)}, f32[80,128]{1,0:T(8,128)S(1)}, u32[]{:S(2)}, u32[]{:S(2)}) collective-permute-start(f32[80,128]{1,0:T(8,128)S(1)} %bitcast.171), channel_id=1, source_target_pairs={{0,1},{1,0},{2,3},{3,2},{4,5},{5,4},{6,7},{7,6},{8,9},{9,8},{10,11... | collective-permute-start | bytes 122888 | tf_op jit(solution)/shard_map/ppermute | solution.py:40
  235.5 15.2 %collective-permute-start.21 = (f32[80,128]{1,0:T(8,128)S(1)}, f32[80,128]{1,0:T(8,128)S(1)}, u32[]{:S(2)}, u32[]{:S(2)}) collective-permute-start(f32[80,128]{1,0:T(8,128)S(1)} %bitcast.172), channel_id=1, source_target_pairs={{0,2},{1,3},{2,0},{3,1},{4,6},{5,7},{6,4},{7,5},{8,10},{9,11},{10,... | collective-permute-start | bytes 122888 | tf_op jit(solution)/shard_map/ppermute | solution.py:40
  235.8 14.9 %collective-permute-start.22 = (f32[80,128]{1,0:T(8,128)S(1)}, f32[80,128]{1,0:T(8,128)S(1)}, u32[]{:S(2)}, u32[]{:S(2)}) collective-permute-start(f32[80,128]{1,0:T(8,128)S(1)} %bitcast.173), channel_id=1, source_target_pairs={{0,3},{1,2},{2,1},{3,0},{4,7},{5,6},{6,5},{7,4},{8,11},{9,10},{10,... | collective-permute-start | bytes 122888 | tf_op jit(solution)/shard_map/ppermute | solution.py:40
  238.8 16.3 %collective-permute-start.29 = (bf16[288,768]{1,0:T(8,128)(2,1)S(1)}, bf16[288,768]{1,0:T(8,128)(2,1)S(1)}, u32[]{:S(2)}, u32[]{:S(2)}) collective-permute-start(bf16[288,768]{1,0:T(8,128)(2,1)S(1)} %dynamic-slice_bitcast_fusion.7), channel_id=1, source_target_pairs={{0,4},{4,0},{8,12},{12,8},{16,20},{20,16},{24,28},{28,24},{1,5},{5... | collective-permute-start | bytes 1327112 | tf_op jit(solution)/shard_map/ppermute | solution.py:40
  254.4 19.5 %collective-permute-start.23 = (bf16[2,192,768]{2,1,0:T(8,128)(2,1)S(1)}, bf16[2,192,768]{2,1,0:T(8,128)(2,1)S(1)}, u32[]{:S(2)}, u32[]{:S(2)}) collective-permute-start(bf16[2,192,768]{2,1,0:T(8,128)(2,1)S(1)} %add_convert_fusion.3), channel_id=1, source_target_pairs={{0,8},{4,12},{8,0},{12,4},{16,24},{20,28},{24,16},{28,20},{1,9},{5... | collective-permute-start | bytes 1769480 | tf_op jit(solution)/shard_map/ppermute | solution.py:40
  255.1 16.9 %collective-permute-start.24 = (bf16[96,768]{1,0:T(8,128)(2,1)S(1)}, bf16[96,768]{1,0:T(8,128)(2,1)S(1)}, u32[]{:S(2)}, u32[]{:S(2)}) collective-permute-start(bf16[96,768]{1,0:T(8,128)(2,1)S(1)} %add_convert_fusion.7), channel_id=1, source_target_pairs={{0,16},{4,20},{8,24},{12,28},{16,0},{20,4},{24,8},{28,12},{1,17},{... | collective-permute-start | bytes 442376 | tf_op jit(solution)/shard_map/ppermute | solution.py:40
  258.8 18.5 %collective-permute-start.30 = (bf16[144,768]{1,0:T(8,128)(2,1)S(1)}, bf16[144,768]{1,0:T(8,128)(2,1)S(1)}, u32[]{:S(2)}, u32[]{:S(2)}) collective-permute-start(bf16[144,768]{1,0:T(8,128)(2,1)S(1)} %dynamic-slice_bitcast_fusion.8), channel_id=1, source_target_pairs={{0,8},{4,12},{8,0},{12,4},{16,24},{20,28},{24,16},{28,20},{1,9},{5... | collective-permute-start | bytes 663560 | tf_op jit(solution)/shard_map/ppermute | solution.py:40
  275.1 16.5 %collective-permute-start.28 = (bf16[384,768]{1,0:T(8,128)(2,1)S(1)}, bf16[384,768]{1,0:T(8,128)(2,1)S(1)}, u32[]{:S(2)}, u32[]{:S(2)}) collective-permute-start(bf16[384,768]{1,0:T(8,128)(2,1)S(1)} %get-tuple-element.253), channel_id=1, source_target_pairs={{0,4},{4,0},{8,12},{12,8},{16,20},{20,16},{24,28},{28,24},{1,5},{5... | collective-permute-start | bytes 1769480 | tf_op jit(solution)/shard_map/ppermute | solution.py:40
  275.7 14.2 %collective-permute-start.32 = (bf16[96,768]{1,0:T(8,128)(2,1)S(1)}, bf16[96,768]{1,0:T(8,128)(2,1)S(1)}, u32[]{:S(2)}, u32[]{:S(2)}) collective-permute-start(bf16[96,768]{1,0:T(8,128)(2,1)S(1)} %add_convert_fusion.6), channel_id=1, source_target_pairs={{0,4},{4,0},{8,12},{12,8},{16,20},{20,16},{24,28},{28,24},{1,5},{5... | collective-permute-start | bytes 442376 | tf_op jit(solution)/shard_map/ppermute | solution.py:40
  277.3 14.2 %collective-permute-start.31 = (bf16[144,768]{1,0:T(8,128)(2,1)S(1)}, bf16[144,768]{1,0:T(8,128)(2,1)S(1)}, u32[]{:S(2)}, u32[]{:S(2)}) collective-permute-start(bf16[144,768]{1,0:T(8,128)(2,1)S(1)} %fusion.16), channel_id=1, source_target_pairs={{0,16},{4,20},{8,24},{12,28},{16,0},{20,4},{24,8},{28,12},{1,17},{... | collective-permute-start | bytes 663560 | tf_op jit(solution)/shard_map/ppermute | solution.py:40
  294.2 19.0 %collective-permute-start.37 = (f32[6,256,256]{2,1,0:T(8,128)}, f32[6,256,256]{2,1,0:T(8,128)}, u32[]{:S(2)}, u32[]{:S(2)}) collective-permute-start(f32[6,256,256]{2,1,0:T(8,128)} %get-tuple-element.201), channel_id=1, source_target_pairs={{0,1},{1,0},{2,3},{3,2},{4,5},{5,4},{6,7},{7,6},{8,9},{9,8},{10,11... | collective-permute-start | bytes 4718600 | tf_op jit(solution)/shard_map/ppermute | solution.py:40
  296.9 16.2 %collective-permute-start.38 = (bf16[384,768]{1,0:T(8,128)(2,1)S(1)}, bf16[384,768]{1,0:T(8,128)(2,1)S(1)}, u32[]{:S(2)}, u32[]{:S(2)}) collective-permute-start(bf16[384,768]{1,0:T(8,128)(2,1)S(1)} %get-tuple-element.208.own_ref), channel_id=1, source_target_pairs={{0,4},{4,0},{8,12},{12,8},{16,20},{20,16},{24,28},{28,24},{1,5},{5... | collective-permute-start | bytes 1769480 | tf_op jit(solution)/shard_map/ppermute | solution.py:40
  303.4 18.1 %collective-permute-start.39 = (bf16[288,768]{1,0:T(8,128)(2,1)}, bf16[288,768]{1,0:T(8,128)(2,1)}, u32[]{:S(2)}, u32[]{:S(2)}) collective-permute-start(bf16[288,768]{1,0:T(8,128)(2,1)} %get-tuple-element.258), channel_id=1, source_target_pairs={{0,4},{4,0},{8,12},{12,8},{16,20},{20,16},{24,28},{28,24},{1,5},{5... | collective-permute-start | bytes 1327112 | tf_op jit(solution)/shard_map/ppermute | solution.py:40
  309.0 27.6 %collective-permute-start.36 = (f32[3,256,256]{2,1,0:T(8,128)}, f32[3,256,256]{2,1,0:T(8,128)}, u32[]{:S(2)}, u32[]{:S(2)}) collective-permute-start(f32[3,256,256]{2,1,0:T(8,128)} %dynamic-slice_bitcast_fusion.4), channel_id=1, source_target_pairs={{0,2},{1,3},{2,0},{3,1},{4,6},{5,7},{6,4},{7,5},{8,10},{9,11},{10,... | collective-permute-start | bytes 2359304 | tf_op jit(solution)/shard_map/ppermute | solution.py:40
  324.6 14.0 %collective-permute-start.41 = (f32[6,256,256]{2,1,0:T(8,128)S(1)}, f32[6,256,256]{2,1,0:T(8,128)}, u32[]{:S(2)}, u32[]{:S(2)}) collective-permute-start(f32[6,256,256]{2,1,0:T(8,128)S(1)} %get-tuple-element.215), channel_id=1, source_target_pairs={{0,1},{1,0},{2,3},{3,2},{4,5},{5,4},{6,7},{7,6},{8,9},{9,8},{10,11... | collective-permute-start | bytes 4718600 | tf_op jit(solution)/shard_map/ppermute | solution.py:40
  338.5 19.8 %collective-permute-start.44 = (f32[3,256,256]{2,1,0:T(8,128)S(1)}, f32[3,256,256]{2,1,0:T(8,128)S(1)}, u32[]{:S(2)}, u32[]{:S(2)}) collective-permute-start(f32[3,256,256]{2,1,0:T(8,128)S(1)} %dynamic-slice_bitcast_fusion.2), channel_id=1, source_target_pairs={{0,2},{1,3},{2,0},{3,1},{4,6},{5,7},{6,4},{7,5},{8,10},{9,11},{10,... | collective-permute-start | bytes 2359304 | tf_op jit(solution)/shard_map/ppermute | solution.py:40
  358.5 20.3 %collective-permute-start.43 = (f32[3,256,256]{2,1,0:T(8,128)}, f32[3,256,256]{2,1,0:T(8,128)}, u32[]{:S(2)}, u32[]{:S(2)}) collective-permute-start(f32[3,256,256]{2,1,0:T(8,128)} %dynamic-slice_bitcast_fusion.3), channel_id=1, source_target_pairs={{0,2},{1,3},{2,0},{3,1},{4,6},{5,7},{6,4},{7,5},{8,10},{9,11},{10,... | collective-permute-start | bytes 2359304 | tf_op jit(solution)/shard_map/ppermute | solution.py:40
  358.9 37.3 %collective-permute-start.42 = (bf16[768,768]{1,0:T(8,128)(2,1)S(1)}, bf16[768,768]{1,0:T(8,128)(2,1)S(1)}, u32[]{:S(2)}, u32[]{:S(2)}) collective-permute-start(bf16[768,768]{1,0:T(8,128)(2,1)S(1)} %muon.3), channel_id=1, source_target_pairs={{0,4},{4,0},{8,12},{12,8},{16,20},{20,16},{24,28},{28,24},{1,5},{5... | collective-permute-start | bytes 3538952 | tf_op jit(solution)/shard_map/ppermute | solution.py:40
  (85 other events, 849.1 us)

commit v4 on v3

--- a/solution.py
+++ b/solution.py
@@ -128,15 +128,13 @@
     return value
 
 
-def sum_pair(value):
-    value = yield from rest_summed(value, 1, True)
-    role = bit_of("dp", 0)
-    mine = lax.dynamic_index_in_dim(value, role, 0, keepdims=False)
-    theirs = lax.dynamic_index_in_dim(value, 1 - role, 0, keepdims=False)
+def swap_roles(up, down):
+    first_role = bit_of("dp", 0) == 0
+    mine, theirs = jnp.where(first_role, up, down), jnp.where(first_role, down, up)
     first = yield (*step(theirs, "dp", 0), "first")
     held = (mine, first)
     second = yield (*step(tie(mine, first)[0], "dp", 0), held)
-    return value, first, second
+    return first, second
 
 
 def sum_up(kept, sent):
@@ -475,7 +473,7 @@
             lax.fori_loop(first // 256, slots // 256, columns, 0)
 
 
-def attend(counts, qkv, group=2):
+def attend(counts, qkv, group=6):
     slots = qkv.shape[2]
     return pl.pallas_call(
         functools.partial(attend_kernel, group),
@@ -494,7 +492,8 @@
 
 
 def attend_back_kernel(group, counts_ref, qkv_ref, attn_ref, log_ref, grad_ref, unit_ref,
-                       scale_ref, vec_ref, _, dqkv_ref, bias_ref, gains_ref, dq_s, dk_s, dv_s):
+                       scale_ref, vec_ref, h_ref, *refs):
+    dqkv_ref, bias_ref, gains_ref, grad_w_ref, dq_s, dk_s, dv_s = refs[-7:]
     used = used_slots(counts_ref)
     has_big = counts_ref[0] == BIG
     slots = attn_ref.shape[1]
@@ -619,13 +618,14 @@
         dqkv_ref[2, rows, :] = result
         biases[2].append(jnp.sum(result.astype(F32), axis=1, keepdims=True))
     for part in range(3):
+        grad_w_ref[part] = mm(dqkv_ref[part], h_ref[...]).astype(LOW)
         bias_ref[part] = to_row(jnp.concatenate(biases[part], axis=0))
     blank = jnp.zeros((HD, 1), F32)
     gains_ref[:, 0:128] += to_row(jnp.concatenate(sums[:2], axis=0))
     gains_ref[:, 128:256] += to_row(jnp.concatenate([sums[2], blank], axis=0))
 
 
-def attend_back(counts, qkv, attn, log_total, attn_grad, unit, scale, vectors, earlier, half,
+def attend_back(counts, qkv, attn, log_total, attn_grad, unit, scale, vectors, h, earlier, half,
                 group=2):
     slots = qkv.shape[2]
     steps = HEADS // group // 2
@@ -633,7 +633,7 @@
     head_block = pl.BlockSpec((group * HD, slots), lambda h, c: (h + first, 0))
     dqkv_block = pl.BlockSpec((3, group * HD, slots), lambda h, c: (0, h + first, 0))
     held = pl.BlockSpec(memory_space=pl.ANY)
-    extra = [vectors if earlier is None else earlier]
+    grad_block = pl.BlockSpec((3, group * HD, D), lambda h, c: (0, h + first, 0))
     return pl.pallas_call(
         functools.partial(attend_back_kernel, group),
         grid_spec=pltpu.PrefetchScalarGridSpec(
@@ -645,19 +645,19 @@
                       head_block,
                       pl.BlockSpec((2, group * HD, slots), lambda h, c: (0, h + first, 0)),
                       pl.BlockSpec((2, group, 1, slots), lambda h, c: (0, h + first, 0, 0)),
-                      whole(vectors.shape), held],
+                      whole(vectors.shape), once(h.shape)] + [held] * len(earlier),
             out_specs=[dqkv_block,
                        pl.BlockSpec((3, 1, group * HD), lambda h, c: (0, 0, h)),
-                       whole((1, 256))],
+                       whole((1, 256)), grad_block],
             scratch_shapes=[pltpu.VMEM((group * HD, slots), F32)] * 3,
         ),
         out_shape=[shape_of((3, D, slots), LOW), shape_of((3, 1, D // 2), F32),
-                   shape_of((1, 256), F32)],
-        input_output_aliases={} if earlier is None else {8: 0},
+                   shape_of((1, 256), F32), shape_of((3, D, D), LOW)],
+        input_output_aliases={9: 0, 10: 3} if earlier else {},
         compiler_params=params(60),
         cost_estimate=cost(2.0, 8e6),
         name="attend_back",
-    )(counts, qkv, attn, log_total, attn_grad, unit, scale, vectors, *extra)
+    )(counts, qkv, attn, log_total, attn_grad, unit, scale, vectors, h, *earlier)
 
 
 def segment_picker(counts_ref, first, width):
@@ -890,7 +890,7 @@
         ),
         out_shape=[shape_of((slots, D), F32), shape_of((8, D), F32)],
         compiler_params=params(22),
-        cost_estimate=cost(2.0, 17e6),
+        cost_estimate=cost(0.2, 17e6),
         name="first_back",
     )(place, patches, dqkv, *w_blocks, vectors, dx2)
 
@@ -968,7 +968,7 @@
     return pl.pallas_call(
         functools.partial(record_kernel, kind),
         grid=(1,),
-        in_specs=[pl.BlockSpec(memory_space=pltpu.SMEM), one_of(own, kind), once(first.shape),
+        in_specs=[pl.BlockSpec(memory_space=pltpu.SMEM), once(own.shape), once(first.shape),
                   once(second.shape), once((rows, D))],
         out_specs=[once(leaf.shape) for leaf in out_shape],
         out_shape=out_shape,
@@ -1174,20 +1174,21 @@
         sizes, place, y, x2, second_grad, row_grad, attn, w_first, row
     )
     out = Chain(sum_blocks(grad_out.reshape(ns_count, -1, D), False))
-    dqkv, bias_a, gains_a = attend_back(
-        sizes, qkv, attn, log_total, attn_grad, unit, scale, row, None, 0
-    )
-    dqkv = meet(up, down, out, also=dqkv)
-    dqkv, bias_b, gains_b = attend_back(
-        sizes, qkv, attn, log_total, attn_grad, unit, scale, row, dqkv, 1
+    dqkv, bias_a, gains_a, grad_qkv = attend_back(
+        sizes, qkv, attn, log_total, attn_grad, unit, scale, row, first_low, (), 0
+    )
+    earlier = meet(up, down, out, also=(dqkv, grad_qkv))
+    dqkv, bias_b, gains_b, grad_qkv = attend_back(
+        sizes, qkv, attn, log_total, attn_grad, unit, scale, row, first_low, earlier, 1
     )
     outgoing = dot32(routing, pooled).astype(low).reshape(dp_count, capacity, D)
-    dqkv = meet(up, down, out, also=dqkv.reshape(3 * D, slot_count))
-    pair = Chain(sum_pair(jnp.stack([up.result, down.result])))
-    grad_qkv = dot32(dqkv, first_low).astype(low)
+    dqkv, grad_qkv = meet(up, down, out, also=(dqkv.reshape(3 * D, slot_count), grad_qkv))
+    up = Chain(rest_summed(up.result, 0, True))
+    down = Chain(rest_summed(down.result, 0, True))
     three = Chain(sum_blocks(grad_qkv.reshape(ns_count, -1, D), True))
     meet(three)
-    middle_grad = meet(pair, out, also=middle_grad)
+    meet(up, also=three.sent)
+    middle_grad = meet(down, out, also=(middle_grad, up.sent))[0]
     patch_grad, sums_one = first_back(place, patches, dqkv, w_first, row, middle_grad)
     sums_one, patch_grad = meet(three, also=(sums_one, patch_grad))
     gains = gains_a + gains_b
@@ -1229,41 +1230,46 @@
             half_ns, *halves_of_gram, moment_parts[kind], masters[kind], step_scale
         )
 
-    meet(pair, out, vector)
-    meet(three)
-    meet(pair, out, vector)
-    meet(three, also=pair.sent)
+    outgoing = meet(up, out, vector, also=outgoing)
+    meet(three, also=up.sent)
+    meet(down, also=three.sent)
+    arrived = lax.all_to_all(outgoing, "dp", split_axis=0, concat_axis=0, tiled=True)
+    pooled_rows = arrived.reshape(dp_count * capacity, D)
+    finish(up)
+    pooled_rows = meet(down, out, vector, also=(pooled_rows, up.result))[0]
+    finish(down)
+    pair = Chain(swap_roles(up.result, down.result))
     meet(out, vector, also=pair.sent)
     finish(out)
     gram_out = momentum(1, *((half[None], 0) for half in out.result))
+    meet(gram_out)
+    meet(three, also=(pair.sent, gram_out.sent))
     while pair.held != ["first"]:
         meet(pair)
-    meet(pair, three, also=gram_out.sent)
+    meet(pair, three, gram_out)
     role_low, gram = role_gram(half_dp, *pair.held[0], role_mom)
     gram_role = Chain(sum_gram(gram))
+    meet(gram_role, three, gram_out)
+    gram_own = tie(gram_out.result[0][0], (three.sent, gram_role.sent))[0]
+    iterate(1, ((gram_own, 0), gram_out.result[1]))
+    meet(pair, also=(gram_role.sent, new_masters[1]))
+    first, second = pair.result
+    for kind, own in ((2, up.result), (3, down.result)):
+        grad_parts[kind], moment_parts[kind] = record(
+            kind - 2, half_dp, own, first, second, moments[kind]
+        )
+    new_masters[1], grad_parts[2], grad_parts[3] = meet(
+        gram_role, also=(new_masters[1], grad_parts[2], grad_parts[3])
+    )
     meet(three, also=gram_role.sent)
-    meet(gram_role, also=three.sent)
-    outgoing = meet(gram_out, pair, also=(gram_role.sent, outgoing))[1]
-    value, first, second = pair.result
-    for kind in (2, 3):
-        grad_parts[kind], moment_parts[kind] = record(
-            kind - 2, half_dp, value, first, second, moments[kind]
-        )
-    arrived = lax.all_to_all(outgoing, "dp", split_axis=0, concat_axis=0, tiled=True)
-    pooled_rows = arrived.reshape(dp_count * capacity, D)
-    grad_parts[2], grad_parts[3] = meet(three, also=(grad_parts[2], grad_parts[3]))
     finish(three)
     gram_three = momentum(0, *((half[None], 0) for half in three.result))
-    pooled_rows = meet(gram_role, also=(pooled_rows, gram_three.sent))[0]
     meet(gram_three, also=gram_role.sent)
     meet(gram_role, also=gram_three.sent)
     finish(vector)
     (ortho,) = muon(half_ns, *gram_role.result, role_low)
     ortho_came = swap(ortho, "dp", 0)
-    meet(gram_out, also=ortho)
-    finish(gram_out)
-    iterate(1, gram_out.result)
-    new_masters[1] = meet(gram_three, also=new_masters[1])
+    meet(gram_three, also=ortho)
     finish(gram_three)
     iterate(0, gram_three.result)
     ortho_came, new_masters[0] = tie(ortho_came, new_masters[0])

time: 408 us -> 386 us (0.946)
  starting transfers between devices: 55.9 us -> 69 us
  Pallas kernels: 168 us -> 160 us
  waiting for transfers between devices: 102 us -> 94.3 us
  matrix products: 6.88 us -> 0.32 us
  other arithmetic: 39.7 us -> 33.4 us
    ppermute x47 -> x50, starting transfers between devices: 45.2 us -> 58.5 us  [exchange(): lax.ppermute(value, axis, [(index, index ^ mask) for index in range(count)])]
    ppermute x47 -> x50, waiting for transfers between devices: 99.2 us -> 86.1 us  [exchange(): lax.ppermute(value, axis, [(index, index ^ mask) for index in range(count)])]
    pallas_call x1, Pallas kernels: 24.1 us -> 16.8 us  [attend(): pl.pallas_call(functools.partial(attend_kernel, group), grid_spec=pltpu.P...]
    dot_general x3 -> x2, matrix products: 6.88 us -> 0.32 us  [dot32(): return jnp.dot(first, second, preferred_element_type=jnp.float32)]
    add x3, other arithmetic: 6.93 us -> 0.62 us  [sum_gram(): gram = gram + (yield step(gram, 'ns', 0))]
    all_to_all x1, waiting for transfers between devices: 3.24 us -> 8.22 us  [per_device(): lax.all_to_all(outgoing, 'dp', split_axis=0, concat_axis=0, tiled=True)]
    convert_element_type x18 -> x20, other arithmetic: 16 us -> 18.2 us  [add_low(): (first.astype(jnp.float32) + second.astype(jnp.float32)).astype(jnp.bfloa...]
    unnamed x136 -> x120, local copies, waits for them, and re-layouts: 13.4 us -> 11.8 us
  transfers between devices with their start and end apart: 49 -> 52, of which waited for: 20 -> 26; matrix products, arithmetic and copies ran while one was open for 9% -> 8% of each run, Pallas kernels for 41% -> 41%
where the time goes in v4:
time: 386 us; the launch traced here: 382 us
  Pallas kernels  160 us (41%)
  waiting for transfers between devices  94.3 us (24%)
  starting transfers between devices  69 us (18%)
  other arithmetic  33.4 us (9%)
  local copies, waits for them, and re-layouts  23.3 us (6%)
    ppermute x50, waiting for transfers between devices, exchange(): lax.ppermute(value, axis, [(index, index ^ mask) for index in range(count)])  86.1 us
    ppermute x50, starting transfers between devices, exchange(): lax.ppermute(value, axis, [(index, index ^ mask) for index in range(count)])  58.5 us
    pallas_call x3, Pallas kernels, muon(): pl.pallas_call(functools.partial(muon_kernel, step_scale), grid=(1,), in_...  37.4 us
    pallas_call x2, Pallas kernels, feed(): pl.pallas_call(functools.partial(feed_kernel, distances, start_y), grid=(...  36 us
    pallas_call x2, Pallas kernels, attend_back(): pl.pallas_call(functools.partial(attend_back_kernel, group), grid_spec=pl...  22.3 us
    convert_element_type x20, other arithmetic, add_low(): (first.astype(jnp.float32) + second.astype(jnp.float32)).astype(jnp.bfloa...  18.2 us
    pallas_call x1, Pallas kernels, attend(): pl.pallas_call(functools.partial(attend_kernel, group), grid_spec=pltpu.P...  16.8 us
    pallas_call x1, Pallas kernels, after(): pl.pallas_call(after_kernel, grid_spec=pltpu.PrefetchScalarGridSpec(num_s...  12 us
  transfers between devices with their start and end apart: 52, of which 26 were waited for; matrix products, arithmetic and copies ran while one was open for 8% of the time, Pallas kernels for 41%

profile of v4, /device:TPU:0, one launch (start us, length us, event | category | flops | bytes accessed | tf_op | source)
XLA Modules:
  0.0 382.2 jit_solution(2562040356542233231)
XLA Ops:
  6.1 5.8 %all-to-all-start = ((bf16[8,2,768]{2,1,0:T(2,128)(2,1)}), bf16[8,2,768]{2,1,0:T(2,128)(2,1)S(1)}, u32[]{:S(2)}, u32[]{:S(2)}) async-start(bf16[8,2,768]{2,1,0:T(2,128)(2,1)} %reshape.148), calls=%async_computation | async-start | bytes 49152 | tf_op jit(solution)/shard_map/all_to_all | solution.py:1138
  19.5 12.0 %collective-permute-done.1.w2 = bf16[768,768]{1,0:T(8,128)(2,1)S(1)} collective-permute-done((bf16[768,768]{1,0:T(8,128)(2,1)S(1)}, bf16[768,768]{1,0:T(8,128)(2,1)S(1)}, u32[]{:S(2)}, u32[]{:S(2)}) %collective-permute-start.1) | collective-permute-done | bytes 1179680 | tf_op jit(solution)/shard_map/ppermute | solution.py:40
  35.9 10.0 %project.1 = (bf16[1024,768]{1,0:T(8,128)(2,1)S(1)}, bf16[3,768,1024]{2,1,0:T(8,128)(2,1)S(1)}, bf16[2,768,1024]{2,1,0:T(8,128)(2,1)S(1)}, f32[2,12,1,1024]{3,2,1,0:T(1,128)S(1)}) custom-call(s32[1]{0:T(128)} %bitcast.1.place_ref, bf16[1024,768]{1,0:T(8,128)(2,1)S(1)} %copy-done.25, bf16[768,768]{1,0:T(8,128)(2,1)S(1)} %pad_maximum_fusion.2.w0, ...), custom_call_target="tpu_custom_call" | custom-call | flops 10000000000 | bytes 16000000 | tf_op jit(solution)/shard_map/project/pallas_call | solution.py:348
  46.0 16.8 %attend.1 = (bf16[768,1024]{1,0:T(8,128)(2,1)S(1)}, f32[12,1,1024]{2,1,0:T(1,128)S(1)}) custom-call(s32[16]{0:T(128)S(1)} %bitcast.140, bf16[3,768,1024]{2,1,0:T(8,128)(2,1)S(1)} %get-tuple-element.141.qkv_ref), custom_call_target="tpu_custom_call" | custom-call | flops 28000000000 | bytes 7000000 | tf_op jit(solution)/shard_map/attend/pallas_call | solution.py:478
  63.5 6.8 %middle.1 = (f32[1024,768]{1,0:T(8,128)S(1)}, bf16[1024,768]{1,0:T(8,128)(2,1)S(1)}, f32[1024,768]{1,0:T(8,128)S(1)}, bf16[1024,768]{1,0:T(8,128)(2,1)S(1)}) custom-call(s32[16]{0:T(128)S(1)} %bitcast.141, s32[1]{0:T(128)} %bitcast.1.place_ref, bf16[1024,768]{1,0:T(8,128)(2,1)S(1)} %copy-done.26, bf16[768,1024]{1,0:T(8,128)(2,1)S(1)} %get-tuple-element.142.attn_ref, ...), custom_call_target="tpu_custom_call" | custom-call | flops 8999999488 | bytes 20000000 | tf_op jit(solution)/shard_map/middle/pallas_call | solution.py:721
  72.1 18.1 %feed.2 = (f32[1024,768]{1,0:T(8,128)S(1)}, f32[1024,768]{1,0:T(8,128)S(1)}, bf16[2,768,768]{2,1,0:T(8,128)(2,1)}, bf16[2,768,768]{2,1,0:T(8,128)(2,1)S(1)}, f32[1,768]{1,0:T(1,128)S(1)}, /*index=5*/f32[1,768]{1,0:T(1,128)S(1)}) custom-call(f32[1024,768]{1,0:T(8,128)S(1)} %get-tuple-element.144.y_in_ref.dh_in_ref.x2_ref, ...), custom_call_target="tpu_custom_call" | custom-call | flops 24000000000 | bytes 25000000 | tf_op jit(solution)/shard_map/feed/pallas_call | solution.py:785
  90.7 6.0 %collective-permute-done.5.up_a.down_a = bf16[2,768,768]{2,1,0:T(8,128)(2,1)S(1)} collective-permute-done((bf16[2,768,768]{2,1,0:T(8,128)(2,1)S(1)}, bf16[2,768,768]{2,1,0:T(8,128)(2,1)S(1)}, u32[]{:S(2)}, u32[]{:S(2)}) %collective-permute-start.5) | collective-permute-done | bytes 2359328 | tf_op jit(solution)/shard_map/ppermute | solution.py:40
  96.7 17.9 %feed.3 = (f32[1024,768]{1,0:T(8,128)S(1)}, f32[1024,768]{1,0:T(8,128)S(1)}, bf16[2,768,768]{2,1,0:T(8,128)(2,1)}, bf16[2,768,768]{2,1,0:T(8,128)(2,1)S(1)}, f32[1,768]{1,0:T(1,128)S(1)}, /*index=5*/f32[1,768]{1,0:T(1,128)S(1)}) custom-call(f32[1024,768]{1,0:T(8,128)S(1)} %get-tuple-element.150.y_in_ref, f32[1024,768]{1,0:T(8,128)S(1)} %get-tuple-element.151.dh_in_ref, ...), custom_call_target="tpu_custom_call" | custom-call | flops 24000000000 | bytes 25000000 | tf_op jit(solution)/shard_map/feed/pallas_call | solution.py:785
  132.3 12.0 %after.1 = (bf16[1024,768]{1,0:T(8,128)(2,1)}, bf16[16,768]{1,0:T(8,128)(2,1)}, f32[1024,768]{1,0:T(8,128)}, bf16[768,1024]{1,0:T(8,128)(2,1)}, bf16[768,768]{1,0:T(8,128)(2,1)}, /*index=5*/f32[8,768]{1,0:T(8,128)}) custom-call(s32[16]{0:T(128)} %bitcast.137, s32[1]{0:T(128)} %bitcast.1.place_ref, f32[1024,768]{1,0:T(8,128)} %copy-done.18, ...), custom_call_target="tpu_custom_call" | custom-call | flops 4000000000 | bytes 25000000 | tf_op jit(solution)/shard_map/after/pallas_call | solution.py:844
  145.5 11.0 %attend_back.2 = (bf16[3,768,1024]{2,1,0:T(8,128)(2,1)}, f32[3,1,384]{2,1,0:T(1,128)}, f32[1,256]{1,0:T(1,128)}, bf16[3,768,768]{2,1,0:T(8,128)(2,1)}) custom-call(s32[16]{0:T(128)} %bitcast.138, bf16[3,768,1024]{2,1,0:T(8,128)(2,1)} %copy-done, bf16[768,1024]{1,0:T(8,128)(2,1)} %copy-done.1, f32[12,1,1024]{2,1,0:T(1,128)} %copy-done.33, ...), custom_call_target="tpu_custom_call" | custom-call | flops 2000000000 | bytes 8000000 | tf_op jit(solution)/shard_map/attend_back/pallas_call | solution.py:637
  167.5 11.2 %attend_back.3 = (bf16[3,768,1024]{2,1,0:T(8,128)(2,1)}, f32[3,1,384]{2,1,0:T(1,128)}, f32[1,256]{1,0:T(1,128)}, bf16[3,768,768]{2,1,0:T(8,128)(2,1)}) custom-call(s32[16]{0:T(128)} %bitcast.139, bf16[3,768,1024]{2,1,0:T(8,128)(2,1)} %copy-done, bf16[768,1024]{1,0:T(8,128)(2,1)} %copy-done.1, ...), custom_call_target="tpu_custom_call", output_to_operand_aliasing={{0}: (9, {}), {3}: (10, {})} | custom-call | flops 2000000000 | bytes 8000000 | tf_op jit(solution)/shard_map/attend_back/pallas_call | solution.py:637
  178.7 3.3 collective-permute-done.13
  187.0 3.6 collective-permute-start.16
  195.3 5.7 %collective-permute-start.15 = (bf16[96,768]{1,0:T(8,128)(2,1)S(1)}, bf16[96,768]{1,0:T(8,128)(2,1)S(1)}, u32[]{:S(2)}, u32[]{:S(2)}) collective-permute-start(bf16[96,768]{1,0:T(8,128)(2,1)S(1)} %dynamic-slice_bitcast_fusion.11), channel_id=1, source_target_pairs={{0,4},{4,0},{8,12},{12,8},{16,20},{20,16},{24,28},{28,24},{1,5},{5... | collective-permute-start | bytes 442376 | tf_op jit(solution)/shard_map/ppermute | solution.py:40
  201.1 3.6 collective-permute-start.21
  206.7 8.8 %first_back.1 = (f32[1024,768]{1,0:T(8,128)}, f32[8,768]{1,0:T(8,128)S(1)}) custom-call(s32[1]{0:T(128)} %bitcast.1.place_ref, bf16[1024,768]{1,0:T(8,128)(2,1)S(1)} %copy-done.27, bf16[2304,1024]{1,0:T(8,128)(2,1)S(1)} %bitcast.121, bf16[768,768]{1,0:T(8,128)(2,1)S(1)} %copy-done.4, bf16[768,768]{1,0:T(8,128)(2,1)} %collective-permute-done.w1, ...), custom_call_target="tpu_custom_call" | custom-call | flops 200000000 | bytes 17000000 | tf_op jit(solution)/shard_map/first_back/pallas_call | solution.py:881
  221.1 5.8 %collective-permute-start.18 = (bf16[192,768]{1,0:T(8,128)(2,1)S(1)}, bf16[192,768]{1,0:T(8,128)(2,1)S(1)}, u32[]{:S(2)}, u32[]{:S(2)}) collective-permute-start(bf16[192,768]{1,0:T(8,128)(2,1)S(1)} %fusion.8), channel_id=1, source_target_pairs={{0,16},{4,20},{8,24},{12,28},{16,0},{20,4},{24,8},{28,12},{1,17},{... | collective-permute-start | bytes 884744 | tf_op jit(solution)/shard_map/ppermute | solution.py:40
  232.7 4.6 %all-to-all-start.1 = ((bf16[8,2,768]{2,1,0:T(2,128)(2,1)}), bf16[8,2,768]{2,1,0:T(2,128)(2,1)S(1)}, u32[]{:S(2)}, u32[]{:S(2)}) async-start(bf16[8,2,768]{2,1,0:T(2,128)(2,1)} %reshape.159), calls=%async_computation.1 | async-start | bytes 49152 | tf_op jit(solution)/shard_map/all_to_all | solution.py:1236
  238.3 8.2 %all-to-all-done.1 = bf16[8,2,768]{2,1,0:T(2,128)(2,1)S(1)} async-done(((bf16[8,2,768]{2,1,0:T(2,128)(2,1)}), bf16[8,2,768]{2,1,0:T(2,128)(2,1)S(1)}, u32[]{:S(2)}, u32[]{:S(2)}) %all-to-all-start.1) | async-done | bytes 24608 | tf_op jit(solution)/shard_map/all_to_all | solution.py:1236
  254.4 4.8 %collective-permute-done.26 = bf16[192,768]{1,0:T(8,128)(2,1)S(1)} collective-permute-done((bf16[192,768]{1,0:T(8,128)(2,1)S(1)}, bf16[192,768]{1,0:T(8,128)(2,1)S(1)}, u32[]{:S(2)}, u32[]{:S(2)}) %collective-permute-start.26) | collective-permute-done | bytes 294944 | tf_op jit(solution)/shard_map/ppermute | solution.py:40
  267.5 3.4 collective-permute-done.35
  271.2 3.3 collective-permute-start.38
  277.0 4.7 %collective-permute-done.32 = bf16[144,768]{1,0:T(8,128)(2,1)S(1)} collective-permute-done((bf16[144,768]{1,0:T(8,128)(2,1)S(1)}, bf16[144,768]{1,0:T(8,128)(2,1)S(1)}, u32[]{:S(2)}, u32[]{:S(2)}) %collective-permute-start.32) | collective-permute-done | bytes 221216 | tf_op jit(solution)/shard_map/ppermute | solution.py:40
  282.9 7.8 %collective-permute-done.36.other_ref.first_ref = bf16[384,768]{1,0:T(8,128)(2,1)S(1)} collective-permute-done((bf16[384,768]{1,0:T(8,128)(2,1)S(1)}, bf16[384,768]{1,0:T(8,128)(2,1)S(1)}, u32[]{:S(2)}, u32[]{:S(2)}) %collective-permute-start.36) | collective-permute-done | bytes 589856 | tf_op jit(solution)/shard_map/ppermute | solution.py:40
  296.1 7.3 %collective-permute-done.40 = bf16[144,768]{1,0:T(8,128)(2,1)S(1)} collective-permute-done((bf16[144,768]{1,0:T(8,128)(2,1)S(1)}, bf16[144,768]{1,0:T(8,128)(2,1)S(1)}, u32[]{:S(2)}, u32[]{:S(2)}) %collective-permute-start.40) | collective-permute-done | bytes 221216 | tf_op jit(solution)/shard_map/ppermute | solution.py:40
  306.7 10.9 %muon.3 = (f32[192,768]{1,0:T(8,128)}, bf16[192,768]{1,0:T(8,128)(2,1)}) custom-call(s32[1]{0:T(128)} %bitcast.50.half_ref, f32[1,3,256,256]{3,2,1,0:T(8,128)S(1)} %bitcast.132, f32[1,3,256,256]{3,2,1,0:T(8,128)S(1)} %bitcast.142, f32[192,768]{1,0:T(8,128)S(1)} %copy-done.37, f32[192,768]{1,0:T(8,128)S(1)} %copy-done.31), custom_call_target="tpu_custom_call" | custom-call | flops 1000000000 | bytes 2064384 | tf_op jit(solution)/shard_map/muon/pallas_call | solution.py:1087
  317.6 3.2 collective-permute-done.44.second_ref
  337.3 13.1 %muon.4 = bf16[768,768]{1,0:T(8,128)(2,1)S(1)} custom-call(s32[1]{0:T(128)} %bitcast.50.half_ref, f32[1,3,256,256]{3,2,1,0:T(8,128)S(1)} %bitcast.122, f32[1,3,256,256]{3,2,1,0:T(8,128)S(1)} %bitcast.133, bf16[768,768]{1,0:T(8,128)(2,1)S(1)} %get-tuple-element.248.moment_ref), custom_call_target="tpu_custom_call" | custom-call | flops 1000000000 | bytes 8257536 | tf_op jit(solution)/shard_map/muon/pallas_call | solution.py:1087
  351.5 4.4 %collective-permute-done.48 = f32[3,256,256]{2,1,0:T(8,128)} collective-permute-done((f32[3,256,256]{2,1,0:T(8,128)}, f32[3,256,256]{2,1,0:T(8,128)}, u32[]{:S(2)}, u32[]{:S(2)}) %collective-permute-start.48) | collective-permute-done | bytes 786464 | tf_op jit(solution)/shard_map/ppermute | solution.py:40
  359.5 13.5 %muon.5 = (f32[576,768]{1,0:T(8,128)}, bf16[576,768]{1,0:T(8,128)(2,1)}) custom-call(s32[1]{0:T(128)} %bitcast.50.half_ref, f32[1,3,256,256]{3,2,1,0:T(8,128)S(1)} %bitcast.123, f32[1,3,256,256]{3,2,1,0:T(8,128)S(1)} %bitcast.134, f32[576,768]{1,0:T(8,128)S(1)} %copy-done.24, f32[576,768]{1,0:T(8,128)S(1)} %copy-done.10), custom_call_target="tpu_custom_call" | custom-call | flops 1000000000 | bytes 6193152 | tf_op jit(solution)/shard_map/muon/pallas_call | solution.py:1087
  373.0 5.3 %collective-permute-done.47 = bf16[768,768]{1,0:T(8,128)(2,1)S(1)} collective-permute-done((bf16[768,768]{1,0:T(8,128)(2,1)S(1)}, bf16[768,768]{1,0:T(8,128)(2,1)S(1)}, u32[]{:S(2)}, u32[]{:S(2)}) %collective-permute-start.47) | collective-permute-done | bytes 1179680 | tf_op jit(solution)/shard_map/ppermute | solution.py:40
  378.3 3.7 fusion.18
  (291 shorter events, 123.6 us)
Async XLA Ops:
  2.5 29.0 %collective-permute-start.1 = (bf16[768,768]{1,0:T(8,128)(2,1)S(1)}, bf16[768,768]{1,0:T(8,128)(2,1)S(1)}, u32[]{:S(2)}, u32[]{:S(2)}) collective-permute-start(bf16[768,768]{1,0:T(8,128)(2,1)S(1)} %pad_maximum_fusion.2.w0), channel_id=1, source_target_pairs={{0,2},{1,3},{2,0},{3,1},{4,6},{5,7},{6,4},{7,5},{8,10},{9,11},{10,... | collective-permute-start | bytes 3538952 | tf_op jit(solution)/shard_map/ppermute | solution.py:40
  5.5 28.4 %collective-permute-start = (bf16[768,768]{1,0:T(8,128)(2,1)S(1)}, bf16[768,768]{1,0:T(8,128)(2,1)}, u32[]{:S(2)}, u32[]{:S(2)}) collective-permute-start(bf16[768,768]{1,0:T(8,128)(2,1)S(1)} %pad_maximum_fusion.2.w0), channel_id=1, source_target_pairs={{0,1},{1,0},{2,3},{3,2},{4,5},{5,4},{6,7},{7,6},{8,9},{9,8},{10,11... | collective-permute-start | bytes 3538952 | tf_op jit(solution)/shard_map/ppermute | solution.py:40
  6.1 13.1 %all-to-all-start = ((bf16[8,2,768]{2,1,0:T(2,128)(2,1)}), bf16[8,2,768]{2,1,0:T(2,128)(2,1)S(1)}, u32[]{:S(2)}, u32[]{:S(2)}) async-start(bf16[8,2,768]{2,1,0:T(2,128)(2,1)} %reshape.148), calls=%async_computation | async-start | bytes 49152 | tf_op jit(solution)/shard_map/all_to_all | solution.py:1138
  31.6 40.4 %collective-permute-start.3 = (bf16[2,768,768]{2,1,0:T(8,128)(2,1)}, bf16[2,768,768]{2,1,0:T(8,128)(2,1)S(1)}, u32[]{:S(2)}, u32[]{:S(2)}) collective-permute-start(bf16[2,768,768]{2,1,0:T(8,128)(2,1)} %pad_maximum_fusion.up_b.down_b), channel_id=1, source_target_pairs={{0,1},{1,0},{2,3},{3,2},{4,5},{5,4},{6,7},{7,6},{8,9},{9,8},{10,11... | collective-permute-start | bytes 7077896 | tf_op jit(solution)/shard_map/ppermute | solution.py:40
  32.2 58.0 %collective-permute-start.4 = (bf16[2,768,768]{2,1,0:T(8,128)(2,1)}, bf16[2,768,768]{2,1,0:T(8,128)(2,1)S(1)}, u32[]{:S(2)}, u32[]{:S(2)}) collective-permute-start(bf16[2,768,768]{2,1,0:T(8,128)(2,1)} %pad_maximum_fusion.up_b.down_b), channel_id=1, source_target_pairs={{0,2},{1,3},{2,0},{3,1},{4,6},{5,7},{6,4},{7,5},{8,10},{9,11},{10,... | collective-permute-start | bytes 7077896 | tf_op jit(solution)/shard_map/ppermute | solution.py:40
  90.3 29.1 %collective-permute-start.7 = (bf16[2,768,768]{2,1,0:T(8,128)(2,1)}, bf16[2,768,768]{2,1,0:T(8,128)(2,1)}, u32[]{:S(2)}, u32[]{:S(2)}) collective-permute-start(bf16[2,768,768]{2,1,0:T(8,128)(2,1)} %get-tuple-element.157), channel_id=1, source_target_pairs={{0,1},{1,0},{2,3},{3,2},{4,5},{5,4},{6,7},{7,6},{8,9},{9,8},{10,11... | collective-permute-start | bytes 7077896 | tf_op jit(solution)/shard_map/ppermute | solution.py:40
  128.9 28.3 %collective-permute-start.9 = (bf16[2,384,768]{2,1,0:T(8,128)(2,1)}, bf16[2,384,768]{2,1,0:T(8,128)(2,1)}, u32[]{:S(2)}, u32[]{:S(2)}) collective-permute-start(bf16[2,384,768]{2,1,0:T(8,128)(2,1)} %dynamic-slice_bitcast_fusion.1), channel_id=1, source_target_pairs={{0,4},{4,0},{8,12},{12,8},{16,20},{20,16},{24,28},{28,24},{1,5},{5... | collective-permute-start | bytes 3538952 | tf_op jit(solution)/shard_map/ppermute | solution.py:40
  130.6 28.0 %collective-permute-start.8 = (bf16[768,768]{1,0:T(8,128)(2,1)}, bf16[768,768]{1,0:T(8,128)(2,1)}, u32[]{:S(2)}, u32[]{:S(2)}) collective-permute-start(bf16[768,768]{1,0:T(8,128)(2,1)} %get-tuple-element.268), channel_id=1, source_target_pairs={{0,2},{1,3},{2,0},{3,1},{4,6},{5,7},{6,4},{7,5},{8,10},{9,11},{10,... | collective-permute-start | bytes 3538952 | tf_op jit(solution)/shard_map/ppermute | solution.py:40
  161.2 20.8 %collective-permute-start.12 = (bf16[384,768]{1,0:T(8,128)(2,1)}, bf16[384,768]{1,0:T(8,128)(2,1)}, u32[]{:S(2)}, u32[]{:S(2)}) collective-permute-start(bf16[384,768]{1,0:T(8,128)(2,1)} %slice_bitcast_fusion.1), channel_id=1, source_target_pairs={{0,2},{1,3},{2,0},{3,1},{4,6},{5,7},{6,4},{7,5},{8,10},{9,11},{10,... | collective-permute-start | bytes 1769480 | tf_op jit(solution)/shard_map/ppermute | solution.py:40
  165.4 16.6 %collective-permute-start.11 = (bf16[384,768]{1,0:T(8,128)(2,1)}, bf16[384,768]{1,0:T(8,128)(2,1)}, u32[]{:S(2)}, u32[]{:S(2)}) collective-permute-start(bf16[384,768]{1,0:T(8,128)(2,1)} %dynamic-slice_bitcast_fusion.5), channel_id=1, source_target_pairs={{0,4},{4,0},{8,12},{12,8},{16,20},{20,16},{24,28},{28,24},{1,5},{5... | collective-permute-start | bytes 1769480 | tf_op jit(solution)/shard_map/ppermute | solution.py:40
  166.9 15.0 %collective-permute-start.13 = (bf16[1,192,768]{2,1,0:T(8,128)(2,1)S(1)}, bf16[1,192,768]{2,1,0:T(8,128)(2,1)S(1)}, u32[]{:S(2)}, u32[]{:S(2)}) collective-permute-start(bf16[1,192,768]{2,1,0:T(8,128)(2,1)S(1)} %constant_dynamic-slice_fusion.5), channel_id=1, source_target_pairs={{0,2},{1,3},{2,0},{3,1},{4,6},{5,7},{6,4},{7,5},{8,10},{9,11},{10,... | collective-permute-start | bytes 884744 | tf_op jit(solution)/shard_map/ppermute | solution.py:40
  187.0 14.0 %collective-permute-start.16 = (bf16[192,768]{1,0:T(8,128)(2,1)S(1)}, bf16[192,768]{1,0:T(8,128)(2,1)S(1)}, u32[]{:S(2)}, u32[]{:S(2)}) collective-permute-start(bf16[192,768]{1,0:T(8,128)(2,1)S(1)} %dynamic-slice_bitcast_fusion.8), channel_id=1, source_target_pairs={{0,8},{4,12},{8,0},{12,4},{16,24},{20,28},{24,16},{28,20},{1,9},{5... | collective-permute-start | bytes 884744 | tf_op jit(solution)/shard_map/ppermute | solution.py:40
  192.0 13.0 %collective-permute-start.14 = (bf16[192,768]{1,0:T(8,128)(2,1)S(1)}, bf16[192,768]{1,0:T(8,128)(2,1)S(1)}, u32[]{:S(2)}, u32[]{:S(2)}) collective-permute-start(bf16[192,768]{1,0:T(8,128)(2,1)S(1)} %dynamic-slice_bitcast_fusion.9), channel_id=1, source_target_pairs={{0,8},{4,12},{8,0},{12,4},{16,24},{20,28},{24,16},{28,20},{1,9},{5... | collective-permute-start | bytes 884744 | tf_op jit(solution)/shard_map/ppermute | solution.py:40
  194.8 21.8 %collective-permute-start.19 = (bf16[1,576,768]{2,1,0:T(8,128)(2,1)S(1)}, bf16[1,576,768]{2,1,0:T(8,128)(2,1)S(1)}, u32[]{:S(2)}, u32[]{:S(2)}) collective-permute-start(bf16[1,576,768]{2,1,0:T(8,128)(2,1)S(1)} %constant_dynamic-slice_fusion.4), channel_id=1, source_target_pairs={{0,2},{1,3},{2,0},{3,1},{4,6},{5,7},{6,4},{7,5},{8,10},{9,11},{10,... | collective-permute-start | bytes 2654216 | tf_op jit(solution)/shard_map/ppermute | solution.py:40
  201.1 25.8 %collective-permute-start.21 = (bf16[192,768]{1,0:T(8,128)(2,1)S(1)}, bf16[192,768]{1,0:T(8,128)(2,1)}, u32[]{:S(2)}, u32[]{:S(2)}) collective-permute-start(bf16[192,768]{1,0:T(8,128)(2,1)S(1)} %fusion.7), channel_id=1, source_target_pairs={{0,16},{4,20},{8,24},{12,28},{16,0},{20,4},{24,8},{28,12},{1,17},{... | collective-permute-start | bytes 884744 | tf_op jit(solution)/shard_map/ppermute | solution.py:40
  205.0 16.1 %collective-permute-start.22 = (bf16[96,768]{1,0:T(8,128)(2,1)S(1)}, bf16[96,768]{1,0:T(8,128)(2,1)}, u32[]{:S(2)}, u32[]{:S(2)}) collective-permute-start(bf16[96,768]{1,0:T(8,128)(2,1)S(1)} %fusion.10), channel_id=1, source_target_pairs={{0,8},{4,12},{8,0},{12,4},{16,24},{20,28},{24,16},{28,20},{1,9},{5... | collective-permute-start | bytes 442376 | tf_op jit(solution)/shard_map/ppermute | solution.py:40
  217.8 11.6 %collective-permute-start.23 = (f32[80,128]{1,0:T(8,128)S(1)}, f32[80,128]{1,0:T(8,128)S(1)}, u32[]{:S(2)}, u32[]{:S(2)}) collective-permute-start(f32[80,128]{1,0:T(8,128)S(1)} %bitcast.168), channel_id=1, source_target_pairs={{0,1},{1,0},{2,3},{3,2},{4,5},{5,4},{6,7},{7,6},{8,9},{9,8},{10,11... | collective-permute-start | bytes 122888 | tf_op jit(solution)/shard_map/ppermute | solution.py:40
  217.9 11.5 %collective-permute-start.24 = (f32[80,128]{1,0:T(8,128)S(1)}, f32[80,128]{1,0:T(8,128)S(1)}, u32[]{:S(2)}, u32[]{:S(2)}) collective-permute-start(f32[80,128]{1,0:T(8,128)S(1)} %bitcast.169), channel_id=1, source_target_pairs={{0,2},{1,3},{2,0},{3,1},{4,6},{5,7},{6,4},{7,5},{8,10},{9,11},{10,... | collective-permute-start | bytes 122888 | tf_op jit(solution)/shard_map/ppermute | solution.py:40
  221.1 28.2 %collective-permute-start.18 = (bf16[192,768]{1,0:T(8,128)(2,1)S(1)}, bf16[192,768]{1,0:T(8,128)(2,1)S(1)}, u32[]{:S(2)}, u32[]{:S(2)}) collective-permute-start(bf16[192,768]{1,0:T(8,128)(2,1)S(1)} %fusion.8), channel_id=1, source_target_pairs={{0,16},{4,20},{8,24},{12,28},{16,0},{20,4},{24,8},{28,12},{1,17},{... | collective-permute-start | bytes 884744 | tf_op jit(solution)/shard_map/ppermute | solution.py:40
  226.9 20.2 %collective-permute-start.20 = (bf16[288,768]{1,0:T(8,128)(2,1)S(1)}, bf16[288,768]{1,0:T(8,128)(2,1)S(1)}, u32[]{:S(2)}, u32[]{:S(2)}) collective-permute-start(bf16[288,768]{1,0:T(8,128)(2,1)S(1)} %dynamic-slice_bitcast_fusion.7), channel_id=1, source_target_pairs={{0,4},{4,0},{8,12},{12,8},{16,20},{20,16},{24,28},{28,24},{1,5},{5... | collective-permute-start | bytes 1327112 | tf_op jit(solution)/shard_map/ppermute | solution.py:40
  230.5 16.7 %collective-permute-start.31 = (bf16[192,768]{1,0:T(8,128)(2,1)S(1)}, bf16[192,768]{1,0:T(8,128)(2,1)S(1)}, u32[]{:S(2)}, u32[]{:S(2)}) collective-permute-start(bf16[192,768]{1,0:T(8,128)(2,1)S(1)} %add_convert_fusion.4), channel_id=1, source_target_pairs={{0,8},{4,12},{8,0},{12,4},{16,24},{20,28},{24,16},{28,20},{1,9},{5... | collective-permute-start | bytes 884744 | tf_op jit(solution)/shard_map/ppermute | solution.py:40
  230.6 19.9 %collective-permute-start.28 = (f32[80,128]{1,0:T(8,128)S(1)}, f32[80,128]{1,0:T(8,128)S(1)}, u32[]{:S(2)}, u32[]{:S(2)}) collective-permute-start(f32[80,128]{1,0:T(8,128)S(1)} %add_add_fusion.1), channel_id=1, source_target_pairs={{0,4},{4,0},{8,12},{12,8},{16,20},{20,16},{24,28},{28,24},{1,5},{5... | collective-permute-start | bytes 122888 | tf_op jit(solution)/shard_map/ppermute | solution.py:40
  231.8 18.7 %collective-permute-start.29 = (f32[80,128]{1,0:T(8,128)S(1)}, f32[80,128]{1,0:T(8,128)S(1)}, u32[]{:S(2)}, u32[]{:S(2)}) collective-permute-start(f32[80,128]{1,0:T(8,128)S(1)} %add_add_fusion.1), channel_id=1, source_target_pairs={{0,8},{4,12},{8,0},{12,4},{16,24},{20,28},{24,16},{28,20},{1,9},{5... | collective-permute-start | bytes 122888 | tf_op jit(solution)/shard_map/ppermute | solution.py:40
  232.7 13.8 %all-to-all-start.1 = ((bf16[8,2,768]{2,1,0:T(2,128)(2,1)}), bf16[8,2,768]{2,1,0:T(2,128)(2,1)S(1)}, u32[]{:S(2)}, u32[]{:S(2)}) async-start(bf16[8,2,768]{2,1,0:T(2,128)(2,1)} %reshape.159), calls=%async_computation.1 | async-start | bytes 49152 | tf_op jit(solution)/shard_map/all_to_all | solution.py:1236
  271.2 22.6 %collective-permute-start.38 = (f32[3,256,256]{2,1,0:T(8,128)S(1)}, f32[3,256,256]{2,1,0:T(8,128)S(1)}, u32[]{:S(2)}, u32[]{:S(2)}) collective-permute-start(f32[3,256,256]{2,1,0:T(8,128)S(1)} %dynamic-slice_bitcast_fusion.4), channel_id=1, source_target_pairs={{0,2},{1,3},{2,0},{3,1},{4,6},{5,7},{6,4},{7,5},{8,10},{9,11},{10,... | collective-permute-start | bytes 2359304 | tf_op jit(solution)/shard_map/ppermute | solution.py:40
  275.9 14.8 %collective-permute-start.36 = (bf16[384,768]{1,0:T(8,128)(2,1)S(1)}, bf16[384,768]{1,0:T(8,128)(2,1)S(1)}, u32[]{:S(2)}, u32[]{:S(2)}) collective-permute-start(bf16[384,768]{1,0:T(8,128)(2,1)S(1)} %get-tuple-element.269), channel_id=1, source_target_pairs={{0,4},{4,0},{8,12},{12,8},{16,20},{20,16},{24,28},{28,24},{1,5},{5... | collective-permute-start | bytes 1769480 | tf_op jit(solution)/shard_map/ppermute | solution.py:40
  281.7 12.0 %collective-permute-start.37 = (bf16[144,768]{1,0:T(8,128)(2,1)S(1)}, bf16[144,768]{1,0:T(8,128)(2,1)S(1)}, u32[]{:S(2)}, u32[]{:S(2)}) collective-permute-start(bf16[144,768]{1,0:T(8,128)(2,1)S(1)} %fusion.9), channel_id=1, source_target_pairs={{0,16},{4,20},{8,24},{12,28},{16,0},{20,4},{24,8},{28,12},{1,17},{... | collective-permute-start | bytes 663560 | tf_op jit(solution)/shard_map/ppermute | solution.py:40
  303.8 22.2 %collective-permute-start.43 = (f32[3,256,256]{2,1,0:T(8,128)S(1)}, f32[3,256,256]{2,1,0:T(8,128)S(1)}, u32[]{:S(2)}, u32[]{:S(2)}) collective-permute-start(f32[3,256,256]{2,1,0:T(8,128)S(1)} %dynamic-slice_bitcast_fusion.3), channel_id=1, source_target_pairs={{0,2},{1,3},{2,0},{3,1},{4,6},{5,7},{6,4},{7,5},{8,10},{9,11},{10,... | collective-permute-start | bytes 2359304 | tf_op jit(solution)/shard_map/ppermute | solution.py:40
  304.5 16.3 %collective-permute-start.44 = (bf16[384,768]{1,0:T(8,128)(2,1)S(1)}, bf16[384,768]{1,0:T(8,128)(2,1)S(1)}, u32[]{:S(2)}, u32[]{:S(2)}) collective-permute-start(bf16[384,768]{1,0:T(8,128)(2,1)S(1)} %get-tuple-element.232.own_ref), channel_id=1, source_target_pairs={{0,4},{4,0},{8,12},{12,8},{16,20},{20,16},{24,28},{28,24},{1,5},{5... | collective-permute-start | bytes 1769480 | tf_op jit(solution)/shard_map/ppermute | solution.py:40
  305.5 22.6 %collective-permute-start.42 = (bf16[288,768]{1,0:T(8,128)(2,1)S(1)}, bf16[288,768]{1,0:T(8,128)(2,1)S(1)}, u32[]{:S(2)}, u32[]{:S(2)}) collective-permute-start(bf16[288,768]{1,0:T(8,128)(2,1)S(1)} %get-tuple-element.276), channel_id=1, source_target_pairs={{0,4},{4,0},{8,12},{12,8},{16,20},{20,16},{24,28},{28,24},{1,5},{5... | collective-permute-start | bytes 1327112 | tf_op jit(solution)/shard_map/ppermute | solution.py:40
  336.0 19.9 %collective-permute-start.48 = (f32[3,256,256]{2,1,0:T(8,128)}, f32[3,256,256]{2,1,0:T(8,128)}, u32[]{:S(2)}, u32[]{:S(2)}) collective-permute-start(f32[3,256,256]{2,1,0:T(8,128)} %dynamic-slice_bitcast_fusion.2), channel_id=1, source_target_pairs={{0,2},{1,3},{2,0},{3,1},{4,6},{5,7},{6,4},{7,5},{8,10},{9,11},{10,... | collective-permute-start | bytes 2359304 | tf_op jit(solution)/shard_map/ppermute | solution.py:40
  350.5 27.8 %collective-permute-start.47 = (bf16[768,768]{1,0:T(8,128)(2,1)S(1)}, bf16[768,768]{1,0:T(8,128)(2,1)S(1)}, u32[]{:S(2)}, u32[]{:S(2)}) collective-permute-start(bf16[768,768]{1,0:T(8,128)(2,1)S(1)} %muon.4), channel_id=1, source_target_pairs={{0,4},{4,0},{8,12},{12,8},{16,20},{20,16},{24,28},{28,24},{1,5},{5... | collective-permute-start | bytes 3538952 | tf_op jit(solution)/shard_map/ppermute | solution.py:40
  (80 other events, 715.8 us)

commit v5 on v4

--- a/solution.py
+++ b/solution.py
@@ -473,7 +473,7 @@
             lax.fori_loop(first // 256, slots // 256, columns, 0)
 
 
-def attend(counts, qkv, group=6):
+def attend(counts, qkv, group=12):
     slots = qkv.shape[2]
     return pl.pallas_call(
         functools.partial(attend_kernel, group),
@@ -485,7 +485,7 @@
                        pl.BlockSpec((group, 1, slots), lambda h, c: (h, 0, 0))],
         ),
         out_shape=[shape_of((D, slots), LOW), shape_of((HEADS, 1, slots), F32)],
-        compiler_params=params(16),
+        compiler_params=params(46),
         cost_estimate=cost(28, 7000000.0),
         name="attend",
     )(counts, qkv)

time: 386 us -> 397 us (1.028)
  Pallas kernels: 160 us -> 166 us
  local copies, waits for them, and re-layouts: 23.3 us -> 28.7 us
  starting transfers between devices: 69 us -> 64.7 us
    unnamed x120, local copies, waits for them, and re-layouts: 11.8 us -> 17.1 us
    pallas_call x1, Pallas kernels: 16.8 us -> 21.7 us  [attend(): pl.pallas_call(functools.partial(attend_kernel, group), grid_spec=pltpu.P...]
  transfers between devices with their start and end apart: 52 -> 52, of which waited for: 26 -> 26; matrix products, arithmetic and copies ran while one was open for 8% -> 7% of each run, Pallas kernels for 41% -> 41%
where the time goes in v5:
time: 397 us; the launch traced here: 392 us
  Pallas kernels  166 us (42%)
  waiting for transfers between devices  97.4 us (25%)
  starting transfers between devices  64.7 us (16%)
  other arithmetic  33.4 us (8%)
  local copies, waits for them, and re-layouts  28.7 us (7%)
    ppermute x50, waiting for transfers between devices, exchange(): lax.ppermute(value, axis, [(index, index ^ mask) for index in range(count)])  89 us
    ppermute x50, starting transfers between devices, exchange(): lax.ppermute(value, axis, [(index, index ^ mask) for index in range(count)])  55.1 us
    pallas_call x3, Pallas kernels, muon(): pl.pallas_call(functools.partial(muon_kernel, step_scale), grid=(1,), in_...  37.4 us
    pallas_call x2, Pallas kernels, feed(): pl.pallas_call(functools.partial(feed_kernel, distances, start_y), grid=(...  37.2 us
    pallas_call x2, Pallas kernels, attend_back(): pl.pallas_call(functools.partial(attend_back_kernel, group), grid_spec=pl...  22.3 us
    pallas_call x1, Pallas kernels, attend(): pl.pallas_call(functools.partial(attend_kernel, group), grid_spec=pltpu.P...  21.7 us
    convert_element_type x20, other arithmetic, add_low(): (first.astype(jnp.float32) + second.astype(jnp.float32)).astype(jnp.bfloa...  18.2 us
    unnamed x120, local copies, waits for them, and re-layouts  17.1 us
  transfers between devices with their start and end apart: 52, of which 26 were waited for; matrix products, arithmetic and copies ran while one was open for 7% of the time, Pallas kernels for 41%

profile of v5, /device:TPU:0, one launch (start us, length us, event | category | flops | bytes accessed | tf_op | source)
XLA Modules:
  0.0 392.1 jit_solution(7060342150651390992)
XLA Ops:
  2.5 3.0 collective-permute-start.1
  6.1 5.8 %all-to-all-start = ((bf16[8,2,768]{2,1,0:T(2,128)(2,1)}), bf16[8,2,768]{2,1,0:T(2,128)(2,1)S(1)}, u32[]{:S(2)}, u32[]{:S(2)}) async-start(bf16[8,2,768]{2,1,0:T(2,128)(2,1)} %reshape.148), calls=%async_computation | async-start | bytes 49152 | tf_op jit(solution)/shard_map/all_to_all | solution.py:1138
  19.5 12.0 %collective-permute-done.1.w2 = bf16[768,768]{1,0:T(8,128)(2,1)S(1)} collective-permute-done((bf16[768,768]{1,0:T(8,128)(2,1)S(1)}, bf16[768,768]{1,0:T(8,128)(2,1)S(1)}, u32[]{:S(2)}, u32[]{:S(2)}) %collective-permute-start.1) | collective-permute-done | bytes 1179680 | tf_op jit(solution)/shard_map/ppermute | solution.py:40
  35.9 10.0 %project.1 = (bf16[1024,768]{1,0:T(8,128)(2,1)S(1)}, bf16[3,768,1024]{2,1,0:T(8,128)(2,1)S(1)}, bf16[2,768,1024]{2,1,0:T(8,128)(2,1)S(1)}, f32[2,12,1,1024]{3,2,1,0:T(1,128)S(1)}) custom-call(s32[1]{0:T(128)} %bitcast.1.place_ref, bf16[1024,768]{1,0:T(8,128)(2,1)S(1)} %copy-done.25, bf16[768,768]{1,0:T(8,128)(2,1)S(1)} %pad_maximum_fusion.2.w0, ...), custom_call_target="tpu_custom_call" | custom-call | flops 10000000000 | bytes 16000000 | tf_op jit(solution)/shard_map/project/pallas_call | solution.py:348
  49.3 21.7 %attend.1 = (bf16[768,1024]{1,0:T(8,128)(2,1)S(1)}, f32[12,1,1024]{2,1,0:T(1,128)S(1)}) custom-call(s32[16]{0:T(128)S(1)} %bitcast.140, bf16[3,768,1024]{2,1,0:T(8,128)(2,1)S(1)} %get-tuple-element.141.qkv_ref), custom_call_target="tpu_custom_call" | custom-call | flops 28000000000 | bytes 7000000 | tf_op jit(solution)/shard_map/attend/pallas_call | solution.py:478
  73.6 6.3 %middle.1 = (f32[1024,768]{1,0:T(8,128)S(1)}, bf16[1024,768]{1,0:T(8,128)(2,1)S(1)}, f32[1024,768]{1,0:T(8,128)S(1)}, bf16[1024,768]{1,0:T(8,128)(2,1)S(1)}) custom-call(s32[16]{0:T(128)S(1)} %bitcast.141, s32[1]{0:T(128)} %bitcast.1.place_ref, bf16[1024,768]{1,0:T(8,128)(2,1)S(1)} %copy-done.26, bf16[768,1024]{1,0:T(8,128)(2,1)S(1)} %get-tuple-element.142.attn_ref, ...), custom_call_target="tpu_custom_call" | custom-call | flops 8999999488 | bytes 20000000 | tf_op jit(solution)/shard_map/middle/pallas_call | solution.py:721
  81.6 18.8 %feed.2 = (f32[1024,768]{1,0:T(8,128)S(1)}, f32[1024,768]{1,0:T(8,128)S(1)}, bf16[2,768,768]{2,1,0:T(8,128)(2,1)}, bf16[2,768,768]{2,1,0:T(8,128)(2,1)S(1)}, f32[1,768]{1,0:T(1,128)S(1)}, /*index=5*/f32[1,768]{1,0:T(1,128)S(1)}) custom-call(f32[1024,768]{1,0:T(8,128)S(1)} %get-tuple-element.144.y_in_ref.dh_in_ref.x2_ref, ...), custom_call_target="tpu_custom_call" | custom-call | flops 24000000000 | bytes 25000000 | tf_op jit(solution)/shard_map/feed/pallas_call | solution.py:785
  101.1 6.1 %collective-permute-done.5.up_a.down_a = bf16[2,768,768]{2,1,0:T(8,128)(2,1)S(1)} collective-permute-done((bf16[2,768,768]{2,1,0:T(8,128)(2,1)}, bf16[2,768,768]{2,1,0:T(8,128)(2,1)S(1)}, u32[]{:S(2)}, u32[]{:S(2)}) %collective-permute-start.5) | collective-permute-done | bytes 2359328 | tf_op jit(solution)/shard_map/ppermute | solution.py:40
  107.2 18.3 %feed.3 = (f32[1024,768]{1,0:T(8,128)S(1)}, f32[1024,768]{1,0:T(8,128)S(1)}, bf16[2,768,768]{2,1,0:T(8,128)(2,1)}, bf16[2,768,768]{2,1,0:T(8,128)(2,1)S(1)}, f32[1,768]{1,0:T(1,128)S(1)}, /*index=5*/f32[1,768]{1,0:T(1,128)S(1)}) custom-call(f32[1024,768]{1,0:T(8,128)S(1)} %get-tuple-element.150.y_in_ref, f32[1024,768]{1,0:T(8,128)S(1)} %get-tuple-element.151.dh_in_ref, ...), custom_call_target="tpu_custom_call" | custom-call | flops 24000000000 | bytes 25000000 | tf_op jit(solution)/shard_map/feed/pallas_call | solution.py:785
  143.2 12.0 %after.1 = (bf16[1024,768]{1,0:T(8,128)(2,1)}, bf16[16,768]{1,0:T(8,128)(2,1)}, f32[1024,768]{1,0:T(8,128)}, bf16[768,1024]{1,0:T(8,128)(2,1)}, bf16[768,768]{1,0:T(8,128)(2,1)}, /*index=5*/f32[8,768]{1,0:T(8,128)}) custom-call(s32[16]{0:T(128)} %bitcast.137, s32[1]{0:T(128)} %bitcast.1.place_ref, f32[1024,768]{1,0:T(8,128)} %copy-done.18, ...), custom_call_target="tpu_custom_call" | custom-call | flops 4000000000 | bytes 25000000 | tf_op jit(solution)/shard_map/after/pallas_call | solution.py:844
  156.4 11.0 %attend_back.2 = (bf16[3,768,1024]{2,1,0:T(8,128)(2,1)}, f32[3,1,384]{2,1,0:T(1,128)}, f32[1,256]{1,0:T(1,128)}, bf16[3,768,768]{2,1,0:T(8,128)(2,1)}) custom-call(s32[16]{0:T(128)} %bitcast.138, bf16[3,768,1024]{2,1,0:T(8,128)(2,1)} %copy-done, bf16[768,1024]{1,0:T(8,128)(2,1)} %copy-done.1, f32[12,1,1024]{2,1,0:T(1,128)} %copy-done.33, ...), custom_call_target="tpu_custom_call" | custom-call | flops 2000000000 | bytes 8000000 | tf_op jit(solution)/shard_map/attend_back/pallas_call | solution.py:637
  179.1 11.3 %attend_back.3 = (bf16[3,768,1024]{2,1,0:T(8,128)(2,1)}, f32[3,1,384]{2,1,0:T(1,128)}, f32[1,256]{1,0:T(1,128)}, bf16[3,768,768]{2,1,0:T(8,128)(2,1)}) custom-call(s32[16]{0:T(128)} %bitcast.139, bf16[3,768,1024]{2,1,0:T(8,128)(2,1)} %copy-done, bf16[768,1024]{1,0:T(8,128)(2,1)} %copy-done.1, ...), custom_call_target="tpu_custom_call", output_to_operand_aliasing={{0}: (9, {}), {3}: (10, {})} | custom-call | flops 2000000000 | bytes 8000000 | tf_op jit(solution)/shard_map/attend_back/pallas_call | solution.py:637
  190.3 3.4 collective-permute-done.13
  206.2 5.9 %collective-permute-start.15 = (bf16[96,768]{1,0:T(8,128)(2,1)S(1)}, bf16[96,768]{1,0:T(8,128)(2,1)S(1)}, u32[]{:S(2)}, u32[]{:S(2)}) collective-permute-start(bf16[96,768]{1,0:T(8,128)(2,1)S(1)} %dynamic-slice_bitcast_fusion.11), channel_id=1, source_target_pairs={{0,4},{4,0},{8,12},{12,8},{16,20},{20,16},{24,28},{28,24},{1,5},{5... | collective-permute-start | bytes 442376 | tf_op jit(solution)/shard_map/ppermute | solution.py:40
  217.6 8.8 %first_back.1 = (f32[1024,768]{1,0:T(8,128)}, f32[8,768]{1,0:T(8,128)S(1)}) custom-call(s32[1]{0:T(128)} %bitcast.1.place_ref, bf16[1024,768]{1,0:T(8,128)(2,1)S(1)} %copy-done.27, bf16[2304,1024]{1,0:T(8,128)(2,1)S(1)} %bitcast.121, bf16[768,768]{1,0:T(8,128)(2,1)S(1)} %copy-done.4, bf16[768,768]{1,0:T(8,128)(2,1)} %collective-permute-done.w1, ...), custom_call_target="tpu_custom_call" | custom-call | flops 200000000 | bytes 17000000 | tf_op jit(solution)/shard_map/first_back/pallas_call | solution.py:881
  231.4 5.3 %collective-permute-start.18 = (bf16[192,768]{1,0:T(8,128)(2,1)S(1)}, bf16[192,768]{1,0:T(8,128)(2,1)S(1)}, u32[]{:S(2)}, u32[]{:S(2)}) collective-permute-start(bf16[192,768]{1,0:T(8,128)(2,1)S(1)} %fusion.8), channel_id=1, source_target_pairs={{0,16},{4,20},{8,24},{12,28},{16,0},{20,4},{24,8},{28,12},{1,17},{... | collective-permute-start | bytes 884744 | tf_op jit(solution)/shard_map/ppermute | solution.py:40
  236.7 4.8 %collective-permute-start.20 = (bf16[288,768]{1,0:T(8,128)(2,1)S(1)}, bf16[288,768]{1,0:T(8,128)(2,1)S(1)}, u32[]{:S(2)}, u32[]{:S(2)}) collective-permute-start(bf16[288,768]{1,0:T(8,128)(2,1)S(1)} %dynamic-slice_bitcast_fusion.7), channel_id=1, source_target_pairs={{0,4},{4,0},{8,12},{12,8},{16,20},{20,16},{24,28},{28,24},{1,5},{5... | collective-permute-start | bytes 1327112 | tf_op jit(solution)/shard_map/ppermute | solution.py:40
  244.8 3.9 all-to-all-start.1
  249.7 8.4 %all-to-all-done.1 = bf16[8,2,768]{2,1,0:T(2,128)(2,1)S(1)} async-done(((bf16[8,2,768]{2,1,0:T(2,128)(2,1)}), bf16[8,2,768]{2,1,0:T(2,128)(2,1)S(1)}, u32[]{:S(2)}, u32[]{:S(2)}) %all-to-all-start.1) | async-done | bytes 24608 | tf_op jit(solution)/shard_map/all_to_all | solution.py:1236
  267.6 4.0 %collective-permute-done.26 = bf16[192,768]{1,0:T(8,128)(2,1)S(1)} collective-permute-done((bf16[192,768]{1,0:T(8,128)(2,1)S(1)}, bf16[192,768]{1,0:T(8,128)(2,1)S(1)}, u32[]{:S(2)}, u32[]{:S(2)}) %collective-permute-start.26) | collective-permute-done | bytes 294944 | tf_op jit(solution)/shard_map/ppermute | solution.py:40
  279.9 3.4 collective-permute-done.35
  285.8 5.4 %collective-permute-done.32 = bf16[144,768]{1,0:T(8,128)(2,1)S(1)} collective-permute-done((bf16[144,768]{1,0:T(8,128)(2,1)S(1)}, bf16[144,768]{1,0:T(8,128)(2,1)S(1)}, u32[]{:S(2)}, u32[]{:S(2)}) %collective-permute-start.32) | collective-permute-done | bytes 221216 | tf_op jit(solution)/shard_map/ppermute | solution.py:40
  292.5 7.3 %collective-permute-done.36.other_ref.first_ref = bf16[384,768]{1,0:T(8,128)(2,1)S(1)} collective-permute-done((bf16[384,768]{1,0:T(8,128)(2,1)S(1)}, bf16[384,768]{1,0:T(8,128)(2,1)S(1)}, u32[]{:S(2)}, u32[]{:S(2)}) %collective-permute-start.36) | collective-permute-done | bytes 589856 | tf_op jit(solution)/shard_map/ppermute | solution.py:40
  299.8 3.7 collective-permute-done.37
  306.5 6.6 %collective-permute-done.40 = bf16[144,768]{1,0:T(8,128)(2,1)S(1)} collective-permute-done((bf16[144,768]{1,0:T(8,128)(2,1)S(1)}, bf16[144,768]{1,0:T(8,128)(2,1)S(1)}, u32[]{:S(2)}, u32[]{:S(2)}) %collective-permute-start.40) | collective-permute-done | bytes 221216 | tf_op jit(solution)/shard_map/ppermute | solution.py:40
  317.3 10.9 %muon.3 = (f32[192,768]{1,0:T(8,128)}, bf16[192,768]{1,0:T(8,128)(2,1)}) custom-call(s32[1]{0:T(128)} %bitcast.50.half_ref, f32[1,3,256,256]{3,2,1,0:T(8,128)S(1)} %bitcast.132, f32[1,3,256,256]{3,2,1,0:T(8,128)S(1)} %bitcast.142, f32[192,768]{1,0:T(8,128)S(1)} %copy-done.37, f32[192,768]{1,0:T(8,128)S(1)} %copy-done.31), custom_call_target="tpu_custom_call" | custom-call | flops 1000000000 | bytes 2064384 | tf_op jit(solution)/shard_map/muon/pallas_call | solution.py:1087
  328.1 3.2 collective-permute-done.44.second_ref
  347.0 13.1 %muon.4 = bf16[768,768]{1,0:T(8,128)(2,1)S(1)} custom-call(s32[1]{0:T(128)} %bitcast.50.half_ref, f32[1,3,256,256]{3,2,1,0:T(8,128)S(1)} %bitcast.122, f32[1,3,256,256]{3,2,1,0:T(8,128)S(1)} %bitcast.133, bf16[768,768]{1,0:T(8,128)(2,1)S(1)} %get-tuple-element.248.moment_ref), custom_call_target="tpu_custom_call" | custom-call | flops 1000000000 | bytes 8257536 | tf_op jit(solution)/shard_map/muon/pallas_call | solution.py:1087
  361.1 5.3 %collective-permute-done.48 = f32[3,256,256]{2,1,0:T(8,128)} collective-permute-done((f32[3,256,256]{2,1,0:T(8,128)}, f32[3,256,256]{2,1,0:T(8,128)}, u32[]{:S(2)}, u32[]{:S(2)}) %collective-permute-start.48) | collective-permute-done | bytes 786464 | tf_op jit(solution)/shard_map/ppermute | solution.py:40
  370.0 13.5 %muon.5 = (f32[576,768]{1,0:T(8,128)}, bf16[576,768]{1,0:T(8,128)(2,1)}) custom-call(s32[1]{0:T(128)} %bitcast.50.half_ref, f32[1,3,256,256]{3,2,1,0:T(8,128)S(1)} %bitcast.123, f32[1,3,256,256]{3,2,1,0:T(8,128)S(1)} %bitcast.134, f32[576,768]{1,0:T(8,128)S(1)} %copy-done.24, f32[576,768]{1,0:T(8,128)S(1)} %copy-done.10), custom_call_target="tpu_custom_call" | custom-call | flops 1000000000 | bytes 6193152 | tf_op jit(solution)/shard_map/muon/pallas_call | solution.py:1087
  383.5 4.5 %collective-permute-done.47 = bf16[768,768]{1,0:T(8,128)(2,1)S(1)} collective-permute-done((bf16[768,768]{1,0:T(8,128)(2,1)S(1)}, bf16[768,768]{1,0:T(8,128)(2,1)S(1)}, u32[]{:S(2)}, u32[]{:S(2)}) %collective-permute-start.47) | collective-permute-done | bytes 1179680 | tf_op jit(solution)/shard_map/ppermute | solution.py:40
  388.0 3.7 fusion.18
  (291 shorter events, 128.6 us)
Async XLA Ops:
  2.5 29.0 %collective-permute-start.1 = (bf16[768,768]{1,0:T(8,128)(2,1)S(1)}, bf16[768,768]{1,0:T(8,128)(2,1)S(1)}, u32[]{:S(2)}, u32[]{:S(2)}) collective-permute-start(bf16[768,768]{1,0:T(8,128)(2,1)S(1)} %pad_maximum_fusion.2.w0), channel_id=1, source_target_pairs={{0,2},{1,3},{2,0},{3,1},{4,6},{5,7},{6,4},{7,5},{8,10},{9,11},{10,... | collective-permute-start | bytes 3538952 | tf_op jit(solution)/shard_map/ppermute | solution.py:40
  5.5 28.4 %collective-permute-start = (bf16[768,768]{1,0:T(8,128)(2,1)S(1)}, bf16[768,768]{1,0:T(8,128)(2,1)}, u32[]{:S(2)}, u32[]{:S(2)}) collective-permute-start(bf16[768,768]{1,0:T(8,128)(2,1)S(1)} %pad_maximum_fusion.2.w0), channel_id=1, source_target_pairs={{0,1},{1,0},{2,3},{3,2},{4,5},{5,4},{6,7},{7,6},{8,9},{9,8},{10,11... | collective-permute-start | bytes 3538952 | tf_op jit(solution)/shard_map/ppermute | solution.py:40
  6.1 13.1 %all-to-all-start = ((bf16[8,2,768]{2,1,0:T(2,128)(2,1)}), bf16[8,2,768]{2,1,0:T(2,128)(2,1)S(1)}, u32[]{:S(2)}, u32[]{:S(2)}) async-start(bf16[8,2,768]{2,1,0:T(2,128)(2,1)} %reshape.148), calls=%async_computation | async-start | bytes 49152 | tf_op jit(solution)/shard_map/all_to_all | solution.py:1138
  31.6 50.0 %collective-permute-start.3 = (bf16[2,768,768]{2,1,0:T(8,128)(2,1)}, bf16[2,768,768]{2,1,0:T(8,128)(2,1)}, u32[]{:S(2)}, u32[]{:S(2)}) collective-permute-start(bf16[2,768,768]{2,1,0:T(8,128)(2,1)} %pad_maximum_fusion.up_b.down_b), channel_id=1, source_target_pairs={{0,1},{1,0},{2,3},{3,2},{4,5},{5,4},{6,7},{7,6},{8,9},{9,8},{10,11... | collective-permute-start | bytes 7077896 | tf_op jit(solution)/shard_map/ppermute | solution.py:40
  32.2 68.3 %collective-permute-start.4 = (bf16[2,768,768]{2,1,0:T(8,128)(2,1)}, bf16[2,768,768]{2,1,0:T(8,128)(2,1)}, u32[]{:S(2)}, u32[]{:S(2)}) collective-permute-start(bf16[2,768,768]{2,1,0:T(8,128)(2,1)} %pad_maximum_fusion.up_b.down_b), channel_id=1, source_target_pairs={{0,2},{1,3},{2,0},{3,1},{4,6},{5,7},{6,4},{7,5},{8,10},{9,11},{10,... | collective-permute-start | bytes 7077896 | tf_op jit(solution)/shard_map/ppermute | solution.py:40
  100.7 29.7 %collective-permute-start.7 = (bf16[2,768,768]{2,1,0:T(8,128)(2,1)}, bf16[2,768,768]{2,1,0:T(8,128)(2,1)}, u32[]{:S(2)}, u32[]{:S(2)}) collective-permute-start(bf16[2,768,768]{2,1,0:T(8,128)(2,1)} %get-tuple-element.157), channel_id=1, source_target_pairs={{0,1},{1,0},{2,3},{3,2},{4,5},{5,4},{6,7},{7,6},{8,9},{9,8},{10,11... | collective-permute-start | bytes 7077896 | tf_op jit(solution)/shard_map/ppermute | solution.py:40
  139.9 29.0 %collective-permute-start.9 = (bf16[2,384,768]{2,1,0:T(8,128)(2,1)}, bf16[2,384,768]{2,1,0:T(8,128)(2,1)}, u32[]{:S(2)}, u32[]{:S(2)}) collective-permute-start(bf16[2,384,768]{2,1,0:T(8,128)(2,1)} %dynamic-slice_bitcast_fusion.1), channel_id=1, source_target_pairs={{0,4},{4,0},{8,12},{12,8},{16,20},{20,16},{24,28},{28,24},{1,5},{5... | collective-permute-start | bytes 3538952 | tf_op jit(solution)/shard_map/ppermute | solution.py:40
  142.3 28.0 %collective-permute-start.8 = (bf16[768,768]{1,0:T(8,128)(2,1)}, bf16[768,768]{1,0:T(8,128)(2,1)}, u32[]{:S(2)}, u32[]{:S(2)}) collective-permute-start(bf16[768,768]{1,0:T(8,128)(2,1)} %get-tuple-element.268), channel_id=1, source_target_pairs={{0,2},{1,3},{2,0},{3,1},{4,6},{5,7},{6,4},{7,5},{8,10},{9,11},{10,... | collective-permute-start | bytes 3538952 | tf_op jit(solution)/shard_map/ppermute | solution.py:40
  173.0 20.8 %collective-permute-start.12 = (bf16[384,768]{1,0:T(8,128)(2,1)}, bf16[384,768]{1,0:T(8,128)(2,1)}, u32[]{:S(2)}, u32[]{:S(2)}) collective-permute-start(bf16[384,768]{1,0:T(8,128)(2,1)} %slice_bitcast_fusion.1), channel_id=1, source_target_pairs={{0,2},{1,3},{2,0},{3,1},{4,6},{5,7},{6,4},{7,5},{8,10},{9,11},{10,... | collective-permute-start | bytes 1769480 | tf_op jit(solution)/shard_map/ppermute | solution.py:40
  176.4 17.4 %collective-permute-start.11 = (bf16[384,768]{1,0:T(8,128)(2,1)}, bf16[384,768]{1,0:T(8,128)(2,1)}, u32[]{:S(2)}, u32[]{:S(2)}) collective-permute-start(bf16[384,768]{1,0:T(8,128)(2,1)} %dynamic-slice_bitcast_fusion.5), channel_id=1, source_target_pairs={{0,4},{4,0},{8,12},{12,8},{16,20},{20,16},{24,28},{28,24},{1,5},{5... | collective-permute-start | bytes 1769480 | tf_op jit(solution)/shard_map/ppermute | solution.py:40
  178.2 15.5 %collective-permute-start.13 = (bf16[1,192,768]{2,1,0:T(8,128)(2,1)S(1)}, bf16[1,192,768]{2,1,0:T(8,128)(2,1)S(1)}, u32[]{:S(2)}, u32[]{:S(2)}) collective-permute-start(bf16[1,192,768]{2,1,0:T(8,128)(2,1)S(1)} %constant_dynamic-slice_fusion.5), channel_id=1, source_target_pairs={{0,2},{1,3},{2,0},{3,1},{4,6},{5,7},{6,4},{7,5},{8,10},{9,11},{10,... | collective-permute-start | bytes 884744 | tf_op jit(solution)/shard_map/ppermute | solution.py:40
  198.8 13.3 %collective-permute-start.16 = (bf16[192,768]{1,0:T(8,128)(2,1)S(1)}, bf16[192,768]{1,0:T(8,128)(2,1)S(1)}, u32[]{:S(2)}, u32[]{:S(2)}) collective-permute-start(bf16[192,768]{1,0:T(8,128)(2,1)S(1)} %dynamic-slice_bitcast_fusion.8), channel_id=1, source_target_pairs={{0,8},{4,12},{8,0},{12,4},{16,24},{20,28},{24,16},{28,20},{1,9},{5... | collective-permute-start | bytes 884744 | tf_op jit(solution)/shard_map/ppermute | solution.py:40
  202.3 13.6 %collective-permute-start.14 = (bf16[192,768]{1,0:T(8,128)(2,1)S(1)}, bf16[192,768]{1,0:T(8,128)(2,1)S(1)}, u32[]{:S(2)}, u32[]{:S(2)}) collective-permute-start(bf16[192,768]{1,0:T(8,128)(2,1)S(1)} %dynamic-slice_bitcast_fusion.9), channel_id=1, source_target_pairs={{0,8},{4,12},{8,0},{12,4},{16,24},{20,28},{24,16},{28,20},{1,9},{5... | collective-permute-start | bytes 884744 | tf_op jit(solution)/shard_map/ppermute | solution.py:40
  205.1 21.8 %collective-permute-start.19 = (bf16[1,576,768]{2,1,0:T(8,128)(2,1)S(1)}, bf16[1,576,768]{2,1,0:T(8,128)(2,1)S(1)}, u32[]{:S(2)}, u32[]{:S(2)}) collective-permute-start(bf16[1,576,768]{2,1,0:T(8,128)(2,1)S(1)} %constant_dynamic-slice_fusion.4), channel_id=1, source_target_pairs={{0,2},{1,3},{2,0},{3,1},{4,6},{5,7},{6,4},{7,5},{8,10},{9,11},{10,... | collective-permute-start | bytes 2654216 | tf_op jit(solution)/shard_map/ppermute | solution.py:40
  212.2 24.5 %collective-permute-start.21 = (bf16[192,768]{1,0:T(8,128)(2,1)S(1)}, bf16[192,768]{1,0:T(8,128)(2,1)}, u32[]{:S(2)}, u32[]{:S(2)}) collective-permute-start(bf16[192,768]{1,0:T(8,128)(2,1)S(1)} %fusion.7), channel_id=1, source_target_pairs={{0,16},{4,20},{8,24},{12,28},{16,0},{20,4},{24,8},{28,12},{1,17},{... | collective-permute-start | bytes 884744 | tf_op jit(solution)/shard_map/ppermute | solution.py:40
  215.9 15.5 %collective-permute-start.22 = (bf16[96,768]{1,0:T(8,128)(2,1)S(1)}, bf16[96,768]{1,0:T(8,128)(2,1)}, u32[]{:S(2)}, u32[]{:S(2)}) collective-permute-start(bf16[96,768]{1,0:T(8,128)(2,1)S(1)} %fusion.10), channel_id=1, source_target_pairs={{0,8},{4,12},{8,0},{12,4},{16,24},{20,28},{24,16},{28,20},{1,9},{5... | collective-permute-start | bytes 442376 | tf_op jit(solution)/shard_map/ppermute | solution.py:40
  228.0 13.5 %collective-permute-start.23 = (f32[80,128]{1,0:T(8,128)S(1)}, f32[80,128]{1,0:T(8,128)S(1)}, u32[]{:S(2)}, u32[]{:S(2)}) collective-permute-start(f32[80,128]{1,0:T(8,128)S(1)} %bitcast.168), channel_id=1, source_target_pairs={{0,1},{1,0},{2,3},{3,2},{4,5},{5,4},{6,7},{7,6},{8,9},{9,8},{10,11... | collective-permute-start | bytes 122888 | tf_op jit(solution)/shard_map/ppermute | solution.py:40
  228.1 13.4 %collective-permute-start.24 = (f32[80,128]{1,0:T(8,128)S(1)}, f32[80,128]{1,0:T(8,128)S(1)}, u32[]{:S(2)}, u32[]{:S(2)}) collective-permute-start(f32[80,128]{1,0:T(8,128)S(1)} %bitcast.169), channel_id=1, source_target_pairs={{0,2},{1,3},{2,0},{3,1},{4,6},{5,7},{6,4},{7,5},{8,10},{9,11},{10,... | collective-permute-start | bytes 122888 | tf_op jit(solution)/shard_map/ppermute | solution.py:40
  229.1 12.4 %collective-permute-start.25 = (f32[80,128]{1,0:T(8,128)S(1)}, f32[80,128]{1,0:T(8,128)S(1)}, u32[]{:S(2)}, u32[]{:S(2)}) collective-permute-start(f32[80,128]{1,0:T(8,128)S(1)} %bitcast.170), channel_id=1, source_target_pairs={{0,3},{1,2},{2,1},{3,0},{4,7},{5,6},{6,5},{7,4},{8,11},{9,10},{10,... | collective-permute-start | bytes 122888 | tf_op jit(solution)/shard_map/ppermute | solution.py:40
  231.4 30.4 %collective-permute-start.18 = (bf16[192,768]{1,0:T(8,128)(2,1)S(1)}, bf16[192,768]{1,0:T(8,128)(2,1)S(1)}, u32[]{:S(2)}, u32[]{:S(2)}) collective-permute-start(bf16[192,768]{1,0:T(8,128)(2,1)S(1)} %fusion.8), channel_id=1, source_target_pairs={{0,16},{4,20},{8,24},{12,28},{16,0},{20,4},{24,8},{28,12},{1,17},{... | collective-permute-start | bytes 884744 | tf_op jit(solution)/shard_map/ppermute | solution.py:40
  236.7 22.0 %collective-permute-start.20 = (bf16[288,768]{1,0:T(8,128)(2,1)S(1)}, bf16[288,768]{1,0:T(8,128)(2,1)S(1)}, u32[]{:S(2)}, u32[]{:S(2)}) collective-permute-start(bf16[288,768]{1,0:T(8,128)(2,1)S(1)} %dynamic-slice_bitcast_fusion.7), channel_id=1, source_target_pairs={{0,4},{4,0},{8,12},{12,8},{16,20},{20,16},{24,28},{28,24},{1,5},{5... | collective-permute-start | bytes 1327112 | tf_op jit(solution)/shard_map/ppermute | solution.py:40
  242.6 16.1 %collective-permute-start.31 = (bf16[192,768]{1,0:T(8,128)(2,1)S(1)}, bf16[192,768]{1,0:T(8,128)(2,1)S(1)}, u32[]{:S(2)}, u32[]{:S(2)}) collective-permute-start(bf16[192,768]{1,0:T(8,128)(2,1)S(1)} %add_convert_fusion.4), channel_id=1, source_target_pairs={{0,8},{4,12},{8,0},{12,4},{16,24},{20,28},{24,16},{28,20},{1,9},{5... | collective-permute-start | bytes 884744 | tf_op jit(solution)/shard_map/ppermute | solution.py:40
  242.7 19.4 %collective-permute-start.28 = (f32[80,128]{1,0:T(8,128)S(1)}, f32[80,128]{1,0:T(8,128)S(1)}, u32[]{:S(2)}, u32[]{:S(2)}) collective-permute-start(f32[80,128]{1,0:T(8,128)S(1)} %add_add_fusion.1), channel_id=1, source_target_pairs={{0,4},{4,0},{8,12},{12,8},{16,20},{20,16},{24,28},{28,24},{1,5},{5... | collective-permute-start | bytes 122888 | tf_op jit(solution)/shard_map/ppermute | solution.py:40
  242.8 19.3 %collective-permute-start.29 = (f32[80,128]{1,0:T(8,128)S(1)}, f32[80,128]{1,0:T(8,128)S(1)}, u32[]{:S(2)}, u32[]{:S(2)}) collective-permute-start(f32[80,128]{1,0:T(8,128)S(1)} %add_add_fusion.1), channel_id=1, source_target_pairs={{0,8},{4,12},{8,0},{12,4},{16,24},{20,28},{24,16},{28,20},{1,9},{5... | collective-permute-start | bytes 122888 | tf_op jit(solution)/shard_map/ppermute | solution.py:40
  244.8 13.3 %all-to-all-start.1 = ((bf16[8,2,768]{2,1,0:T(2,128)(2,1)}), bf16[8,2,768]{2,1,0:T(2,128)(2,1)S(1)}, u32[]{:S(2)}, u32[]{:S(2)}) async-start(bf16[8,2,768]{2,1,0:T(2,128)(2,1)} %reshape.159), calls=%async_computation.1 | async-start | bytes 49152 | tf_op jit(solution)/shard_map/all_to_all | solution.py:1236
  283.6 19.8 %collective-permute-start.38 = (f32[3,256,256]{2,1,0:T(8,128)S(1)}, f32[3,256,256]{2,1,0:T(8,128)S(1)}, u32[]{:S(2)}, u32[]{:S(2)}) collective-permute-start(f32[3,256,256]{2,1,0:T(8,128)S(1)} %dynamic-slice_bitcast_fusion.4), channel_id=1, source_target_pairs={{0,2},{1,3},{2,0},{3,1},{4,6},{5,7},{6,4},{7,5},{8,10},{9,11},{10,... | collective-permute-start | bytes 2359304 | tf_op jit(solution)/shard_map/ppermute | solution.py:40
  284.7 15.1 %collective-permute-start.36 = (bf16[384,768]{1,0:T(8,128)(2,1)S(1)}, bf16[384,768]{1,0:T(8,128)(2,1)S(1)}, u32[]{:S(2)}, u32[]{:S(2)}) collective-permute-start(bf16[384,768]{1,0:T(8,128)(2,1)S(1)} %get-tuple-element.269), channel_id=1, source_target_pairs={{0,4},{4,0},{8,12},{12,8},{16,20},{20,16},{24,28},{28,24},{1,5},{5... | collective-permute-start | bytes 1769480 | tf_op jit(solution)/shard_map/ppermute | solution.py:40
  313.5 23.0 %collective-permute-start.43 = (f32[3,256,256]{2,1,0:T(8,128)S(1)}, f32[3,256,256]{2,1,0:T(8,128)S(1)}, u32[]{:S(2)}, u32[]{:S(2)}) collective-permute-start(f32[3,256,256]{2,1,0:T(8,128)S(1)} %dynamic-slice_bitcast_fusion.3), channel_id=1, source_target_pairs={{0,2},{1,3},{2,0},{3,1},{4,6},{5,7},{6,4},{7,5},{8,10},{9,11},{10,... | collective-permute-start | bytes 2359304 | tf_op jit(solution)/shard_map/ppermute | solution.py:40
  315.1 16.3 %collective-permute-start.44 = (bf16[384,768]{1,0:T(8,128)(2,1)S(1)}, bf16[384,768]{1,0:T(8,128)(2,1)S(1)}, u32[]{:S(2)}, u32[]{:S(2)}) collective-permute-start(bf16[384,768]{1,0:T(8,128)(2,1)S(1)} %get-tuple-element.232.own_ref), channel_id=1, source_target_pairs={{0,4},{4,0},{8,12},{12,8},{16,20},{20,16},{24,28},{28,24},{1,5},{5... | collective-permute-start | bytes 1769480 | tf_op jit(solution)/shard_map/ppermute | solution.py:40
  316.1 22.6 %collective-permute-start.42 = (bf16[288,768]{1,0:T(8,128)(2,1)S(1)}, bf16[288,768]{1,0:T(8,128)(2,1)S(1)}, u32[]{:S(2)}, u32[]{:S(2)}) collective-permute-start(bf16[288,768]{1,0:T(8,128)(2,1)S(1)} %get-tuple-element.276), channel_id=1, source_target_pairs={{0,4},{4,0},{8,12},{12,8},{16,20},{20,16},{24,28},{28,24},{1,5},{5... | collective-permute-start | bytes 1327112 | tf_op jit(solution)/shard_map/ppermute | solution.py:40
  346.5 19.9 %collective-permute-start.48 = (f32[3,256,256]{2,1,0:T(8,128)}, f32[3,256,256]{2,1,0:T(8,128)}, u32[]{:S(2)}, u32[]{:S(2)}) collective-permute-start(f32[3,256,256]{2,1,0:T(8,128)} %dynamic-slice_bitcast_fusion.2), channel_id=1, source_target_pairs={{0,2},{1,3},{2,0},{3,1},{4,6},{5,7},{6,4},{7,5},{8,10},{9,11},{10,... | collective-permute-start | bytes 2359304 | tf_op jit(solution)/shard_map/ppermute | solution.py:40
  360.2 27.8 %collective-permute-start.47 = (bf16[768,768]{1,0:T(8,128)(2,1)S(1)}, bf16[768,768]{1,0:T(8,128)(2,1)S(1)}, u32[]{:S(2)}, u32[]{:S(2)}) collective-permute-start(bf16[768,768]{1,0:T(8,128)(2,1)S(1)} %muon.4), channel_id=1, source_target_pairs={{0,4},{4,0},{8,12},{12,8},{16,20},{20,16},{24,28},{28,24},{1,5},{5... | collective-permute-start | bytes 3538952 | tf_op jit(solution)/shard_map/ppermute | solution.py:40
  (80 other events, 683.3 us)
